TPU v7x, 512 devices: a whole 4x4x16 slice. The times are simulated.
512 devices in a mesh: section: 8 (over y, z_hi), tp: 64 (over z_lo, x, core).
Axes of the slice: x: 4, y: 4, z: 16 (z_hi: 2, z_lo: 8; z = z_hi * 8 + z_lo), core: 2. Of those that a mesh axis runs over, the one named last changes fastest.
Arguments:
- acts: bfloat16 [8192, 4096], P(('section', 'tp')), may hold values from -6 to 6
- cotangent: bfloat16 [8192, 4096], P(('section', 'tp')), may hold values from -6 to 6
- gains: float32 [8, 2, 4096], P('section'), may hold values from 0.1 to 1.9
- gate_blocks: bfloat16 [8, 192, 128, 128], P('section', 'tp'), may hold values from -0.4375 to 0.4375
- up_blocks: bfloat16 [8, 192, 128, 128], P('section', 'tp'), may hold values from -0.4375 to 0.4375
- down_blocks: bfloat16 [8, 192, 128, 128], P('section', 'tp'), may hold values from -0.21875 to 0.21875
- block_place: int32 [8, 192], P('section'), may hold values from -1 to 63, as said below
Outputs:
- layer_out: bfloat16 [8192, 4096], P(('section', 'tp'))
- grad_back: bfloat16 [8192, 4096], P(('section', 'tp'))
- gate_grad: bfloat16 [8, 192, 128, 128], P('section', 'tp')
- up_grad: bfloat16 [8, 192, 128, 128], P('section', 'tp')
- down_grad: bfloat16 [8, 192, 128, 128], P('section', 'tp')
- gain_grad: float32 [8, 2, 4096], P('section')
Inputs may be any that keep to these rules, and one draw needn't show every extreme that they name: `block_place`: A value p >= 0 places the slot at feature block p // 2 and at block p % 2 of its device's hidden units; -1 marks an empty slot. Slots j with the same j // 3 belong to one device; on one device the live slots come first and their values are distinct; every device has 1 or more live slots, and one device of every section has all 3 live.
All inputs are finite; a program needn't handle non-finite values.
Results may differ from a plain program's by a relative error of at most 0.0073.
Values may be sent and summed in bfloat16 or wider, within the bound.
No kernel may reach another device: no remote copies, remote signals or barrier semaphores. Data moves between devices by JAX's collectives and lax.ppermute only.
A program may use at most 64 MiB of HBM per device.

v0:
```python
import jax
import jax.numpy as jnp
from jax import lax
from jax.sharding import PartitionSpec as P

COLS_DEV = 2


epsilon = 1e-05
highest = lax.Precision.HIGHEST


def from_behind(value, axis, steps):
    count = lax.axis_size(axis)
    first, last = (max(0, -steps), min(count, count - steps))
    return lax.ppermute(value, axis, [(source, source + steps) for source in range(first, last)])


def slot_tables(slot_place, row_blocks, col_blocks):
    live_flag = (slot_place >= 0).astype(jnp.float32)
    position = jnp.maximum(slot_place, 0)
    row_ids = position // col_blocks
    col_ids = position % col_blocks
    row_onehot = (row_ids[:, None] == jnp.arange(row_blocks, dtype=jnp.int32)[None, :]).astype(
        jnp.float32
    ) * live_flag[:, None]
    col_onehot = (col_ids[:, None] == jnp.arange(col_blocks, dtype=jnp.int32)[None, :]).astype(
        jnp.float32
    ) * live_flag[:, None]
    return (row_ids, col_ids, row_onehot, col_onehot, live_flag)


def to_columns(per_slot, col_onehot):
    return jnp.einsum("tsn,sc->tcn", per_slot, col_onehot, precision=highest)


def row_norm(values):
    return lax.rsqrt(jnp.mean(values * values, axis=-1, keepdims=True) + epsilon)


def body(acts, cotangent, gains, gate_blocks, up_blocks, down_blocks, block_place):
    tok_rows, model_width = acts.shape
    block_size = gate_blocks.shape[-1]
    slot_count = gate_blocks.shape[1]
    row_blocks = model_width // block_size
    device_count = lax.axis_size("tp")
    gate_w = gate_blocks[0]
    up_w = up_blocks[0]
    down_w = down_blocks[0]
    every_place = block_place[0]
    own_place = lax.dynamic_slice_in_dim(
        every_place, lax.axis_index("tp") * slot_count, slot_count, 0
    )
    row_ids, col_ids, row_onehot, col_onehot, live_flag = slot_tables(
        own_place, row_blocks, COLS_DEV
    )
    every_rows, every_cols, every_onehot, every_colhot, every_live = slot_tables(
        every_place, row_blocks, COLS_DEV
    )
    every_onehot = every_onehot.astype(jnp.bfloat16).reshape(device_count, slot_count, row_blocks)
    gain_pre = gains[0, 0]
    gain_post = gains[0, 1]

    def to_devices(rows):
        picked = jnp.take(rows.reshape(tok_rows, row_blocks, block_size), every_rows, axis=1)
        return picked.reshape(tok_rows, device_count, 1, slot_count * block_size)

    def from_devices(received):
        pieces = received.reshape(tok_rows, device_count, slot_count, block_size)
        summed = jnp.einsum(
            "tdsk,dsr->trk", pieces, every_onehot, preferred_element_type=jnp.float32
        )
        return summed.reshape(tok_rows, model_width)

    inputs = acts.astype(jnp.float32)
    scale_in = row_norm(inputs)
    normed_in = inputs * scale_in
    normed_share = (normed_in * gain_pre).astype(jnp.bfloat16)
    sent = to_devices(normed_share)
    whole_rows = tok_rows * device_count
    received = lax.all_to_all(sent, "tp", split_axis=1, concat_axis=2, tiled=True)
    item_count = received.shape[0]
    picked_in = received.reshape(item_count * device_count, slot_count, block_size)
    gate_sum = to_columns(
        jnp.einsum("tsk,skn->tsn", picked_in, gate_w, preferred_element_type=jnp.float32),
        col_onehot,
    )
    up_sum = to_columns(
        jnp.einsum("tsk,skn->tsn", picked_in, up_w, preferred_element_type=jnp.float32), col_onehot
    )
    hidden = (jax.nn.silu(gate_sum) * up_sum).astype(jnp.bfloat16)
    picked_hidden = jnp.take(hidden, col_ids, axis=1)
    terms = jnp.einsum(
        "tsn,snk->tsk", picked_hidden, down_w, preferred_element_type=jnp.float32
    ).astype(jnp.bfloat16)
    terms = terms.reshape(item_count, 1, device_count, slot_count * block_size)
    terms, gate_sum, up_sum, hidden, picked_in = (terms, gate_sum, up_sum, hidden, picked_in)
    returned = lax.all_to_all(terms, "tp", split_axis=2, concat_axis=1, tiled=True)
    branch = from_devices(returned)
    sigmoid_gate = jax.nn.sigmoid(gate_sum)
    silu_gate = gate_sum * sigmoid_gate
    picked_hidden = jnp.take(hidden, col_ids, axis=1)
    scale_out = row_norm(branch)
    unit_branch = branch * scale_out
    layer_out = (inputs + unit_branch * gain_post).astype(jnp.bfloat16)
    grad_out = cotangent.astype(jnp.float32)
    scaled_grad = grad_out * gain_post
    grad_branch_rows = (
        scale_out
        * (scaled_grad - unit_branch * jnp.mean(scaled_grad * unit_branch, axis=-1, keepdims=True))
    ).astype(jnp.bfloat16)
    post_part = jnp.sum(grad_out * unit_branch, axis=0)
    grad_sent = to_devices(grad_branch_rows)
    grad_recv = lax.all_to_all(grad_sent, "tp", split_axis=1, concat_axis=2, tiled=True)
    picked_grad = grad_recv.reshape(whole_rows, slot_count, block_size)
    grad_hidden = to_columns(
        jnp.einsum("tsk,snk->tsn", picked_grad, down_w, preferred_element_type=jnp.float32),
        col_onehot,
    )
    slot_mask = live_flag[:, None, None]
    down_grad = (
        jnp.einsum("tsn,tsk->snk", picked_hidden, picked_grad, preferred_element_type=jnp.float32)
        * slot_mask
    ).astype(jnp.bfloat16)
    grad_gate = (
        grad_hidden * up_sum * sigmoid_gate * (1.0 + gate_sum * (1.0 - sigmoid_gate))
    ).astype(jnp.bfloat16)
    grad_up = (grad_hidden * silu_gate).astype(jnp.bfloat16)
    picked_gate = jnp.take(grad_gate, col_ids, axis=1)
    picked_up = jnp.take(grad_up, col_ids, axis=1)
    gate_grad = (
        jnp.einsum("tsk,tsn->skn", picked_in, picked_gate, preferred_element_type=jnp.float32)
        * slot_mask
    ).astype(jnp.bfloat16)
    up_grad = (
        jnp.einsum("tsk,tsn->skn", picked_in, picked_up, preferred_element_type=jnp.float32)
        * slot_mask
    ).astype(jnp.bfloat16)
    mixed_sum = jnp.einsum("tsn,skn->tsk", picked_gate, gate_w, preferred_element_type=jnp.float32)
    mixed_sum = mixed_sum + jnp.einsum(
        "tsn,skn->tsk", picked_up, up_w, preferred_element_type=jnp.float32
    )
    mixed_terms = mixed_sum.astype(jnp.bfloat16).reshape(
        tok_rows, 1, device_count, slot_count * block_size
    )
    grad_normed = from_devices(
        lax.all_to_all(mixed_terms, "tp", split_axis=2, concat_axis=1, tiled=True)
    )
    pre_part = jnp.sum(grad_normed * normed_in, axis=0)
    scaled_in = grad_normed * gain_pre
    input_grad = (
        grad_out
        + scale_in
        * (scaled_in - normed_in * jnp.mean(scaled_in * normed_in, axis=-1, keepdims=True))
    ).astype(jnp.bfloat16)
    grad_back = from_behind(input_grad, "section", -1)
    pre_total, post_total = lax.psum((pre_part, post_part), "tp")
    gain_grad = jnp.stack([pre_total, post_total])[None]
    return (layer_out, grad_back, gate_grad[None], up_grad[None], down_grad[None], gain_grad)


def solution(mesh):
    return jax.shard_map(
        body,
        mesh=mesh,
        in_specs=(
            P(("section", "tp"), None),
            P(("section", "tp"), None),
            P("section", None, None),
            P("section", "tp", None, None),
            P("section", "tp", None, None),
            P("section", "tp", None, None),
            P("section", None),
        ),
        out_specs=(
            P(("section", "tp"), None),
            P(("section", "tp"), None),
            P("section", "tp", None, None),
            P("section", "tp", None, None),
            P("section", "tp", None, None),
            P("section", None, None),
        ),
        check_vma=False,
    )
```

profile of v0, /device:TPU:17, one launch (start us, length us, event | category | flops | bytes accessed | tf_op | source)
XLA Modules:
  0.0 706.9 jit_solution(14565577693920057838)
XLA Ops:
  6.8 1.3 copy.93
  8.1 16.2 %all-to-all-start = ((bf16[16,64,1,384]{3,0,2,1:T(8,128)(2,1)}), bf16[16,64,1,384]{3,0,2,1:T(8,128)(2,1)S(1)}, u32[]{:S(2)}, u32[]{:S(2)}) async-start(bf16[16,64,1,384]{3,0,2,1:T(8,128)(2,1)} %copy.93), calls=%async_computation | async-start | bytes 1572864 | tf_op jit(solution)/shard_map/all_to_all | solution.py:81
  24.6 40.4 %all-to-all-done = bf16[16,64,1,384]{3,0,2,1:T(8,128)(2,1)S(1)} async-done(((bf16[16,64,1,384]{3,0,2,1:T(8,128)(2,1)}), bf16[16,64,1,384]{3,0,2,1:T(8,128)(2,1)S(1)}, u32[]{:S(2)}, u32[]{:S(2)}) %all-to-all-start) | async-done | bytes 786464 | tf_op jit(solution)/shard_map/all_to_all | solution.py:81
  65.0 1.4 copy.127
  68.9 7.3 %fusion.2 = f32[2,1024,128]{2,0,1:T(2,128)S(1)} fusion(f32[1024,3,128]{2,0,1:T(8,128)S(1)} %convolution_bitcast_fusion.1, f32[3]{0:T(128)S(1)} %fusion.74, s32[3]{0:T(128)S(1)} %get-tuple-element.15), kind=kOutput, calls=%fused_computation.7 | convolution fusion | flops 9437196 | bytes 2621464 | tf_op jit(solution)/shard_map/tsn,sc->tcn/dot_general | solution.py:34
  76.3 7.3 %fusion.4 = f32[2,1024,128]{2,0,1:T(2,128)S(1)} fusion(f32[1024,3,128]{2,0,1:T(8,128)S(1)} %convolution_bitcast_fusion.2, f32[3]{0:T(128)S(1)} %fusion.74, s32[3]{0:T(128)S(1)} %get-tuple-element.15), kind=kOutput, calls=%fused_computation.9 | convolution fusion | flops 9437196 | bytes 2621464 | tf_op jit(solution)/shard_map/tsn,sc->tcn/dot_general | solution.py:34
  83.9 1.6 gather_fusion.1
  85.5 1.5 fusion.6
  87.0 1.7 copy.101
  88.7 3.2 reshape.221
  91.9 2.5 copy.102
  94.4 7.6 %all-to-all-start.1 = ((bf16[16,1,64,384]{3,0,1,2:T(8,128)(2,1)}), bf16[16,1,64,384]{3,0,1,2:T(8,128)(2,1)}, u32[]{:S(2)}, u32[]{:S(2)}) async-start(bf16[16,1,64,384]{3,0,1,2:T(8,128)(2,1)} %copy.102), calls=%async_computation.1 | async-start | bytes 1572864 | tf_op jit(solution)/shard_map/all_to_all | solution.py:98
  102.7 39.9 %all-to-all-done.1 = bf16[16,1,64,384]{3,0,1,2:T(8,128)(2,1)} async-done(((bf16[16,1,64,384]{3,0,1,2:T(8,128)(2,1)}), bf16[16,1,64,384]{3,0,1,2:T(8,128)(2,1)}, u32[]{:S(2)}, u32[]{:S(2)}) %all-to-all-start.1) | async-done | bytes 786464 | tf_op jit(solution)/shard_map/all_to_all | solution.py:98
  142.6 3.2 reshape.291
  145.8 2.3 fusion.54
  149.4 1.8 gather_fusion.2
  151.1 1.4 select_bitcast_fusion
  153.6 2.2 reshape.225
  155.8 1.6 copy.107
  157.4 47.8 %all_to_all.16 = bf16[16,64,1,384]{3,0,2,1:T(8,128)(2,1)S(1)} all-to-all(bf16[16,64,1,384]{3,0,2,1:T(8,128)(2,1)S(1)} %copy.107), channel_id=1, replica_groups=mesh['section'=8,'tp'=64] {'tp'}, dimensions={1} | all-to-all | bytes 1572864 | tf_op jit(solution)/shard_map/all_to_all | solution.py:114
  206.3 3.2 reshape.226
  209.6 1.6 convolution_bitcast_fusion
  211.2 7.3 %fusion = f32[2,1024,128]{2,0,1:T(2,128)S(1)} fusion(f32[1024,3,128]{2,0,1:T(8,128)S(1)} %convolution_bitcast_fusion, f32[3]{0:T(128)S(1)} %copy-done.23, s32[3]{0:T(128)S(1)} %copy-done.20), kind=kOutput, calls=%fused_computation.5 | convolution fusion | flops 9437196 | bytes 2621464 | tf_op jit(solution)/shard_map/tsn,sc->tcn/dot_general | solution.py:34
  219.9 2.7 gather_fusion.4
  222.6 1.8 gather_fusion.3
  224.4 1.6 fusion.28
  227.9 1.3 copy.113
  229.2 7.7 %all-to-all-start.3 = ((bf16[16,1,64,384]{3,0,1,2:T(8,128)(2,1)}), bf16[16,1,64,384]{3,0,1,2:T(8,128)(2,1)}, u32[]{:S(2)}, u32[]{:S(2)}) async-start(bf16[16,1,64,384]{3,0,1,2:T(8,128)(2,1)} %copy.113), calls=%async_computation.3 | async-start | bytes 1572864 | tf_op jit(solution)/shard_map/all_to_all | solution.py:147
  240.7 36.8 %all-to-all-done.3 = bf16[16,1,64,384]{3,0,1,2:T(8,128)(2,1)} async-done(((bf16[16,1,64,384]{3,0,1,2:T(8,128)(2,1)}), bf16[16,1,64,384]{3,0,1,2:T(8,128)(2,1)}, u32[]{:S(2)}, u32[]{:S(2)}) %all-to-all-start.3) | async-done | bytes 786464 | tf_op jit(solution)/shard_map/all_to_all | solution.py:147
  277.5 2.4 reshape.292
  281.4 7.8 %collective-permute-start = (bf16[16,4096]{1,0:T(8,128)(2,1)S(1)}, bf16[16,4096]{1,0:T(8,128)(2,1)S(1)}, u32[]{:S(2)}, u32[]{:S(2)}) collective-permute-start(bf16[16,4096]{1,0:T(8,128)(2,1)S(1)} %fusion.52), channel_id=1, source_target_pairs={{64,0},{128,64},{192,128},{256,192},{320,256},{384,320},{448,384},... | collective-permute-start | bytes 393224 | tf_op jit(solution)/shard_map/ppermute | solution.py:16
  289.3 416.3 %all-reduce = (f32[1,4096]{1,0:T(1,128)S(1)}, f32[1,4096]{1,0:T(1,128)S(1)}) all-reduce(f32[1,4096]{1,0:T(1,128)S(1)} %bitcast.184, f32[1,4096]{1,0:T(1,128)S(1)} %bitcast.185), channel_id=1, replica_groups=mesh['section'=8,'tp'=64] {'tp'}, use_global_device_ids=true, to_apply=%region_7.10 | all-reduce | flops 8192 | bytes 65536 | tf_op jit(solution)/shard_map/psum | solution.py:157
  (114 shorter events, 22.7 us)
Async XLA Ops:
  0.6 84.8 %copy-start = (bf16[1,3,128,128]{3,2,1,0:T(8,128)(2,1)S(1)}, bf16[1,3,128,128]{3,2,1,0:T(8,128)(2,1)}, u32[]{:S(2)}) copy-start(bf16[1,3,128,128]{3,2,1,0:T(8,128)(2,1)} %param.16) | copy-start | bytes 294916
  1.4 4.8 copy-start.31
  3.1 3.0 copy-start.26
  3.2 3.0 copy-start.24
  3.2 3.0 copy-start.18
  6.8 17.6 %copy-start.30 = (s32[1,192]{1,0:T(1,128)S(1)}, s32[1,192]{1,0:T(1,128)}, u32[]{:S(2)}) copy-start(s32[1,192]{1,0:T(1,128)} %param.17) | copy-start | bytes 2308
  8.1 56.9 %all-to-all-start = ((bf16[16,64,1,384]{3,0,2,1:T(8,128)(2,1)}), bf16[16,64,1,384]{3,0,2,1:T(8,128)(2,1)S(1)}, u32[]{:S(2)}, u32[]{:S(2)}) async-start(bf16[16,64,1,384]{3,0,2,1:T(8,128)(2,1)} %copy.93), calls=%async_computation | async-start | bytes 1572864 | tf_op jit(solution)/shard_map/all_to_all | solution.py:81
  24.5 51.8 %copy-start.22 = (f32[3]{0:T(128)}, f32[3]{0:T(128)S(1)}, u32[]{:S(2)}) copy-start(f32[3]{0:T(128)S(1)} %fusion.74) | copy-start | bytes 40
  24.5 51.7 %copy-start.19 = (s32[3]{0:T(128)}, s32[3]{0:T(128)S(1)}, u32[]{:S(2)}) copy-start(s32[3]{0:T(128)S(1)} %get-tuple-element.15) | copy-start | bytes 40
  24.5 60.9 %copy-start.28 = (pred[3]{0:T(512)(128)(4,1)}, pred[3]{0:T(512)(128)(4,1)S(1)}, u32[]{:S(2)}) copy-start(pred[3]{0:T(512)(128)(4,1)S(1)} %get-tuple-element.14) | copy-start | bytes 13
  24.6 59.3 %copy-start.21 = (s32[1024]{0:T(1024)}, s32[1024]{0:T(1024)S(1)}, u32[]{:S(2)}) copy-start(s32[1024]{0:T(1024)S(1)} %pad_clamp_fusion) | copy-start | bytes 12292
  91.9 10.1 %copy-start.32 = (pred[192]{0:T(512)(128)(4,1)S(1)}, pred[192]{0:T(512)(128)(4,1)}, u32[]{:S(2)}) copy-start(pred[192]{0:T(512)(128)(4,1)} %copy-done.31) | copy-start | bytes 580
  94.4 48.2 %all-to-all-start.1 = ((bf16[16,1,64,384]{3,0,1,2:T(8,128)(2,1)}), bf16[16,1,64,384]{3,0,1,2:T(8,128)(2,1)}, u32[]{:S(2)}, u32[]{:S(2)}) async-start(bf16[16,1,64,384]{3,0,1,2:T(8,128)(2,1)} %copy.102), calls=%async_computation.1 | async-start | bytes 1572864 | tf_op jit(solution)/shard_map/all_to_all | solution.py:98
  102.0 46.1 %copy-start.8 = (bf16[16,4096]{1,0:T(8,128)(2,1)S(1)}, bf16[16,4096]{1,0:T(8,128)(2,1)}, u32[]{:S(2)}) copy-start(bf16[16,4096]{1,0:T(8,128)(2,1)} %param.12) | copy-start | bytes 393220
  102.4 46.0 %copy-start.16 = (bf16[64,3]{0,1:T(4,128)(2,1)}, bf16[64,3]{0,1:T(4,128)(2,1)S(1)}, u32[]{:S(2)}) copy-start(bf16[64,3]{0,1:T(4,128)(2,1)S(1)} %copy.90) | copy-start | bytes 1156
  102.7 45.8 %copy-start.14 = (s32[64,3]{0,1:T(4,128)}, s32[64,3]{0,1:T(4,128)S(1)}, u32[]{:S(2)}) copy-start(s32[64,3]{0,1:T(4,128)S(1)} %copy.89) | copy-start | bytes 2308
  102.7 45.8 %copy-start.4 = (bf16[16,4096]{1,0:T(8,128)(2,1)S(1)}, bf16[16,4096]{1,0:T(8,128)(2,1)}, u32[]{:S(2)}) copy-start(bf16[16,4096]{1,0:T(8,128)(2,1)} %param.11) | copy-start | bytes 393220
  148.1 3.0 copy-start.25
  209.6 1.6 copy-start.23
  222.6 1.8 copy-start.13
  222.6 1.8 copy-start.29
  224.4 1.6 copy-start.1
  224.4 1.6 copy-start.11
  227.9 9.1 %copy-start.2 = (bf16[3,1024,128]{2,1,0:T(8,128)(2,1)S(1)}, bf16[3,1024,128]{2,1,0:T(8,128)(2,1)}, u32[]{:S(2)}) copy-start(bf16[3,1024,128]{2,1,0:T(8,128)(2,1)} %gather_fusion.4) | copy-start | bytes 2359300
  229.2 8.8 %copy-start.3 = (bf16[3,1024,128]{2,1,0:T(8,128)(2,1)S(1)}, bf16[3,1024,128]{2,1,0:T(8,128)(2,1)}, u32[]{:S(2)}) copy-start(bf16[3,1024,128]{2,1,0:T(8,128)(2,1)} %gather_fusion.3) | copy-start | bytes 2359300
  229.2 48.3 %all-to-all-start.3 = ((bf16[16,1,64,384]{3,0,1,2:T(8,128)(2,1)}), bf16[16,1,64,384]{3,0,1,2:T(8,128)(2,1)}, u32[]{:S(2)}, u32[]{:S(2)}) async-start(bf16[16,1,64,384]{3,0,1,2:T(8,128)(2,1)} %copy.113), calls=%async_computation.3 | async-start | bytes 1572864 | tf_op jit(solution)/shard_map/all_to_all | solution.py:147
  239.5 40.4 %copy-start.15 = (s32[64,3]{0,1:T(4,128)S(1)}, s32[64,3]{0,1:T(4,128)}, u32[]{:S(2)}) copy-start(s32[64,3]{0,1:T(4,128)} %copy-done.14) | copy-start | bytes 2308
  239.5 40.4 %copy-start.17 = (bf16[64,3]{0,1:T(4,128)(2,1)S(1)}, bf16[64,3]{0,1:T(4,128)(2,1)}, u32[]{:S(2)}) copy-start(bf16[64,3]{0,1:T(4,128)(2,1)} %copy-done.16) | copy-start | bytes 1156
  240.7 40.2 %copy-start.5 = (bf16[16,4096]{1,0:T(8,128)(2,1)S(1)}, bf16[16,4096]{1,0:T(8,128)(2,1)}, u32[]{:S(2)}) copy-start(bf16[16,4096]{1,0:T(8,128)(2,1)} %param.11) | copy-start | bytes 393220
  240.7 40.2 %copy-start.27 = (f32[16]{0:T(128)S(1)}, f32[16]{0:T(128)}, u32[]{:S(2)}) copy-start(f32[16]{0:T(128)} %copy-done.26) | copy-start | bytes 196
  240.7 40.5 %copy-start.9 = (bf16[16,4096]{1,0:T(8,128)(2,1)S(1)}, bf16[16,4096]{1,0:T(8,128)(2,1)}, u32[]{:S(2)}) copy-start(bf16[16,4096]{1,0:T(8,128)(2,1)} %param.12) | copy-start | bytes 393220
  281.4 424.8 %collective-permute-start = (bf16[16,4096]{1,0:T(8,128)(2,1)S(1)}, bf16[16,4096]{1,0:T(8,128)(2,1)S(1)}, u32[]{:S(2)}, u32[]{:S(2)}) collective-permute-start(bf16[16,4096]{1,0:T(8,128)(2,1)S(1)} %fusion.52), channel_id=1, source_target_pairs={{64,0},{128,64},{192,128},{256,192},{320,256},{384,320},{448,384},... | collective-permute-start | bytes 393224 | tf_op jit(solution)/shard_map/ppermute | solution.py:16
  (5 other events, 6.4 us)
where the time goes:
time: 718 us; the launch traced here: 707 us
  blocking collectives  464 us (65%)
  waiting for transfers between devices  117 us (16%)
  local copies, waits for them, and re-layouts  41.2 us (6%)
  starting transfers between devices  39.3 us (5%)
  matrix products  34.6 us (5%)
  other arithmetic  9.32 us (1%)
    psum x1, blocking collectives, body(): pre_total, post_total = lax.psum((pre_part, post_part), 'tp')  416 us
    all_to_all x1, blocking collectives, body(): lax.all_to_all(grad_sent, 'tp', split_axis=1, concat_axis=2, tiled=True)  47.8 us
    all_to_all x1, waiting for transfers between devices, body(): lax.all_to_all(sent, 'tp', split_axis=1, concat_axis=2, tiled=True)  40.4 us
    all_to_all x1, waiting for transfers between devices, body(): lax.all_to_all(terms, 'tp', split_axis=2, concat_axis=1, tiled=True)  39.9 us
    all_to_all x1, waiting for transfers between devices, body(): lax.all_to_all(mixed_terms, 'tp', split_axis=2, concat_axis=1, tiled=True)  36.8 us
    dot_general x3, matrix products, to_columns(): return jnp.einsum('tsn,sc->tcn', per_slot, col_onehot, precision=highest)  22 us
    all_to_all x1, starting transfers between devices, body(): lax.all_to_all(sent, 'tp', split_axis=1, concat_axis=2, tiled=True)  16.2 us
  transfers between devices with their start and end apart: 4, of which 3 were waited for; matrix products, arithmetic and copies ran while one was open for 1% of the time, Pallas kernels for 0%

commit v1 on v0

v1 whole, which is shorter than its diff:
```python
import functools

import jax
import jax.numpy as jnp
from jax import lax
from jax.experimental import pallas as pl
from jax.experimental.pallas import tpu as pltpu
from jax.sharding import Mesh
from jax.sharding import PartitionSpec as P

epsilon = 1e-05
f32 = jnp.float32
bf16 = jnp.bfloat16
B = 128


def dot(left, right, contract):
    return lax.dot_general(left, right, ((contract[:1], contract[1:]), ((), ())), preferred_element_type=f32)


def block_cols(index):
    return slice(index * B, (index + 1) * B)


def slot_place(place_ref, half, peer, group, slot, peers, slots):
    return place_ref[0, ((half ^ group) * peers + peer) * slots + slot]


def feature_block(place):
    return lax.shift_right_logical(jnp.maximum(place, 0), 1)


def column_masks(place):
    live = place >= 0
    odd = (place & 1) == 1
    first = jnp.where(live & jnp.logical_not(odd), 1.0, 0.0).astype(f32)
    second = jnp.where(live & odd, 1.0, 0.0).astype(f32)
    return first, second


def scaled_block(block, factor):
    return (block.astype(f32) * factor).astype(bf16)


def pick_blocks(place_ref, blocks_ref, out_ref, half, peers, slots):
    def one_peer(peer, carry):
        for group in range(2):
            for slot in range(slots):
                place = slot_place(place_ref, half, peer, group, slot, peers, slots)
                out_ref[peer, :, block_cols(group * slots + slot)] = blocks_ref[feature_block(place)]
        return carry

    lax.fori_loop(0, peers, one_peer, 0)


def sum_blocks(place_ref, got_ref, total_ref, half, peers, slots):
    total_ref[...] = jnp.zeros_like(total_ref)

    def one_peer(peer, carry):
        for group in range(2):
            for slot in range(slots):
                place = slot_place(place_ref, half, peer, group, slot, peers, slots)
                row = feature_block(place)
                term = got_ref[peer, :, block_cols(group * slots + slot)].astype(f32)
                total_ref[row] = total_ref[row] + term
        return carry

    lax.fori_loop(0, peers, one_peer, 0)


def inverse_norm(squares, width):
    return lax.rsqrt(squares / width + epsilon)


def send_normed(slots, place_ref, acts_ref, gains_ref, out_ref, blocks_ref):
    peers = out_ref.shape[0]
    half = lax.axis_index("half")
    inputs = acts_ref[...].astype(f32)
    scale_in = inverse_norm(jnp.sum(inputs * inputs, axis=1, keepdims=True), inputs.shape[1])
    normed = (inputs * scale_in * gains_ref[0, 0:1, :]).astype(bf16)
    for row in range(blocks_ref.shape[0]):
        blocks_ref[row] = normed[:, block_cols(row)]
    pick_blocks(place_ref, blocks_ref, out_ref, half, peers, slots)


def masked_weights(place_ref, half, peer, group, peers, gate_ref, up_ref, down_ref):
    slots = gate_ref.shape[1]
    ins, downs = [], []
    for slot in range(slots):
        place = slot_place(place_ref, half, peer, group, slot, peers, slots)
        first, second = column_masks(place)
        gate, up, down = gate_ref[0, slot], up_ref[0, slot], down_ref[0, slot]
        ins.append(
            jnp.concatenate(
                [
                    scaled_block(gate, first),
                    scaled_block(gate, second),
                    scaled_block(up, first),
                    scaled_block(up, second),
                ],
                axis=1,
            )
        )
        downs.append(jnp.concatenate([scaled_block(down, first), scaled_block(down, second)], axis=0))
    return jnp.concatenate(ins, axis=0), jnp.concatenate(downs, axis=1)


def forward(
    place_ref, got_ref, gate0, up0, down0, gate1, up1, down1, terms_ref, hidden_ref, dgate_ref, dup_ref
):
    peers, rows, _ = got_ref.shape
    slots = gate0.shape[1]
    wide = slots * B
    half, peer = lax.axis_index("half"), lax.axis_index("peer")
    for group, (gate, up, down) in enumerate(((gate0, up0, down0), (gate1, up1, down1))):
        w_in, w_down = masked_weights(place_ref, half, peer, group, peers, gate, up, down)
        picked = got_ref[:, :, group * wide : (group + 1) * wide].reshape(peers * rows, wide)
        sums = dot(picked, w_in, (1, 0))
        gate_sum, up_sum = sums[:, : 2 * B], sums[:, 2 * B :]
        sigmoid = jax.nn.sigmoid(gate_sum)
        silu = gate_sum * sigmoid
        hidden = (silu * up_sum).astype(bf16)
        terms = dot(hidden, w_down, (1, 0)).astype(bf16)
        terms_ref[:, :, group * wide : (group + 1) * wide] = terms.reshape(peers, rows, wide)
        hidden_ref[group] = hidden
        dgate_ref[group] = up_sum * sigmoid * (1.0 + gate_sum * (1.0 - sigmoid))
        dup_ref[group] = silu


def middle(
    slots, place_ref, got_ref, acts_ref, cot_ref, gains_ref, layer_ref, out_ref, total_ref, blocks_ref
):
    peers = got_ref.shape[0]
    rows, width = acts_ref.shape
    half = lax.axis_index("half")
    sum_blocks(place_ref, got_ref, total_ref, half, peers, slots)
    branch = total_ref[...]
    squares = jnp.sum(jnp.sum(branch * branch, axis=0), axis=1, keepdims=True)
    scale_out = inverse_norm(squares, width)
    row_id = lax.broadcasted_iota(jnp.int32, (rows, B), 0)
    mixed = jnp.zeros((rows, B), f32)
    for block in range(width // B):
        cols = block_cols(block)
        grad = cot_ref[:, cols].astype(f32)
        unit = total_ref[block] * scale_out
        gain = gains_ref[0, 1:2, cols]
        layer_ref[:, cols] = (acts_ref[:, cols].astype(f32) + unit * gain).astype(bf16)
        mixed = mixed + grad * gain * unit
        part = jnp.sum(grad * unit, axis=0, keepdims=True)
        high = part.astype(bf16).astype(f32)
        aside = jnp.where(row_id == 0, high, jnp.where(row_id == 1, part - high, 0.0))
        out_ref[block, :, 2 * slots * B :] = aside.astype(bf16)
    mean = jnp.sum(mixed, axis=1, keepdims=True) / width
    for block in range(width // B):
        cols = block_cols(block)
        scaled = cot_ref[:, cols].astype(f32) * gains_ref[0, 1:2, cols]
        unit = total_ref[block] * scale_out
        blocks_ref[block] = (scale_out * (scaled - unit * mean)).astype(bf16)
    pick_blocks(place_ref, blocks_ref, out_ref, half, peers, slots)


def backward(
    place_ref, got_ref, picked_ref, gate0, up0, down0, gate1, up1, down1, dgate_ref, dup_ref, out_ref, grads_ref
):
    peers, rows, _ = got_ref.shape
    slots = gate0.shape[1]
    wide = slots * B
    half, peer = lax.axis_index("half"), lax.axis_index("peer")
    parts = []
    for group, (gate, up, down) in enumerate(((gate0, up0, down0), (gate1, up1, down1))):
        w_in, w_down = masked_weights(place_ref, half, peer, group, peers, gate, up, down)
        cols = slice(group * wide, (group + 1) * wide)
        grad = got_ref[:, :, cols].reshape(peers * rows, wide)
        grad_hidden = dot(grad, w_down, (1, 1))
        both = jnp.concatenate([grad_hidden * dgate_ref[group], grad_hidden * dup_ref[group]], axis=1).astype(bf16)
        grads_ref[group] = both
        back = dot(both, w_in, (1, 1))
        out_ref[:, :, cols] = back.astype(bf16).reshape(peers, rows, wide)
        normed = picked_ref[:, :, cols].reshape(peers * rows, wide).astype(f32)
        part = jnp.sum(normed * back, axis=0, keepdims=True)
        parts.extend(part[:, block_cols(slot)] for slot in range(slots))
    aside = jnp.sum(got_ref[:, :, 2 * wide :].astype(f32), axis=0)
    parts.append(aside[0:1] + aside[1:2])
    row_id = lax.broadcasted_iota(jnp.int32, (rows, B), 0)
    sent = jnp.zeros((rows, B), f32)
    for index, part in enumerate(parts):
        high = part.astype(bf16).astype(f32)
        sent = jnp.where(row_id == 2 * index, high, sent)
        sent = jnp.where(row_id == 2 * index + 1, part - high, sent)
    out_ref[:, :, 2 * wide :] = jnp.broadcast_to(sent.astype(bf16)[None], (peers, rows, B))


def weight_grads(place_ref, got_ref, picked_ref, hidden_ref, grads_ref, own_ref, other_ref):
    peers, rows, _ = got_ref.shape
    slots = own_ref.shape[1]
    wide = slots * B
    half, peer = lax.axis_index("half"), lax.axis_index("peer")
    for group in (1, 0):
        target = (own_ref, other_ref)[group]
        cols = slice(group * wide, (group + 1) * wide)
        grad = got_ref[:, :, cols].reshape(peers * rows, wide)
        picked = picked_ref[:, :, cols].reshape(peers * rows, wide)
        down = dot(hidden_ref[group], grad, (0, 0))
        ins = dot(picked, grads_ref[group], (0, 0))
        for slot in range(slots):
            place = slot_place(place_ref, half, peer, group, slot, peers, slots)
            first, second = column_masks(place)
            line = ins[block_cols(slot)]
            gate = line[:, block_cols(0)] * first + line[:, block_cols(1)] * second
            up = line[:, block_cols(2)] * first + line[:, block_cols(3)] * second
            lane = down[:, block_cols(slot)]
            into = lane[block_cols(0)] * first + lane[block_cols(1)] * second
            for kind, value in enumerate((gate, up, into)):
                target[kind, slot] = value.astype(target.dtype)


def last(
    slots, place_ref, got_ref, acts_ref, cot_ref, gains_ref, grad_ref, gain_ref, total_ref, gain_total_ref
):
    peers = got_ref.shape[0]
    rows, width = acts_ref.shape
    half = lax.axis_index("half")
    sum_blocks(place_ref, got_ref, total_ref, half, peers, slots)
    gain_total_ref[...] = jnp.zeros_like(gain_total_ref)
    for peer in range(peers):
        aside = got_ref[peer, :, 2 * slots * B :].astype(f32)
        for group in range(2):
            for slot in range(slots):
                place = slot_place(place_ref, half, peer, group, slot, peers, slots)
                row = feature_block(place)
                at = 2 * (group * slots + slot)
                gain_total_ref[row] = gain_total_ref[row] + (aside[at : at + 1] + aside[at + 1 : at + 2])
        at = 4 * slots
        gain_ref[1:2, block_cols(peer)] = aside[at : at + 1] + aside[at + 1 : at + 2]
    inputs = acts_ref[...].astype(f32)
    scale_in = inverse_norm(jnp.sum(inputs * inputs, axis=1, keepdims=True), width)
    mixed = jnp.zeros((rows, B), f32)
    for block in range(width // B):
        cols = block_cols(block)
        normed_in = acts_ref[:, cols].astype(f32) * scale_in
        gain = gains_ref[0, 0:1, cols]
        mixed = mixed + total_ref[block] * gain * normed_in
        gain_ref[0:1, cols] = gain_total_ref[block] / gain
    mean = jnp.sum(mixed, axis=1, keepdims=True) / width
    for block in range(width // B):
        cols = block_cols(block)
        normed_in = acts_ref[:, cols].astype(f32) * scale_in
        scaled_in = total_ref[block] * gains_ref[0, 0:1, cols]
        grad = cot_ref[:, cols].astype(f32)
        grad_ref[:, cols] = (grad + scale_in * (scaled_in - normed_in * mean)).astype(bf16)


def finish(own_ref, other_ref, gain_ref, gain_other_ref, gate_ref, up_ref, down_ref, gain_out_ref):
    for kind, target in enumerate((gate_ref, up_ref, down_ref)):
        target[0] = (own_ref[kind] + other_ref[kind].astype(f32)).astype(bf16)
    gain_out_ref[0] = gain_ref[...] + gain_other_ref[...]


def call(kernel, name, outs, operands, scratch=()):
    vmem = pl.BlockSpec(memory_space=pltpu.VMEM)
    specs = [pl.BlockSpec(memory_space=pltpu.SMEM) if o.dtype == jnp.int32 else vmem for o in operands]
    shapes = [jax.ShapeDtypeStruct(shape, dtype) for shape, dtype in outs]
    return pl.pallas_call(
        kernel,
        name=name,
        out_shape=shapes,
        in_specs=specs,
        out_specs=[vmem] * len(shapes),
        scratch_shapes=list(scratch),
        compiler_params=pltpu.CompilerParams(vmem_limit_bytes=40 * 1024 * 1024),
    )(*operands)


def body(acts, cotangent, gains, gate_blocks, up_blocks, down_blocks, block_place):
    rows, width = acts.shape
    slots = gate_blocks.shape[1]
    peers = lax.axis_size("peer")
    features = width // B
    pairs = 2 * slots * B
    tokens = peers * rows

    def to_other(value):
        return lax.ppermute(value, "half", [(0, 1), (1, 0)])

    def exchange(value):
        return lax.all_to_all(value, "peer", split_axis=0, concat_axis=0, tiled=True)

    own = (gate_blocks, up_blocks, down_blocks)
    other = tuple(to_other(value) for value in own)
    feature_sums = pltpu.VMEM((features, rows, B), f32)
    feature_blocks = pltpu.VMEM((features, rows, B), bf16)

    (sent,) = call(
        functools.partial(send_normed, slots),
        "send_normed",
        [((peers, rows, pairs), bf16)],
        (block_place, acts, gains),
        [feature_blocks],
    )
    picked = exchange(sent)
    terms, hidden, dgate, dup = call(
        forward,
        "forward",
        [
            ((peers, rows, pairs), bf16),
            ((2, tokens, 2 * B), bf16),
            ((2, tokens, 2 * B), f32),
            ((2, tokens, 2 * B), f32),
        ],
        (block_place, picked, *own, *other),
    )
    layer_out, grad_sent = call(
        functools.partial(middle, slots),
        "middle",
        [((rows, width), bf16), ((peers, rows, pairs + B), bf16)],
        (block_place, exchange(terms), acts, cotangent, gains),
        [feature_sums, feature_blocks],
    )
    grad_got = exchange(grad_sent)
    back_sent, grads = call(
        backward,
        "backward",
        [((peers, rows, pairs + B), bf16), ((2, tokens, 4 * B), bf16)],
        (block_place, grad_got, picked, *own, *other, dgate, dup),
    )
    back_got = exchange(back_sent)
    own_grads, other_grads = call(
        weight_grads,
        "weight_grads",
        [((3, slots, B, B), f32), ((3, slots, B, B), bf16)],
        (block_place, grad_got, picked, hidden, grads),
    )
    grads_got = to_other(other_grads)
    input_grad, gain_half = call(
        functools.partial(last, slots),
        "last",
        [((rows, width), bf16), ((2, width), f32)],
        (block_place, back_got, acts, cotangent, gains),
        [feature_sums, pltpu.VMEM((features, 1, B), f32)],
    )
    count = lax.axis_size("section")
    grad_back = lax.ppermute(input_grad, "section", [(source, source - 1) for source in range(1, count)])
    gain_other = to_other(gain_half)
    gate_grad, up_grad, down_grad, gain_grad = call(
        finish,
        "finish",
        [((1, slots, B, B), bf16)] * 3 + [((1, 2, width), f32)],
        (own_grads, grads_got, gain_half, gain_other),
    )
    return (layer_out, grad_back, gate_grad, up_grad, down_grad, gain_grad)


def solution(mesh):
    sections, devices = mesh.devices.shape
    split = Mesh(mesh.devices.reshape(sections, 2, devices // 2), ("section", "half", "peer"))
    tp = ("half", "peer")
    tokens = P(("section", *tp), None)
    blocks = P("section", tp, None, None)
    return jax.shard_map(
        body,
        mesh=split,
        in_specs=(tokens, tokens, P("section", None, None), blocks, blocks, blocks, P("section", None)),
        out_specs=(tokens, tokens, blocks, blocks, blocks, P("section", None, None)),
        check_vma=False,
    )
```

time: 718 us -> 189 us (0.26); the launches traced: 707 us -> 188 us
  blocking collectives: 464 us -> 64.2 us
  waiting for transfers between devices: 117 us -> 55.1 us
  matrix products: 34.6 us -> 0 us
  local copies, waits for them, and re-layouts: 41.2 us -> 7.97 us
  Pallas kernels: 0 us -> 13.8 us
  other arithmetic: 9.32 us -> 0 us
    psum x1 -> x0, blocking collectives: 416 us -> none  [body(): pre_total, post_total = lax.psum((pre_part, post_part), 'tp')]
    all_to_all x3 -> x2, waiting for transfers between devices: 117 us -> 27.4 us  [exchange(): lax.all_to_all(value, 'peer', split_axis=0, concat_axis=0, tiled=True)]
    dot_general x14 -> x0, matrix products: 34.6 us -> none  [the longest x3 22 us: to_columns(): return jnp.einsum('tsn,sc->tcn', per_slot, col_onehot, precision=highest)]
    ppermute x1 -> x6, waiting for transfers between devices: 0.01 us -> 27.7 us  [the longest x5 26.6 us: to_other(): return lax.ppermute(value, 'half', [(0, 1), (1, 0)])]
    reshape x14 -> x0, local copies, waits for them, and re-layouts: 24.7 us -> none  [the longest x2 5.7 us: body(): terms = terms.reshape(item_count, 1, device_count, slot_count * block_size)]
    ppermute x1 -> x6, starting transfers between devices: 7.82 us -> 32.1 us  [the longest x5 24.6 us: to_other(): return lax.ppermute(value, 'half', [(0, 1), (1, 0)])]
    all_to_all x3 -> x2, starting transfers between devices: 31.5 us -> 14.3 us  [exchange(): lax.all_to_all(value, 'peer', split_axis=0, concat_axis=0, tiled=True)]
    all_to_all x1 -> x2, blocking collectives: 47.8 us -> 64.2 us  [exchange(): lax.all_to_all(value, 'peer', split_axis=0, concat_axis=0, tiled=True)]
  transfers between devices with their start and end apart: 4 -> 8, of which waited for: 3 -> 5; matrix products, arithmetic and copies ran while one was open for 1% -> 0% of each run, Pallas kernels for 0% -> 3%
where the time goes in v1:
time: 189 us; the launch traced here: 188 us
  blocking collectives  64.2 us (34%)
  waiting for transfers between devices  55.1 us (29%)
  starting transfers between devices  46.4 us (25%)
  Pallas kernels  13.8 us (7%)
  local copies, waits for them, and re-layouts  7.97 us (4%)
    all_to_all x2, blocking collectives, exchange(): lax.all_to_all(value, 'peer', split_axis=0, concat_axis=0, tiled=True)  64.2 us
    all_to_all x2, waiting for transfers between devices, exchange(): lax.all_to_all(value, 'peer', split_axis=0, concat_axis=0, tiled=True)  27.4 us
    ppermute x5, waiting for transfers between devices, to_other(): return lax.ppermute(value, 'half', [(0, 1), (1, 0)])  26.6 us
    ppermute x5, starting transfers between devices, to_other(): return lax.ppermute(value, 'half', [(0, 1), (1, 0)])  24.6 us
    all_to_all x2, starting transfers between devices, exchange(): lax.all_to_all(value, 'peer', split_axis=0, concat_axis=0, tiled=True)  14.3 us
    pallas_call x7, Pallas kernels, call(): pl.pallas_call(kernel, name=name, out_shape=shapes, in_specs=specs, out_s...  13.8 us
    unnamed x31, local copies, waits for them, and re-layouts  7.97 us
    ppermute x1, starting transfers between devices, body(): lax.ppermute(input_grad, 'section', [(source, source - 1) for source in r...  7.5 us
  transfers between devices with their start and end apart: 8, of which 5 were waited for; matrix products, arithmetic and copies ran while one was open for 0% of the time, Pallas kernels for 3%

profile of v1, /device:TPU:17, one launch (start us, length us, event | category | flops | bytes accessed | tf_op | source)
XLA Modules:
  0.0 188.2 jit_solution(4346788971301779226)
XLA Ops:
  0.6 0.0 copy-start
  0.6 0.9 copy-done
  1.5 0.8 copy-done.11
  2.3 0.7 copy-done.13
  3.0 2.2 %send_normed.1 = bf16[32,16,768]{2,1,0:T(8,128)(2,1)} custom-call(s32[1,192]{1,0:T(1,128)S(1)} %copy-done.13, bf16[16,4096]{1,0:T(8,128)(2,1)S(1)} %copy-done, f32[1,2,4096]{2,1,0:T(2,128)S(1)} %copy-done.11), custom_call_target="tpu_custom_call" | custom-call | tf_op jit(solution)/shard_map/send_normed/pallas_call | solution.py:263
  5.1 9.3 %all-to-all-start = ((bf16[32,16,768]{2,1,0:T(8,128)(2,1)}), bf16[32,16,768]{2,1,0:T(8,128)(2,1)S(1)}, u32[]{:S(2)}, u32[]{:S(2)}) async-start(bf16[32,16,768]{2,1,0:T(8,128)(2,1)} %send_normed.1), calls=%async_computation | async-start | bytes 1572864 | tf_op jit(solution)/shard_map/all_to_all | solution.py:286
  14.5 8.8 %collective-permute-start = (bf16[1,3,128,128]{3,2,1,0:T(8,128)(2,1)S(1)}, bf16[1,3,128,128]{3,2,1,0:T(8,128)(2,1)S(1)}, u32[]{:S(2)}, u32[]{:S(2)}) collective-permute-start(bf16[1,3,128,128]{3,2,1,0:T(8,128)(2,1)S(1)} %copy-done.8), channel_id=1, source_target_pairs={{0,32},{32,0},{1,33},{33,1},{2,34},{34,2},{3,35},{35,3},{4,36},{36... | collective-permute-start | bytes 294920 | tf_op jit(solution)/shard_map/ppermute | solution.py:283
  23.3 1.9 %collective-permute-start.1 = (bf16[1,3,128,128]{3,2,1,0:T(8,128)(2,1)S(1)}, bf16[1,3,128,128]{3,2,1,0:T(8,128)(2,1)S(1)}, u32[]{:S(2)}, u32[]{:S(2)}) collective-permute-start(bf16[1,3,128,128]{3,2,1,0:T(8,128)(2,1)S(1)} %copy-done.9), channel_id=1, source_target_pairs={{0,32},{32,0},{1,33},{33,1},{2,34},{34,2},{3,35},{35,3},{4,36},{36... | collective-permute-start | bytes 294920 | tf_op jit(solution)/shard_map/ppermute | solution.py:283
  25.3 7.3 %collective-permute-start.2 = (bf16[1,3,128,128]{3,2,1,0:T(8,128)(2,1)S(1)}, bf16[1,3,128,128]{3,2,1,0:T(8,128)(2,1)S(1)}, u32[]{:S(2)}, u32[]{:S(2)}) collective-permute-start(bf16[1,3,128,128]{3,2,1,0:T(8,128)(2,1)S(1)} %copy-done.10), channel_id=1, source_target_pairs={{0,32},{32,0},{1,33},{33,1},{2,34},{34,2},{3,35},{35,3},{4,36},{36... | collective-permute-start | bytes 294920 | tf_op jit(solution)/shard_map/ppermute | solution.py:283
  32.6 2.7 %collective-permute-done.1.up1 = bf16[1,3,128,128]{3,2,1,0:T(8,128)(2,1)S(1)} collective-permute-done((bf16[1,3,128,128]{3,2,1,0:T(8,128)(2,1)S(1)}, bf16[1,3,128,128]{3,2,1,0:T(8,128)(2,1)S(1)}, u32[]{:S(2)}, u32[]{:S(2)}) %collective-permute-start.1) | collective-permute-done | bytes 98336 | tf_op jit(solution)/shard_map/ppermute | solution.py:283
  35.3 10.7 %collective-permute-done.2.down1 = bf16[1,3,128,128]{3,2,1,0:T(8,128)(2,1)S(1)} collective-permute-done((bf16[1,3,128,128]{3,2,1,0:T(8,128)(2,1)S(1)}, bf16[1,3,128,128]{3,2,1,0:T(8,128)(2,1)S(1)}, u32[]{:S(2)}, u32[]{:S(2)}) %collective-permute-start.2) | collective-permute-done | bytes 98336 | tf_op jit(solution)/shard_map/ppermute | solution.py:283
  46.0 1.7 forward.1
  47.7 0.8 copy-done.5
  48.5 35.7 %all_to_all.20.got_ref = bf16[32,16,768]{2,1,0:T(8,128)(2,1)S(1)} all-to-all(bf16[32,16,768]{2,1,0:T(8,128)(2,1)S(1)} %get-tuple-element.22), channel_id=1, replica_groups=mesh['section'=8,'half'=2,'peer'=32] {'peer'}, dimensions={0} | all-to-all | bytes 1572864 | tf_op jit(solution)/shard_map/all_to_all | solution.py:286
  84.2 2.9 %middle.1 = (bf16[16,4096]{1,0:T(8,128)(2,1)}, bf16[32,16,896]{2,1,0:T(8,128)(2,1)S(1)}) custom-call(s32[1,192]{1,0:T(1,128)S(1)} %copy-done.14, bf16[32,16,768]{2,1,0:T(8,128)(2,1)S(1)} %all_to_all.20.got_ref, bf16[16,4096]{1,0:T(8,128)(2,1)S(1)} %copy-done.1, bf16[16,4096]{1,0:T(8,128)(2,1)S(1)} %copy-done.7, f32[1,2,4096]{2,1,0:T(2,128)S(1)} %copy-done.12), custom_call_target="tpu_custom_call" | custom-call | tf_op jit(solution)/shard_map/middle/pallas_call | solution.py:263
  87.1 28.5 %all_to_all.21.got_ref = bf16[32,16,896]{2,1,0:T(8,128)(2,1)S(1)} all-to-all(bf16[32,16,896]{2,1,0:T(8,128)(2,1)S(1)} %get-tuple-element.24), channel_id=1, replica_groups=mesh['section'=8,'half'=2,'peer'=32] {'peer'}, dimensions={0} | all-to-all | bytes 1835008 | tf_op jit(solution)/shard_map/all_to_all | solution.py:286
  115.5 1.8 backward.1
  117.4 1.0 copy-done.2
  118.4 0.9 copy-done.4
  119.3 4.9 %all-to-all-start.3 = ((bf16[32,16,896]{2,1,0:T(8,128)(2,1)}), bf16[32,16,896]{2,1,0:T(8,128)(2,1)S(1)}, u32[]{:S(2)}, u32[]{:S(2)}) async-start(bf16[32,16,896]{2,1,0:T(8,128)(2,1)} %copy-done.4), calls=%async_computation.3 | async-start | bytes 1835008 | tf_op jit(solution)/shard_map/all_to_all | solution.py:286
  124.3 1.2 copy-done.3
  125.5 1.0 copy-done.6
  126.5 1.9 %weight_grads.1 = (f32[3,3,128,128]{3,2,1,0:T(8,128)S(1)}, bf16[3,3,128,128]{3,2,1,0:T(8,128)(2,1)}) custom-call(s32[1,192]{1,0:T(1,128)S(1)} %copy-done.14, bf16[32,16,896]{2,1,0:T(8,128)(2,1)S(1)} %all_to_all.21.got_ref, bf16[32,16,768]{2,1,0:T(8,128)(2,1)S(1)} %all-to-all-done.got_ref.picked_ref, bf16[2,512,256]{2,1,0:T(8,128)(2,1)S(1)} %copy-done.6, ...), custom_call_target="tpu_custom_call" | custom-call | tf_op jit(solution)/shard_map/weight_grads/pallas_call | solution.py:263
  128.4 4.7 %collective-permute-start.4 = (bf16[3,3,128,128]{3,2,1,0:T(8,128)(2,1)}, bf16[3,3,128,128]{3,2,1,0:T(8,128)(2,1)S(1)}, u32[]{:S(2)}, u32[]{:S(2)}) collective-permute-start(bf16[3,3,128,128]{3,2,1,0:T(8,128)(2,1)} %get-tuple-element.32), channel_id=1, source_target_pairs={{0,32},{32,0},{1,33},{33,1},{2,34},{34,2},{3,35},{35,3},{4,36},{36... | collective-permute-start | bytes 884744 | tf_op jit(solution)/shard_map/ppermute | solution.py:283
  133.1 27.4 %all-to-all-done.3.got_ref = bf16[32,16,896]{2,1,0:T(8,128)(2,1)S(1)} async-done(((bf16[32,16,896]{2,1,0:T(8,128)(2,1)}), bf16[32,16,896]{2,1,0:T(8,128)(2,1)S(1)}, u32[]{:S(2)}, u32[]{:S(2)}) %all-to-all-start.3) | async-done | bytes 917536 | tf_op jit(solution)/shard_map/all_to_all | solution.py:286
  160.4 2.6 %last.1 = (bf16[16,4096]{1,0:T(8,128)(2,1)S(1)}, f32[2,4096]{1,0:T(2,128)S(1)}) custom-call(s32[1,192]{1,0:T(1,128)S(1)} %copy-done.14, bf16[32,16,896]{2,1,0:T(8,128)(2,1)S(1)} %all-to-all-done.3.got_ref, bf16[16,4096]{1,0:T(8,128)(2,1)S(1)} %copy-done.1, bf16[16,4096]{1,0:T(8,128)(2,1)S(1)} %copy-done.7, f32[1,2,4096]{2,1,0:T(2,128)S(1)} %copy-done.12), custom_call_target="tpu_custom_call" | custom-call | tf_op jit(solution)/shard_map/last/pallas_call | solution.py:263
  163.0 7.5 %collective-permute-start.3 = (bf16[16,4096]{1,0:T(8,128)(2,1)S(1)}, bf16[16,4096]{1,0:T(8,128)(2,1)S(1)}, u32[]{:S(2)}, u32[]{:S(2)}) collective-permute-start(bf16[16,4096]{1,0:T(8,128)(2,1)S(1)} %get-tuple-element.28), channel_id=1, source_target_pairs={{64,0},{128,64},{192,128},{256,192},{320,256},{384,320},{448,384},... | collective-permute-start | bytes 393224 | tf_op jit(solution)/shard_map/ppermute | solution.py:342
  170.5 1.9 %collective-permute-start.5 = (f32[2,4096]{1,0:T(2,128)S(1)}, f32[2,4096]{1,0:T(2,128)S(1)}, u32[]{:S(2)}, u32[]{:S(2)}) collective-permute-start(f32[2,4096]{1,0:T(2,128)S(1)} %get-tuple-element.33.gain_ref), channel_id=1, source_target_pairs={{0,32},{32,0},{1,33},{33,1},{2,34},{34,2},{3,35},{35,3},{4,36},{36... | collective-permute-start | bytes 98312 | tf_op jit(solution)/shard_map/ppermute | solution.py:283
  172.5 13.1 %collective-permute-done.5.gain_other_ref = f32[2,4096]{1,0:T(2,128)S(1)} collective-permute-done((f32[2,4096]{1,0:T(2,128)S(1)}, f32[2,4096]{1,0:T(2,128)S(1)}, u32[]{:S(2)}, u32[]{:S(2)}) %collective-permute-start.5) | collective-permute-done | bytes 32800 | tf_op jit(solution)/shard_map/ppermute | solution.py:283
  185.6 0.8 finish.1
  186.4 1.2 collective-permute-done.3
  187.5 0.7 copy.14
  (24 shorter events, 0.0 us)
Async XLA Ops:
  0.6 0.9 copy-start
  1.5 0.8 copy-start.11
  2.3 0.7 copy-start.13
  5.1 9.4 %copy-start.8 = (bf16[1,3,128,128]{3,2,1,0:T(8,128)(2,1)S(1)}, bf16[1,3,128,128]{3,2,1,0:T(8,128)(2,1)}, u32[]{:S(2)}) copy-start(bf16[1,3,128,128]{3,2,1,0:T(8,128)(2,1)} %gate0.3) | copy-start | bytes 294916
  5.1 18.2 %copy-start.9 = (bf16[1,3,128,128]{3,2,1,0:T(8,128)(2,1)S(1)}, bf16[1,3,128,128]{3,2,1,0:T(8,128)(2,1)}, u32[]{:S(2)}) copy-start(bf16[1,3,128,128]{3,2,1,0:T(8,128)(2,1)} %up0.3) | copy-start | bytes 294916
  5.1 20.1 %copy-start.10 = (bf16[1,3,128,128]{3,2,1,0:T(8,128)(2,1)S(1)}, bf16[1,3,128,128]{3,2,1,0:T(8,128)(2,1)}, u32[]{:S(2)}) copy-start(bf16[1,3,128,128]{3,2,1,0:T(8,128)(2,1)} %down0.3) | copy-start | bytes 294916
  5.1 40.9 %copy-start.14 = (s32[1,192]{1,0:T(1,128)S(1)}, s32[1,192]{1,0:T(1,128)}, u32[]{:S(2)}) copy-start(s32[1,192]{1,0:T(1,128)} %place_ref.11) | copy-start | bytes 2308
  5.1 40.9 %all-to-all-start = ((bf16[32,16,768]{2,1,0:T(8,128)(2,1)}), bf16[32,16,768]{2,1,0:T(8,128)(2,1)S(1)}, u32[]{:S(2)}, u32[]{:S(2)}) async-start(bf16[32,16,768]{2,1,0:T(8,128)(2,1)} %send_normed.1), calls=%async_computation | async-start | bytes 1572864 | tf_op jit(solution)/shard_map/all_to_all | solution.py:286
  14.5 18.1 %collective-permute-start = (bf16[1,3,128,128]{3,2,1,0:T(8,128)(2,1)S(1)}, bf16[1,3,128,128]{3,2,1,0:T(8,128)(2,1)S(1)}, u32[]{:S(2)}, u32[]{:S(2)}) collective-permute-start(bf16[1,3,128,128]{3,2,1,0:T(8,128)(2,1)S(1)} %copy-done.8), channel_id=1, source_target_pairs={{0,32},{32,0},{1,33},{33,1},{2,34},{34,2},{3,35},{35,3},{4,36},{36... | collective-permute-start | bytes 294920 | tf_op jit(solution)/shard_map/ppermute | solution.py:283
  23.3 11.9 %collective-permute-start.1 = (bf16[1,3,128,128]{3,2,1,0:T(8,128)(2,1)S(1)}, bf16[1,3,128,128]{3,2,1,0:T(8,128)(2,1)S(1)}, u32[]{:S(2)}, u32[]{:S(2)}) collective-permute-start(bf16[1,3,128,128]{3,2,1,0:T(8,128)(2,1)S(1)} %copy-done.9), channel_id=1, source_target_pairs={{0,32},{32,0},{1,33},{33,1},{2,34},{34,2},{3,35},{35,3},{4,36},{36... | collective-permute-start | bytes 294920 | tf_op jit(solution)/shard_map/ppermute | solution.py:283
  25.3 20.7 %collective-permute-start.2 = (bf16[1,3,128,128]{3,2,1,0:T(8,128)(2,1)S(1)}, bf16[1,3,128,128]{3,2,1,0:T(8,128)(2,1)S(1)}, u32[]{:S(2)}, u32[]{:S(2)}) collective-permute-start(bf16[1,3,128,128]{3,2,1,0:T(8,128)(2,1)S(1)} %copy-done.10), channel_id=1, source_target_pairs={{0,32},{32,0},{1,33},{33,1},{2,34},{34,2},{3,35},{35,3},{4,36},{36... | collective-permute-start | bytes 294920 | tf_op jit(solution)/shard_map/ppermute | solution.py:283
  47.7 0.8 copy-start.5
  48.5 35.7 %copy-start.1 = (bf16[16,4096]{1,0:T(8,128)(2,1)S(1)}, bf16[16,4096]{1,0:T(8,128)(2,1)}, u32[]{:S(2)}) copy-start(bf16[16,4096]{1,0:T(8,128)(2,1)} %acts_ref.5) | copy-start | bytes 393220
  48.5 35.7 %copy-start.7 = (bf16[16,4096]{1,0:T(8,128)(2,1)S(1)}, bf16[16,4096]{1,0:T(8,128)(2,1)}, u32[]{:S(2)}) copy-start(bf16[16,4096]{1,0:T(8,128)(2,1)} %cot_ref.3) | copy-start | bytes 393220
  48.5 35.7 %copy-start.12 = (f32[1,2,4096]{2,1,0:T(2,128)S(1)}, f32[1,2,4096]{2,1,0:T(2,128)}, u32[]{:S(2)}) copy-start(f32[1,2,4096]{2,1,0:T(2,128)} %gains_ref.5) | copy-start | bytes 98308
  117.4 1.0 copy-start.2
  118.4 0.9 copy-start.4
  119.3 41.1 %all-to-all-start.3 = ((bf16[32,16,896]{2,1,0:T(8,128)(2,1)}), bf16[32,16,896]{2,1,0:T(8,128)(2,1)S(1)}, u32[]{:S(2)}, u32[]{:S(2)}) async-start(bf16[32,16,896]{2,1,0:T(8,128)(2,1)} %copy-done.4), calls=%async_computation.3 | async-start | bytes 1835008 | tf_op jit(solution)/shard_map/all_to_all | solution.py:286
  124.2 1.2 copy-start.3
  125.5 1.0 copy-start.6
  128.4 44.1 %collective-permute-start.4 = (bf16[3,3,128,128]{3,2,1,0:T(8,128)(2,1)}, bf16[3,3,128,128]{3,2,1,0:T(8,128)(2,1)S(1)}, u32[]{:S(2)}, u32[]{:S(2)}) collective-permute-start(bf16[3,3,128,128]{3,2,1,0:T(8,128)(2,1)} %get-tuple-element.32), channel_id=1, source_target_pairs={{0,32},{32,0},{1,33},{33,1},{2,34},{34,2},{3,35},{35,3},{4,36},{36... | collective-permute-start | bytes 884744 | tf_op jit(solution)/shard_map/ppermute | solution.py:283
  163.0 24.5 %collective-permute-start.3 = (bf16[16,4096]{1,0:T(8,128)(2,1)S(1)}, bf16[16,4096]{1,0:T(8,128)(2,1)S(1)}, u32[]{:S(2)}, u32[]{:S(2)}) collective-permute-start(bf16[16,4096]{1,0:T(8,128)(2,1)S(1)} %get-tuple-element.28), channel_id=1, source_target_pairs={{64,0},{128,64},{192,128},{256,192},{320,256},{384,320},{448,384},... | collective-permute-start | bytes 393224 | tf_op jit(solution)/shard_map/ppermute | solution.py:342
  170.5 15.1 %collective-permute-start.5 = (f32[2,4096]{1,0:T(2,128)S(1)}, f32[2,4096]{1,0:T(2,128)S(1)}, u32[]{:S(2)}, u32[]{:S(2)}) collective-permute-start(f32[2,4096]{1,0:T(2,128)S(1)} %get-tuple-element.33.gain_ref), channel_id=1, source_target_pairs={{0,32},{32,0},{1,33},{33,1},{2,34},{34,2},{3,35},{35,3},{4,36},{36... | collective-permute-start | bytes 98312 | tf_op jit(solution)/shard_map/ppermute | solution.py:283

commit v2 on v1

v2 whole, which is shorter than its diff:
```python
import functools

import jax
import jax.numpy as jnp
from jax import lax
from jax.experimental import pallas as pl
from jax.experimental.pallas import tpu as pltpu
from jax.sharding import Mesh
from jax.sharding import PartitionSpec as P

epsilon = 1e-05
f32 = jnp.float32
bf16 = jnp.bfloat16
B = 128
SUMS = 3
ASIDE = 8


def dot(left, right, contract):
    return lax.dot_general(left, right, ((contract[:1], contract[1:]), ((), ())), preferred_element_type=f32)


def block_cols(index):
    return slice(index * B, (index + 1) * B)


def slot_place(place_ref, half, peer, group, slot, peers, slots):
    return place_ref[0, ((half ^ group) * peers + peer) * slots + slot]


def feature_block(place):
    return lax.shift_right_logical(jnp.maximum(place, 0), 1)


def column_masks(place):
    live = place >= 0
    odd = (place & 1) == 1
    first = jnp.where(live & jnp.logical_not(odd), 1.0, 0.0).astype(f32)
    second = jnp.where(live & odd, 1.0, 0.0).astype(f32)
    return first, second


def scaled_block(block, factor):
    return (block.astype(f32) * factor).astype(bf16)


def pick_blocks(place_ref, blocks_ref, out_ref, half, peers, slots):
    for peer in range(peers):
        for group in range(2):
            for slot in range(slots):
                place = slot_place(place_ref, half, peer, group, slot, peers, slots)
                out_ref[peer, :, block_cols(group * slots + slot)] = blocks_ref[feature_block(place)]


def sum_blocks(place_ref, got_ref, total_refs, half, peers, slots):
    for total_ref in total_refs:
        total_ref[...] = jnp.zeros_like(total_ref)
    count = 0
    for peer in range(peers):
        for group in range(2):
            for slot in range(slots):
                place = slot_place(place_ref, half, peer, group, slot, peers, slots)
                row = feature_block(place)
                total_ref = total_refs[count % len(total_refs)]
                count += 1
                term = got_ref[peer, :, block_cols(group * slots + slot)].astype(f32)
                total_ref[row] = total_ref[row] + term
    for total_ref in total_refs[1:]:
        total_refs[0][...] += total_ref[...]


def inverse_norm(squares, width):
    return lax.rsqrt(squares / width + epsilon)


def send_normed(
    slots, place_ref, acts_ref, gains_ref, out_ref, blocks_ref
):
    peers = out_ref.shape[0]
    half = lax.axis_index("za")
    inputs = acts_ref[...].astype(f32)
    scale_in = inverse_norm(jnp.sum(inputs * inputs, axis=1, keepdims=True), inputs.shape[1])
    normed = (inputs * scale_in * gains_ref[0, 0:1, :]).astype(bf16)
    for row in range(blocks_ref.shape[0]):
        blocks_ref[row] = normed[:, block_cols(row)]
    pick_blocks(place_ref, blocks_ref, out_ref, half, peers, slots)


def own_peer():
    return lax.axis_index("zb") * lax.axis_size("xc") + lax.axis_index("xc")


def masked_weights(place_ref, half, peer, group, peers, weights):
    gate_ref, up_ref, down_ref = weights[3 * group : 3 * group + 3]
    slots = gate_ref.shape[1]
    ins, downs = [], []
    for slot in range(slots):
        place = slot_place(place_ref, half, peer, group, slot, peers, slots)
        first, second = column_masks(place)
        gate, up, down = gate_ref[0, slot], up_ref[0, slot], down_ref[0, slot]
        ins.append(
            jnp.concatenate(
                [
                    scaled_block(gate, first),
                    scaled_block(gate, second),
                    scaled_block(up, first),
                    scaled_block(up, second),
                ],
                axis=1,
            )
        )
        downs.append(jnp.concatenate([scaled_block(down, first), scaled_block(down, second)], axis=0))
    return jnp.concatenate(ins, axis=0), jnp.concatenate(downs, axis=1)


def forward(
    place_ref, got_ref, gate0, up0, down0, gate1, up1, down1, terms_ref, hidden_ref, dgate_ref, dup_ref
):
    peers, rows, _ = got_ref.shape
    weights = (gate0, up0, down0, gate1, up1, down1)
    slots = gate0.shape[1]
    wide = slots * B
    half, peer = lax.axis_index("za"), own_peer()
    for group in range(2):
        w_in, w_down = masked_weights(place_ref, half, peer, group, peers, weights)
        picked = got_ref[:, :, group * wide : (group + 1) * wide].reshape(peers * rows, wide)
        sums = dot(picked, w_in, (1, 0))
        gate_sum, up_sum = sums[:, : 2 * B], sums[:, 2 * B :]
        sigmoid = jax.nn.sigmoid(gate_sum)
        silu = gate_sum * sigmoid
        hidden = (silu * up_sum).astype(bf16)
        terms = dot(hidden, w_down, (1, 0)).astype(bf16)
        terms_ref[:, :, group * wide : (group + 1) * wide] = terms.reshape(peers, rows, wide)
        hidden_ref[group] = hidden
        dgate_ref[group] = up_sum * sigmoid * (1.0 + gate_sum * (1.0 - sigmoid))
        dup_ref[group] = silu


def middle(
    slots,
    place_ref,
    got_ref,
    acts_ref,
    cot_ref,
    gains_ref,
    layer_ref,
    out_ref,
    blocks_ref,
    total_ref,
    *more_refs,
):
    peers = got_ref.shape[0]
    rows, width = acts_ref.shape
    half = lax.axis_index("za")
    sum_blocks(place_ref, got_ref, (total_ref, *more_refs), half, peers, slots)
    branch = total_ref[...]
    squares = jnp.sum(jnp.sum(branch * branch, axis=0), axis=1, keepdims=True)
    scale_out = inverse_norm(squares, width)
    row_id = lax.broadcasted_iota(jnp.int32, (rows, B), 0)
    mixed = jnp.zeros((rows, B), f32)
    for block in range(width // B):
        cols = block_cols(block)
        grad = cot_ref[:, cols].astype(f32)
        unit = total_ref[block] * scale_out
        gain = gains_ref[0, 1:2, cols]
        layer_ref[:, cols] = (acts_ref[:, cols].astype(f32) + unit * gain).astype(bf16)
        mixed = mixed + grad * gain * unit
        part = jnp.sum(grad * unit, axis=0, keepdims=True)
        high = part.astype(bf16).astype(f32)
        aside = jnp.where(row_id == 0, high, jnp.where(row_id == 1, part - high, 0.0))
        out_ref[block, :, 2 * slots * B :] = aside.astype(bf16)
    mean = jnp.sum(mixed, axis=1, keepdims=True) / width
    for block in range(width // B):
        cols = block_cols(block)
        scaled = cot_ref[:, cols].astype(f32) * gains_ref[0, 1:2, cols]
        unit = total_ref[block] * scale_out
        blocks_ref[block] = (scale_out * (scaled - unit * mean)).astype(bf16)
    pick_blocks(place_ref, blocks_ref, out_ref, half, peers, slots)


def backward(
    place_ref,
    got_ref,
    picked_ref,
    gate0,
    up0,
    down0,
    gate1,
    up1,
    down1,
    hidden_ref,
    dgate_ref,
    dup_ref,
    out_ref,
    own_grad_ref,
    other_grad_ref,
):
    peers, rows, _ = got_ref.shape
    weights = (gate0, up0, down0, gate1, up1, down1)
    slots = gate0.shape[1]
    wide = slots * B
    half, peer = lax.axis_index("za"), own_peer()
    parts = []
    for group in range(2):
        w_in, w_down = masked_weights(place_ref, half, peer, group, peers, weights)
        cols = slice(group * wide, (group + 1) * wide)
        grad = got_ref[:, :, cols].reshape(peers * rows, wide)
        grad_hidden = dot(grad, w_down, (1, 1))
        both = jnp.concatenate([grad_hidden * dgate_ref[group], grad_hidden * dup_ref[group]], axis=1).astype(bf16)
        back = dot(both, w_in, (1, 1))
        out_ref[:, :, cols] = back.astype(bf16).reshape(peers, rows, wide)
        picked = picked_ref[:, :, cols].reshape(peers * rows, wide)
        ins = dot(picked, both, (0, 0))
        down = dot(hidden_ref[group], grad, (0, 0))
        target = (own_grad_ref, other_grad_ref)[group]
        for slot in range(slots):
            place = slot_place(place_ref, half, peer, group, slot, peers, slots)
            first, second = column_masks(place)
            line = ins[block_cols(slot)]
            lane = down[:, block_cols(slot)]
            target[0, slot] = (line[:, block_cols(0)] * first + line[:, block_cols(1)] * second).astype(target.dtype)
            target[1, slot] = (line[:, block_cols(2)] * first + line[:, block_cols(3)] * second).astype(target.dtype)
            target[2, slot] = (lane[block_cols(0)] * first + lane[block_cols(1)] * second).astype(target.dtype)
        part = jnp.sum(picked.astype(f32) * back, axis=0, keepdims=True)
        parts.extend(part[:, block_cols(slot)] for slot in range(slots))
    aside = jnp.sum(got_ref[:, :, 2 * wide :].astype(f32), axis=0)
    parts.append(aside[0:1] + aside[1:2])
    row_id = lax.broadcasted_iota(jnp.int32, (rows, B), 0)
    sent = jnp.zeros((rows, B), f32)
    for index, part in enumerate(parts):
        high = part.astype(bf16).astype(f32)
        sent = jnp.where(row_id == index, high, sent)
        sent = jnp.where(row_id == ASIDE + index, part - high, sent)
    out_ref[:, :, 2 * wide :] = jnp.broadcast_to(sent.astype(bf16)[None], (peers, rows, B))


def last(
    slots,
    place_ref,
    got_ref,
    acts_ref,
    cot_ref,
    gains_ref,
    grad_ref,
    gain_ref,
    total_ref,
    *more_refs,
):
    peers = got_ref.shape[0]
    rows, width = acts_ref.shape
    half = lax.axis_index("za")
    gain_refs = more_refs[-SUMS:]
    sum_blocks(place_ref, got_ref, (total_ref, *more_refs[:-SUMS]), half, peers, slots)
    for gain_total_ref in gain_refs:
        gain_total_ref[...] = jnp.zeros_like(gain_total_ref)
    for peer in range(peers):
        aside = got_ref[peer, :, 2 * slots * B :].astype(f32)
        aside = aside[:ASIDE] + aside[ASIDE:]
        for group in range(2):
            for slot in range(slots):
                place = slot_place(place_ref, half, peer, group, slot, peers, slots)
                row = feature_block(place)
                at = group * slots + slot
                gain_total_ref = gain_refs[at % SUMS]
                gain_total_ref[row] = gain_total_ref[row] + aside[at : at + 1]
        gain_ref[1:2, block_cols(peer)] = aside[2 * slots : 2 * slots + 1]
    inputs = acts_ref[...].astype(f32)
    scale_in = inverse_norm(jnp.sum(inputs * inputs, axis=1, keepdims=True), width)
    mixed = jnp.zeros((rows, B), f32)
    for block in range(width // B):
        cols = block_cols(block)
        normed_in = acts_ref[:, cols].astype(f32) * scale_in
        gain = gains_ref[0, 0:1, cols]
        mixed = mixed + total_ref[block] * gain * normed_in
        gain_ref[0:1, cols] = sum(ref[block] for ref in gain_refs) / gain
    mean = jnp.sum(mixed, axis=1, keepdims=True) / width
    for block in range(width // B):
        cols = block_cols(block)
        normed_in = acts_ref[:, cols].astype(f32) * scale_in
        scaled_in = total_ref[block] * gains_ref[0, 0:1, cols]
        grad = cot_ref[:, cols].astype(f32)
        grad_ref[:, cols] = (grad + scale_in * (scaled_in - normed_in * mean)).astype(bf16)


def finish(own_ref, other_ref, gain_ref, gain_other_ref, gate_ref, up_ref, down_ref, gain_out):
    for kind, target in enumerate((gate_ref, up_ref, down_ref)):
        target[0] = (own_ref[kind] + other_ref[kind].astype(f32)).astype(bf16)
    gain_out[0] = gain_ref[...] + gain_other_ref[...]


def call(kernel, name, outs, operands, scratch=(), far_in=(), far_out=()):
    near, far = pl.BlockSpec(memory_space=pltpu.VMEM), pl.BlockSpec(memory_space=pl.ANY)
    scalars = pl.BlockSpec(memory_space=pltpu.SMEM)
    specs = [
        far if index in far_in else scalars if value.dtype == jnp.int32 else near
        for index, value in enumerate(operands)
    ]
    return pl.pallas_call(
        kernel,
        name=name,
        out_shape=[jax.ShapeDtypeStruct(shape, dtype) for shape, dtype in outs],
        in_specs=specs,
        out_specs=[far if index in far_out else near for index in range(len(outs))],
        scratch_shapes=list(scratch),
        compiler_params=pltpu.CompilerParams(vmem_limit_bytes=40 * 1024 * 1024),
    )(*operands)


def body(acts, cotangent, gains, gate_blocks, up_blocks, down_blocks, block_place):
    rows, width = acts.shape
    slots = gate_blocks.shape[1]
    peer_axes = ("zb", "xc")
    peers = lax.axis_size(peer_axes)
    features = width // B
    pairs = 2 * slots * B
    tokens = peers * rows

    def to_other(value):
        return lax.ppermute(value, "za", [(0, 1), (1, 0)])

    def exchange(value):
        return lax.all_to_all(value, peer_axes, split_axis=0, concat_axis=0, tiled=True)

    feature_sums = pltpu.VMEM((features, rows, B), f32)
    feature_blocks = pltpu.VMEM((features, rows, B), bf16)

    own = (gate_blocks, up_blocks, down_blocks)
    both = (*own, *(to_other(value) for value in own))
    (sent,) = call(
        functools.partial(send_normed, slots),
        "send_normed",
        [((peers, rows, pairs), bf16)],
        (block_place, acts, gains),
        [feature_blocks],
    )
    picked = exchange(sent)
    terms, hidden, dgate, dup = call(
        forward,
        "forward",
        [
            ((peers, rows, pairs), bf16),
            ((2, tokens, 2 * B), bf16),
            ((2, tokens, 2 * B), f32),
            ((2, tokens, 2 * B), f32),
        ],
        (block_place, picked, *both),
    )
    layer_out, grad_sent = call(
        functools.partial(middle, slots),
        "middle",
        [((rows, width), bf16), ((peers, rows, pairs + B), bf16)],
        (block_place, exchange(terms), acts, cotangent, gains),
        [feature_blocks] + [feature_sums] * SUMS,
    )
    weights = (3, slots, B, B)
    back_sent, own_grads, other_grads = call(
        backward,
        "backward",
        [((peers, rows, pairs + B), bf16), (weights, f32), (weights, bf16)],
        (block_place, exchange(grad_sent), picked, *both, hidden, dgate, dup),
    )
    grads_got = to_other(other_grads)
    input_grad, gain_half = call(
        functools.partial(last, slots),
        "last",
        [((rows, width), bf16), ((2, width), f32)],
        (block_place, exchange(back_sent), acts, cotangent, gains),
        [feature_sums] * SUMS + [pltpu.VMEM((features, 1, B), f32)] * SUMS,
    )
    section = ("y", "zh")
    count = lax.axis_size(section)
    grad_back = lax.ppermute(input_grad, section, [(source, source - 1) for source in range(1, count)])
    gain_other = to_other(gain_half)
    gate_grad, up_grad, down_grad, gain_grad = call(
        finish,
        "finish",
        [((1, slots, B, B), bf16)] * 3 + [((1, 2, width), f32)],
        (own_grads, grads_got, gain_half, gain_other),
    )
    return (layer_out, grad_back, gate_grad, up_grad, down_grad, gain_grad)


def solution(mesh):
    names = ("y", "zh", "za", "zb", "xc")
    split = Mesh(mesh.devices.reshape(4, 2, 2, 4, 8), names)
    section, tp = names[:2], names[2:]
    tokens = P(names, None)
    blocks = P(section, tp, None, None)
    whole = P(section, None, None)
    return jax.shard_map(
        body,
        mesh=split,
        in_specs=(tokens, tokens, whole, blocks, blocks, blocks, P(section, None)),
        out_specs=(tokens, tokens, blocks, blocks, blocks, whole),
        check_vma=False,
    )
```

time: 189 us -> 186 us (0.984)
  local copies, waits for them, and re-layouts: 7.97 us -> 3.02 us
  waiting for transfers between devices: 55.1 us -> 59.3 us
  Pallas kernels: 13.8 us -> 11.3 us
    unnamed x31 -> x21, local copies, waits for them, and re-layouts: 7.97 us -> 3.02 us
    all_to_all x2, waiting for transfers between devices: 27.4 us -> 31.5 us  [exchange(): lax.all_to_all(value, peer_axes, split_axis=0, concat_axis=0, tiled=True)]
    pallas_call x7 -> x6, Pallas kernels: 13.8 us -> 11.3 us  [call(): pl.pallas_call(kernel, name=name, out_shape=[jax.ShapeDtypeStruct(shape,...]
  transfers between devices with their start and end apart: 8 -> 8, of which waited for: 5 -> 5; matrix products, arithmetic and copies ran while one was open for 0% -> 0% of each run, Pallas kernels for 3% -> 1%
where the time goes in v2:
time: 186 us; the launch traced here: 185 us
  blocking collectives  64.2 us (35%)
  waiting for transfers between devices  59.3 us (32%)
  starting transfers between devices  46.3 us (25%)
  Pallas kernels  11.3 us (6%)
  local copies, waits for them, and re-layouts  3.02 us (2%)
    all_to_all x2, blocking collectives, exchange(): lax.all_to_all(value, peer_axes, split_axis=0, concat_axis=0, tiled=True)  64.2 us
    all_to_all x2, waiting for transfers between devices, exchange(): lax.all_to_all(value, peer_axes, split_axis=0, concat_axis=0, tiled=True)  31.5 us
    ppermute x5, waiting for transfers between devices, to_other(): return lax.ppermute(value, 'za', [(0, 1), (1, 0)])  27.5 us
    ppermute x5, starting transfers between devices, to_other(): return lax.ppermute(value, 'za', [(0, 1), (1, 0)])  24.6 us
    all_to_all x2, starting transfers between devices, exchange(): lax.all_to_all(value, peer_axes, split_axis=0, concat_axis=0, tiled=True)  14.3 us
    pallas_call x6, Pallas kernels, call(): pl.pallas_call(kernel, name=name, out_shape=[jax.ShapeDtypeStruct(shape,...  11.3 us
    ppermute x1, starting transfers between devices, body(): lax.ppermute(input_grad, section, [(source, source - 1) for source in ran...  7.48 us
  transfers between devices with their start and end apart: 8, of which 5 were waited for; matrix products, arithmetic and copies ran while one was open for 0% of the time, Pallas kernels for 1%

profile of v2, /device:TPU:17, one launch (start us, length us, event | category | flops | bytes accessed | tf_op | source)
XLA Modules:
  0.0 185.0 jit_solution(10610280491999006004)
XLA Ops:
  0.6 0.0 copy-start
  0.6 0.9 copy-done
  1.5 0.8 copy-done.6
  2.3 0.7 copy-done.8
  3.0 1.9 %send_normed.1 = bf16[32,16,768]{2,1,0:T(8,128)(2,1)} custom-call(s32[1,192]{1,0:T(1,128)S(1)} %copy-done.8, bf16[16,4096]{1,0:T(8,128)(2,1)S(1)} %copy-done, f32[1,2,4096]{2,1,0:T(2,128)S(1)} %copy-done.6), custom_call_target="tpu_custom_call" | custom-call | tf_op jit(solution)/shard_map/send_normed/pallas_call | solution.py:298
  4.9 9.3 %all-to-all-start = ((bf16[32,16,768]{2,1,0:T(8,128)(2,1)}), bf16[32,16,768]{2,1,0:T(8,128)(2,1)S(1)}, u32[]{:S(2)}, u32[]{:S(2)}) async-start(bf16[32,16,768]{2,1,0:T(8,128)(2,1)} %send_normed.1), calls=%async_computation | async-start | bytes 1572864 | tf_op jit(solution)/shard_map/all_to_all | solution.py:322
  14.3 8.8 %collective-permute-start = (bf16[1,3,128,128]{3,2,1,0:T(8,128)(2,1)S(1)}, bf16[1,3,128,128]{3,2,1,0:T(8,128)(2,1)S(1)}, u32[]{:S(2)}, u32[]{:S(2)}) collective-permute-start(bf16[1,3,128,128]{3,2,1,0:T(8,128)(2,1)S(1)} %copy-done.3), channel_id=1, source_target_pairs={{0,32},{32,0},{1,33},{33,1},{2,34},{34,2},{3,35},{35,3},{4,36},{36... | collective-permute-start | bytes 294920 | tf_op jit(solution)/shard_map/ppermute | solution.py:319
  23.1 1.9 %collective-permute-start.1 = (bf16[1,3,128,128]{3,2,1,0:T(8,128)(2,1)S(1)}, bf16[1,3,128,128]{3,2,1,0:T(8,128)(2,1)S(1)}, u32[]{:S(2)}, u32[]{:S(2)}) collective-permute-start(bf16[1,3,128,128]{3,2,1,0:T(8,128)(2,1)S(1)} %copy-done.4), channel_id=1, source_target_pairs={{0,32},{32,0},{1,33},{33,1},{2,34},{34,2},{3,35},{35,3},{4,36},{36... | collective-permute-start | bytes 294920 | tf_op jit(solution)/shard_map/ppermute | solution.py:319
  25.0 7.3 %collective-permute-start.2 = (bf16[1,3,128,128]{3,2,1,0:T(8,128)(2,1)S(1)}, bf16[1,3,128,128]{3,2,1,0:T(8,128)(2,1)S(1)}, u32[]{:S(2)}, u32[]{:S(2)}) collective-permute-start(bf16[1,3,128,128]{3,2,1,0:T(8,128)(2,1)S(1)} %copy-done.5), channel_id=1, source_target_pairs={{0,32},{32,0},{1,33},{33,1},{2,34},{34,2},{3,35},{35,3},{4,36},{36... | collective-permute-start | bytes 294920 | tf_op jit(solution)/shard_map/ppermute | solution.py:319
  32.3 0.0 collective-permute-done.gate1
  32.3 2.7 %collective-permute-done.1.up1 = bf16[1,3,128,128]{3,2,1,0:T(8,128)(2,1)S(1)} collective-permute-done((bf16[1,3,128,128]{3,2,1,0:T(8,128)(2,1)S(1)}, bf16[1,3,128,128]{3,2,1,0:T(8,128)(2,1)S(1)}, u32[]{:S(2)}, u32[]{:S(2)}) %collective-permute-start.1) | collective-permute-done | bytes 98336 | tf_op jit(solution)/shard_map/ppermute | solution.py:319
  35.0 10.7 %collective-permute-done.2.down1 = bf16[1,3,128,128]{3,2,1,0:T(8,128)(2,1)S(1)} collective-permute-done((bf16[1,3,128,128]{3,2,1,0:T(8,128)(2,1)S(1)}, bf16[1,3,128,128]{3,2,1,0:T(8,128)(2,1)S(1)}, u32[]{:S(2)}, u32[]{:S(2)}) %collective-permute-start.2) | collective-permute-done | bytes 98336 | tf_op jit(solution)/shard_map/ppermute | solution.py:319
  45.7 0.0 all-to-all-done.got_ref.picked_ref
  45.8 1.7 forward.1
  47.5 0.0 copy-start.1
  47.5 0.0 copy-start.2
  47.5 0.0 copy-start.7
  47.5 35.7 %all_to_all.20.got_ref = bf16[32,16,768]{2,1,0:T(8,128)(2,1)S(1)} all-to-all(bf16[32,16,768]{2,1,0:T(8,128)(2,1)S(1)} %get-tuple-element.21), channel_id=1, replica_groups=mesh['y'=4,'zh'=2,'za'=2,'zb'=4,'xc'=8] {'zb','xc'}, dimensions={0} | all-to-all | bytes 1572864 | tf_op jit(solution)/shard_map/all_to_all | solution.py:322
  83.2 2.3 %middle.1 = (bf16[16,4096]{1,0:T(8,128)(2,1)}, bf16[32,16,896]{2,1,0:T(8,128)(2,1)S(1)}) custom-call(s32[1,192]{1,0:T(1,128)S(1)} %copy-done.9, bf16[32,16,768]{2,1,0:T(8,128)(2,1)S(1)} %all_to_all.20.got_ref, bf16[16,4096]{1,0:T(8,128)(2,1)S(1)} %copy-done.1, bf16[16,4096]{1,0:T(8,128)(2,1)S(1)} %copy-done.2, f32[1,2,4096]{2,1,0:T(2,128)S(1)} %copy-done.7), custom_call_target="tpu_custom_call" | custom-call | tf_op jit(solution)/shard_map/middle/pallas_call | solution.py:298
  85.5 28.5 %all_to_all.21.got_ref = bf16[32,16,896]{2,1,0:T(8,128)(2,1)S(1)} all-to-all(bf16[32,16,896]{2,1,0:T(8,128)(2,1)S(1)} %get-tuple-element.23), channel_id=1, replica_groups=mesh['y'=4,'zh'=2,'za'=2,'zb'=4,'xc'=8] {'zb','xc'}, dimensions={0} | all-to-all | bytes 1835008 | tf_op jit(solution)/shard_map/all_to_all | solution.py:322
  114.0 3.1 %backward.1 = (bf16[32,16,896]{2,1,0:T(8,128)(2,1)}, f32[3,3,128,128]{3,2,1,0:T(8,128)S(1)}, bf16[3,3,128,128]{3,2,1,0:T(8,128)(2,1)S(1)}) custom-call(s32[1,192]{1,0:T(1,128)S(1)} %copy-done.9, bf16[32,16,896]{2,1,0:T(8,128)(2,1)S(1)} %all_to_all.21.got_ref, bf16[32,16,768]{2,1,0:T(8,128)(2,1)S(1)} %all-to-all-done.got_ref.picked_ref, ...), custom_call_target="tpu_custom_call" | custom-call | tf_op jit(solution)/shard_map/backward/pallas_call | solution.py:298
  117.1 4.9 %all-to-all-start.3 = ((bf16[32,16,896]{2,1,0:T(8,128)(2,1)}), bf16[32,16,896]{2,1,0:T(8,128)(2,1)S(1)}, u32[]{:S(2)}, u32[]{:S(2)}) async-start(bf16[32,16,896]{2,1,0:T(8,128)(2,1)} %get-tuple-element.27), calls=%async_computation.3 | async-start | bytes 1835008 | tf_op jit(solution)/shard_map/all_to_all | solution.py:322
  122.0 4.7 %collective-permute-start.4 = (bf16[3,3,128,128]{3,2,1,0:T(8,128)(2,1)S(1)}, bf16[3,3,128,128]{3,2,1,0:T(8,128)(2,1)S(1)}, u32[]{:S(2)}, u32[]{:S(2)}) collective-permute-start(bf16[3,3,128,128]{3,2,1,0:T(8,128)(2,1)S(1)} %get-tuple-element.30), channel_id=1, source_target_pairs={{0,32},{32,0},{1,33},{33,1},{2,34},{34,2},{3,35},{35,3},{4,36},{36... | collective-permute-start | bytes 884744 | tf_op jit(solution)/shard_map/ppermute | solution.py:319
  126.7 31.5 %all-to-all-done.3.got_ref = bf16[32,16,896]{2,1,0:T(8,128)(2,1)S(1)} async-done(((bf16[32,16,896]{2,1,0:T(8,128)(2,1)}), bf16[32,16,896]{2,1,0:T(8,128)(2,1)S(1)}, u32[]{:S(2)}, u32[]{:S(2)}) %all-to-all-start.3) | async-done | bytes 917536 | tf_op jit(solution)/shard_map/all_to_all | solution.py:322
  158.2 1.5 last.1
  159.8 7.5 %collective-permute-start.3 = (bf16[16,4096]{1,0:T(8,128)(2,1)S(1)}, bf16[16,4096]{1,0:T(8,128)(2,1)S(1)}, u32[]{:S(2)}, u32[]{:S(2)}) collective-permute-start(bf16[16,4096]{1,0:T(8,128)(2,1)S(1)} %get-tuple-element.28), channel_id=1, source_target_pairs={{64,0},{128,64},{192,128},{256,192},{320,256},{384,320},{448,384},... | collective-permute-start | bytes 393224 | tf_op jit(solution)/shard_map/ppermute | solution.py:372
  167.2 1.9 %collective-permute-start.5 = (f32[2,4096]{1,0:T(2,128)S(1)}, f32[2,4096]{1,0:T(2,128)S(1)}, u32[]{:S(2)}, u32[]{:S(2)}) collective-permute-start(f32[2,4096]{1,0:T(2,128)S(1)} %get-tuple-element.31.gain_ref), channel_id=1, source_target_pairs={{0,32},{32,0},{1,33},{33,1},{2,34},{34,2},{3,35},{35,3},{4,36},{36... | collective-permute-start | bytes 98312 | tf_op jit(solution)/shard_map/ppermute | solution.py:319
  169.2 0.0 collective-permute-done.4.other_ref
  169.2 14.0 %collective-permute-done.5.gain_other_ref = f32[2,4096]{1,0:T(2,128)S(1)} collective-permute-done((f32[2,4096]{1,0:T(2,128)S(1)}, f32[2,4096]{1,0:T(2,128)S(1)}, u32[]{:S(2)}, u32[]{:S(2)}) %collective-permute-start.5) | collective-permute-done | bytes 32800 | tf_op jit(solution)/shard_map/ppermute | solution.py:319
  183.2 0.8 finish.1
  184.0 0.4 collective-permute-done.3
  184.3 0.7 copy.14
  (13 shorter events, 0.0 us)
Async XLA Ops:
  0.6 0.9 copy-start
  1.5 0.8 copy-start.6
  2.3 0.7 copy-start.8
  4.9 9.4 %copy-start.3 = (bf16[1,3,128,128]{3,2,1,0:T(8,128)(2,1)S(1)}, bf16[1,3,128,128]{3,2,1,0:T(8,128)(2,1)}, u32[]{:S(2)}) copy-start(bf16[1,3,128,128]{3,2,1,0:T(8,128)(2,1)} %gate0.3) | copy-start | bytes 294916
  4.9 18.2 %copy-start.4 = (bf16[1,3,128,128]{3,2,1,0:T(8,128)(2,1)S(1)}, bf16[1,3,128,128]{3,2,1,0:T(8,128)(2,1)}, u32[]{:S(2)}) copy-start(bf16[1,3,128,128]{3,2,1,0:T(8,128)(2,1)} %up0.3) | copy-start | bytes 294916
  4.9 20.1 %copy-start.5 = (bf16[1,3,128,128]{3,2,1,0:T(8,128)(2,1)S(1)}, bf16[1,3,128,128]{3,2,1,0:T(8,128)(2,1)}, u32[]{:S(2)}) copy-start(bf16[1,3,128,128]{3,2,1,0:T(8,128)(2,1)} %down0.3) | copy-start | bytes 294916
  4.9 40.9 %copy-start.9 = (s32[1,192]{1,0:T(1,128)S(1)}, s32[1,192]{1,0:T(1,128)}, u32[]{:S(2)}) copy-start(s32[1,192]{1,0:T(1,128)} %place_ref.9) | copy-start | bytes 2308
  4.9 40.9 %all-to-all-start = ((bf16[32,16,768]{2,1,0:T(8,128)(2,1)}), bf16[32,16,768]{2,1,0:T(8,128)(2,1)S(1)}, u32[]{:S(2)}, u32[]{:S(2)}) async-start(bf16[32,16,768]{2,1,0:T(8,128)(2,1)} %send_normed.1), calls=%async_computation | async-start | bytes 1572864 | tf_op jit(solution)/shard_map/all_to_all | solution.py:322
  14.3 18.1 %collective-permute-start = (bf16[1,3,128,128]{3,2,1,0:T(8,128)(2,1)S(1)}, bf16[1,3,128,128]{3,2,1,0:T(8,128)(2,1)S(1)}, u32[]{:S(2)}, u32[]{:S(2)}) collective-permute-start(bf16[1,3,128,128]{3,2,1,0:T(8,128)(2,1)S(1)} %copy-done.3), channel_id=1, source_target_pairs={{0,32},{32,0},{1,33},{33,1},{2,34},{34,2},{3,35},{35,3},{4,36},{36... | collective-permute-start | bytes 294920 | tf_op jit(solution)/shard_map/ppermute | solution.py:319
  23.1 11.9 %collective-permute-start.1 = (bf16[1,3,128,128]{3,2,1,0:T(8,128)(2,1)S(1)}, bf16[1,3,128,128]{3,2,1,0:T(8,128)(2,1)S(1)}, u32[]{:S(2)}, u32[]{:S(2)}) collective-permute-start(bf16[1,3,128,128]{3,2,1,0:T(8,128)(2,1)S(1)} %copy-done.4), channel_id=1, source_target_pairs={{0,32},{32,0},{1,33},{33,1},{2,34},{34,2},{3,35},{35,3},{4,36},{36... | collective-permute-start | bytes 294920 | tf_op jit(solution)/shard_map/ppermute | solution.py:319
  25.0 20.7 %collective-permute-start.2 = (bf16[1,3,128,128]{3,2,1,0:T(8,128)(2,1)S(1)}, bf16[1,3,128,128]{3,2,1,0:T(8,128)(2,1)S(1)}, u32[]{:S(2)}, u32[]{:S(2)}) collective-permute-start(bf16[1,3,128,128]{3,2,1,0:T(8,128)(2,1)S(1)} %copy-done.5), channel_id=1, source_target_pairs={{0,32},{32,0},{1,33},{33,1},{2,34},{34,2},{3,35},{35,3},{4,36},{36... | collective-permute-start | bytes 294920 | tf_op jit(solution)/shard_map/ppermute | solution.py:319
  47.5 35.7 %copy-start.1 = (bf16[16,4096]{1,0:T(8,128)(2,1)S(1)}, bf16[16,4096]{1,0:T(8,128)(2,1)}, u32[]{:S(2)}) copy-start(bf16[16,4096]{1,0:T(8,128)(2,1)} %acts_ref.5) | copy-start | bytes 393220
  47.5 35.7 %copy-start.2 = (bf16[16,4096]{1,0:T(8,128)(2,1)S(1)}, bf16[16,4096]{1,0:T(8,128)(2,1)}, u32[]{:S(2)}) copy-start(bf16[16,4096]{1,0:T(8,128)(2,1)} %cot_ref.3) | copy-start | bytes 393220
  47.5 35.7 %copy-start.7 = (f32[1,2,4096]{2,1,0:T(2,128)S(1)}, f32[1,2,4096]{2,1,0:T(2,128)}, u32[]{:S(2)}) copy-start(f32[1,2,4096]{2,1,0:T(2,128)} %gains_ref.5) | copy-start | bytes 98308
  117.1 41.1 %all-to-all-start.3 = ((bf16[32,16,896]{2,1,0:T(8,128)(2,1)}), bf16[32,16,896]{2,1,0:T(8,128)(2,1)S(1)}, u32[]{:S(2)}, u32[]{:S(2)}) async-start(bf16[32,16,896]{2,1,0:T(8,128)(2,1)} %get-tuple-element.27), calls=%async_computation.3 | async-start | bytes 1835008 | tf_op jit(solution)/shard_map/all_to_all | solution.py:322
  122.0 47.1 %collective-permute-start.4 = (bf16[3,3,128,128]{3,2,1,0:T(8,128)(2,1)S(1)}, bf16[3,3,128,128]{3,2,1,0:T(8,128)(2,1)S(1)}, u32[]{:S(2)}, u32[]{:S(2)}) collective-permute-start(bf16[3,3,128,128]{3,2,1,0:T(8,128)(2,1)S(1)} %get-tuple-element.30), channel_id=1, source_target_pairs={{0,32},{32,0},{1,33},{33,1},{2,34},{34,2},{3,35},{35,3},{4,36},{36... | collective-permute-start | bytes 884744 | tf_op jit(solution)/shard_map/ppermute | solution.py:319
  159.8 24.6 %collective-permute-start.3 = (bf16[16,4096]{1,0:T(8,128)(2,1)S(1)}, bf16[16,4096]{1,0:T(8,128)(2,1)S(1)}, u32[]{:S(2)}, u32[]{:S(2)}) collective-permute-start(bf16[16,4096]{1,0:T(8,128)(2,1)S(1)} %get-tuple-element.28), channel_id=1, source_target_pairs={{64,0},{128,64},{192,128},{256,192},{320,256},{384,320},{448,384},... | collective-permute-start | bytes 393224 | tf_op jit(solution)/shard_map/ppermute | solution.py:372
  167.2 16.0 %collective-permute-start.5 = (f32[2,4096]{1,0:T(2,128)S(1)}, f32[2,4096]{1,0:T(2,128)S(1)}, u32[]{:S(2)}, u32[]{:S(2)}) collective-permute-start(f32[2,4096]{1,0:T(2,128)S(1)} %get-tuple-element.31.gain_ref), channel_id=1, source_target_pairs={{0,32},{32,0},{1,33},{33,1},{2,34},{34,2},{3,35},{35,3},{4,36},{36... | collective-permute-start | bytes 98312 | tf_op jit(solution)/shard_map/ppermute | solution.py:319

commit v3 on v2

--- a/solution.py
+++ b/solution.py
@@ -24,6 +24,20 @@
     return slice(index * B, (index + 1) * B)
 
 
+def slot_rows(index, rows):
+    return slice(index * rows, (index + 1) * rows)
+
+
+def slots_side_by_side(got_ref, group, slots, rows):
+    parts = [got_ref[:, slot_rows(group * slots + slot, rows), :] for slot in range(slots)]
+    return jnp.concatenate([part.reshape(-1, B) for part in parts], axis=1)
+
+
+def store_slots(out_ref, values, group, slots, rows):
+    for slot in range(slots):
+        out_ref[:, slot_rows(group * slots + slot, rows), :] = values[:, block_cols(slot)].reshape(-1, rows, B)
+
+
 def slot_place(place_ref, half, peer, group, slot, peers, slots):
     return place_ref[0, ((half ^ group) * peers + peer) * slots + slot]
 
@@ -45,16 +59,18 @@
 
 
 def pick_blocks(place_ref, blocks_ref, out_ref, half, peers, slots):
+    rows = blocks_ref.shape[1]
     for peer in range(peers):
         for group in range(2):
             for slot in range(slots):
                 place = slot_place(place_ref, half, peer, group, slot, peers, slots)
-                out_ref[peer, :, block_cols(group * slots + slot)] = blocks_ref[feature_block(place)]
+                out_ref[peer, slot_rows(group * slots + slot, rows), :] = blocks_ref[feature_block(place)]
 
 
 def sum_blocks(place_ref, got_ref, total_refs, half, peers, slots):
     for total_ref in total_refs:
         total_ref[...] = jnp.zeros_like(total_ref)
+    rows = total_refs[0].shape[1]
     count = 0
     for peer in range(peers):
         for group in range(2):
@@ -63,7 +79,7 @@
                 row = feature_block(place)
                 total_ref = total_refs[count % len(total_refs)]
                 count += 1
-                term = got_ref[peer, :, block_cols(group * slots + slot)].astype(f32)
+                term = got_ref[peer, slot_rows(group * slots + slot, rows), :].astype(f32)
                 total_ref[row] = total_ref[row] + term
     for total_ref in total_refs[1:]:
         total_refs[0][...] += total_ref[...]
@@ -116,21 +132,21 @@
 def forward(
     place_ref, got_ref, gate0, up0, down0, gate1, up1, down1, terms_ref, hidden_ref, dgate_ref, dup_ref
 ):
-    peers, rows, _ = got_ref.shape
+    peers = got_ref.shape[0]
     weights = (gate0, up0, down0, gate1, up1, down1)
     slots = gate0.shape[1]
-    wide = slots * B
+    rows = terms_ref.shape[1] // (2 * slots)
     half, peer = lax.axis_index("za"), own_peer()
     for group in range(2):
         w_in, w_down = masked_weights(place_ref, half, peer, group, peers, weights)
-        picked = got_ref[:, :, group * wide : (group + 1) * wide].reshape(peers * rows, wide)
+        picked = slots_side_by_side(got_ref, group, slots, rows)
         sums = dot(picked, w_in, (1, 0))
         gate_sum, up_sum = sums[:, : 2 * B], sums[:, 2 * B :]
         sigmoid = jax.nn.sigmoid(gate_sum)
         silu = gate_sum * sigmoid
         hidden = (silu * up_sum).astype(bf16)
         terms = dot(hidden, w_down, (1, 0)).astype(bf16)
-        terms_ref[:, :, group * wide : (group + 1) * wide] = terms.reshape(peers, rows, wide)
+        store_slots(terms_ref, terms, group, slots, rows)
         hidden_ref[group] = hidden
         dgate_ref[group] = up_sum * sigmoid * (1.0 + gate_sum * (1.0 - sigmoid))
         dup_ref[group] = silu
@@ -156,7 +172,7 @@
     branch = total_ref[...]
     squares = jnp.sum(jnp.sum(branch * branch, axis=0), axis=1, keepdims=True)
     scale_out = inverse_norm(squares, width)
-    row_id = lax.broadcasted_iota(jnp.int32, (rows, B), 0)
+    row_id = lax.broadcasted_iota(jnp.int32, (ASIDE, B), 0)
     mixed = jnp.zeros((rows, B), f32)
     for block in range(width // B):
         cols = block_cols(block)
@@ -166,9 +182,7 @@
         layer_ref[:, cols] = (acts_ref[:, cols].astype(f32) + unit * gain).astype(bf16)
         mixed = mixed + grad * gain * unit
         part = jnp.sum(grad * unit, axis=0, keepdims=True)
-        high = part.astype(bf16).astype(f32)
-        aside = jnp.where(row_id == 0, high, jnp.where(row_id == 1, part - high, 0.0))
-        out_ref[block, :, 2 * slots * B :] = aside.astype(bf16)
+        out_ref[block, 2 * slots * rows :, :] = jnp.where(row_id == 0, part, 0.0).astype(bf16)
     mean = jnp.sum(mixed, axis=1, keepdims=True) / width
     for block in range(width // B):
         cols = block_cols(block)
@@ -195,21 +209,20 @@
     own_grad_ref,
     other_grad_ref,
 ):
-    peers, rows, _ = got_ref.shape
+    peers = got_ref.shape[0]
     weights = (gate0, up0, down0, gate1, up1, down1)
     slots = gate0.shape[1]
-    wide = slots * B
+    rows = picked_ref.shape[1] // (2 * slots)
     half, peer = lax.axis_index("za"), own_peer()
     parts = []
     for group in range(2):
         w_in, w_down = masked_weights(place_ref, half, peer, group, peers, weights)
-        cols = slice(group * wide, (group + 1) * wide)
-        grad = got_ref[:, :, cols].reshape(peers * rows, wide)
+        grad = slots_side_by_side(got_ref, group, slots, rows)
         grad_hidden = dot(grad, w_down, (1, 1))
         both = jnp.concatenate([grad_hidden * dgate_ref[group], grad_hidden * dup_ref[group]], axis=1).astype(bf16)
         back = dot(both, w_in, (1, 1))
-        out_ref[:, :, cols] = back.astype(bf16).reshape(peers, rows, wide)
-        picked = picked_ref[:, :, cols].reshape(peers * rows, wide)
+        store_slots(out_ref, back.astype(bf16), group, slots, rows)
+        picked = slots_side_by_side(picked_ref, group, slots, rows)
         ins = dot(picked, both, (0, 0))
         down = dot(hidden_ref[group], grad, (0, 0))
         target = (own_grad_ref, other_grad_ref)[group]
@@ -223,15 +236,13 @@
             target[2, slot] = (lane[block_cols(0)] * first + lane[block_cols(1)] * second).astype(target.dtype)
         part = jnp.sum(picked.astype(f32) * back, axis=0, keepdims=True)
         parts.extend(part[:, block_cols(slot)] for slot in range(slots))
-    aside = jnp.sum(got_ref[:, :, 2 * wide :].astype(f32), axis=0)
-    parts.append(aside[0:1] + aside[1:2])
-    row_id = lax.broadcasted_iota(jnp.int32, (rows, B), 0)
-    sent = jnp.zeros((rows, B), f32)
+    aside = jnp.sum(got_ref[:, 2 * slots * rows :, :].astype(f32), axis=0)
+    parts.append(aside[0:1])
+    row_id = lax.broadcasted_iota(jnp.int32, (ASIDE, B), 0)
+    sent = jnp.zeros((ASIDE, B), f32)
     for index, part in enumerate(parts):
-        high = part.astype(bf16).astype(f32)
-        sent = jnp.where(row_id == index, high, sent)
-        sent = jnp.where(row_id == ASIDE + index, part - high, sent)
-    out_ref[:, :, 2 * wide :] = jnp.broadcast_to(sent.astype(bf16)[None], (peers, rows, B))
+        sent = jnp.where(row_id == index, part, sent)
+    out_ref[:, 2 * slots * rows :, :] = jnp.broadcast_to(sent.astype(bf16)[None], (peers, ASIDE, B))
 
 
 def last(
@@ -254,8 +265,7 @@
     for gain_total_ref in gain_refs:
         gain_total_ref[...] = jnp.zeros_like(gain_total_ref)
     for peer in range(peers):
-        aside = got_ref[peer, :, 2 * slots * B :].astype(f32)
-        aside = aside[:ASIDE] + aside[ASIDE:]
+        aside = got_ref[peer, 2 * slots * rows :, :].astype(f32)
         for group in range(2):
             for slot in range(slots):
                 place = slot_place(place_ref, half, peer, group, slot, peers, slots)
@@ -312,7 +322,7 @@
     peer_axes = ("zb", "xc")
     peers = lax.axis_size(peer_axes)
     features = width // B
-    pairs = 2 * slots * B
+    sent_rows = 2 * slots * rows
     tokens = peers * rows
 
     def to_other(value):
@@ -329,7 +339,7 @@
     (sent,) = call(
         functools.partial(send_normed, slots),
         "send_normed",
-        [((peers, rows, pairs), bf16)],
+        [((peers, sent_rows, B), bf16)],
         (block_place, acts, gains),
         [feature_blocks],
     )
@@ -338,7 +348,7 @@
         forward,
         "forward",
         [
-            ((peers, rows, pairs), bf16),
+            ((peers, sent_rows, B), bf16),
             ((2, tokens, 2 * B), bf16),
             ((2, tokens, 2 * B), f32),
             ((2, tokens, 2 * B), f32),
@@ -348,7 +358,7 @@
     layer_out, grad_sent = call(
         functools.partial(middle, slots),
         "middle",
-        [((rows, width), bf16), ((peers, rows, pairs + B), bf16)],
+        [((rows, width), bf16), ((peers, sent_rows + ASIDE, B), bf16)],
         (block_place, exchange(terms), acts, cotangent, gains),
         [feature_blocks] + [feature_sums] * SUMS,
     )
@@ -356,7 +366,7 @@
     back_sent, own_grads, other_grads = call(
         backward,
         "backward",
-        [((peers, rows, pairs + B), bf16), (weights, f32), (weights, bf16)],
+        [((peers, sent_rows + ASIDE, B), bf16), (weights, f32), (weights, bf16)],
         (block_place, exchange(grad_sent), picked, *both, hidden, dgate, dup),
     )
     grads_got = to_other(other_grads)

time: 186 us -> 183 us (0.984)
  the two profiles are of different devices: /device:TPU:17 before, /device:TPU:19 now
where the time goes in v3:
time: 183 us; the launch traced here: 182 us
  blocking collectives  62.9 us (34%)
  waiting for transfers between devices  56.9 us (31%)
  starting transfers between devices  47.3 us (26%)
  Pallas kernels  11.2 us (6%)
  local copies, waits for them, and re-layouts  3.02 us (2%)
    all_to_all x2, blocking collectives, exchange(): lax.all_to_all(value, peer_axes, split_axis=0, concat_axis=0, tiled=True)  62.9 us
    all_to_all x2, waiting for transfers between devices, exchange(): lax.all_to_all(value, peer_axes, split_axis=0, concat_axis=0, tiled=True)  29.4 us
    ppermute x5, waiting for transfers between devices, to_other(): return lax.ppermute(value, 'za', [(0, 1), (1, 0)])  27.5 us
    ppermute x5, starting transfers between devices, to_other(): return lax.ppermute(value, 'za', [(0, 1), (1, 0)])  24.6 us
    all_to_all x2, starting transfers between devices, exchange(): lax.all_to_all(value, peer_axes, split_axis=0, concat_axis=0, tiled=True)  14.8 us
    pallas_call x6, Pallas kernels, call(): pl.pallas_call(kernel, name=name, out_shape=[jax.ShapeDtypeStruct(shape,...  11.2 us
    ppermute x1, starting transfers between devices, body(): lax.ppermute(input_grad, section, [(source, source - 1) for source in ran...  7.83 us
  transfers between devices with their start and end apart: 8, of which 4 were waited for; matrix products, arithmetic and copies ran while one was open for 0% of the time, Pallas kernels for 1%

profile of v3, /device:TPU:19, one launch (start us, length us, event | category | flops | bytes accessed | tf_op | source)
XLA Modules:
  0.0 182.1 jit_solution(9593964539353502408)
XLA Ops:
  0.6 0.0 copy-start
  0.6 0.9 copy-done
  1.5 0.8 copy-done.6
  2.3 0.7 copy-done.8
  3.0 1.9 %send_normed.1 = bf16[32,96,128]{2,1,0:T(8,128)(2,1)} custom-call(s32[1,192]{1,0:T(1,128)S(1)} %copy-done.8, bf16[16,4096]{1,0:T(8,128)(2,1)S(1)} %copy-done, f32[1,2,4096]{2,1,0:T(2,128)S(1)} %copy-done.6), custom_call_target="tpu_custom_call" | custom-call | tf_op jit(solution)/shard_map/send_normed/pallas_call | solution.py:308
  4.9 9.5 %all-to-all-start = ((bf16[32,96,128]{2,1,0:T(8,128)(2,1)}), bf16[32,96,128]{2,1,0:T(8,128)(2,1)S(1)}, u32[]{:S(2)}, u32[]{:S(2)}) async-start(bf16[32,96,128]{2,1,0:T(8,128)(2,1)} %send_normed.1), calls=%async_computation | async-start | bytes 1572864 | tf_op jit(solution)/shard_map/all_to_all | solution.py:332
  14.4 8.8 %collective-permute-start = (bf16[1,3,128,128]{3,2,1,0:T(8,128)(2,1)S(1)}, bf16[1,3,128,128]{3,2,1,0:T(8,128)(2,1)S(1)}, u32[]{:S(2)}, u32[]{:S(2)}) collective-permute-start(bf16[1,3,128,128]{3,2,1,0:T(8,128)(2,1)S(1)} %copy-done.3), channel_id=1, source_target_pairs={{0,32},{32,0},{1,33},{33,1},{2,34},{34,2},{3,35},{35,3},{4,36},{36... | collective-permute-start | bytes 294920 | tf_op jit(solution)/shard_map/ppermute | solution.py:329
  23.2 1.9 %collective-permute-start.1 = (bf16[1,3,128,128]{3,2,1,0:T(8,128)(2,1)S(1)}, bf16[1,3,128,128]{3,2,1,0:T(8,128)(2,1)S(1)}, u32[]{:S(2)}, u32[]{:S(2)}) collective-permute-start(bf16[1,3,128,128]{3,2,1,0:T(8,128)(2,1)S(1)} %copy-done.4), channel_id=1, source_target_pairs={{0,32},{32,0},{1,33},{33,1},{2,34},{34,2},{3,35},{35,3},{4,36},{36... | collective-permute-start | bytes 294920 | tf_op jit(solution)/shard_map/ppermute | solution.py:329
  25.2 7.3 %collective-permute-start.2 = (bf16[1,3,128,128]{3,2,1,0:T(8,128)(2,1)S(1)}, bf16[1,3,128,128]{3,2,1,0:T(8,128)(2,1)S(1)}, u32[]{:S(2)}, u32[]{:S(2)}) collective-permute-start(bf16[1,3,128,128]{3,2,1,0:T(8,128)(2,1)S(1)} %copy-done.5), channel_id=1, source_target_pairs={{0,32},{32,0},{1,33},{33,1},{2,34},{34,2},{3,35},{35,3},{4,36},{36... | collective-permute-start | bytes 294920 | tf_op jit(solution)/shard_map/ppermute | solution.py:329
  32.5 0.0 collective-permute-done.gate1
  32.5 1.9 %collective-permute-done.1.up1 = bf16[1,3,128,128]{3,2,1,0:T(8,128)(2,1)S(1)} collective-permute-done((bf16[1,3,128,128]{3,2,1,0:T(8,128)(2,1)S(1)}, bf16[1,3,128,128]{3,2,1,0:T(8,128)(2,1)S(1)}, u32[]{:S(2)}, u32[]{:S(2)}) %collective-permute-start.1) | collective-permute-done | bytes 98336 | tf_op jit(solution)/shard_map/ppermute | solution.py:329
  34.4 11.0 %collective-permute-done.2.down1 = bf16[1,3,128,128]{3,2,1,0:T(8,128)(2,1)S(1)} collective-permute-done((bf16[1,3,128,128]{3,2,1,0:T(8,128)(2,1)S(1)}, bf16[1,3,128,128]{3,2,1,0:T(8,128)(2,1)S(1)}, u32[]{:S(2)}, u32[]{:S(2)}) %collective-permute-start.2) | collective-permute-done | bytes 98336 | tf_op jit(solution)/shard_map/ppermute | solution.py:329
  45.4 0.0 all-to-all-done.got_ref.picked_ref
  45.4 1.7 forward.1
  47.1 0.0 copy-start.1
  47.1 0.0 copy-start.2
  47.2 0.0 copy-start.7
  47.2 35.6 %all_to_all.20.got_ref = bf16[32,96,128]{2,1,0:T(8,128)(2,1)S(1)} all-to-all(bf16[32,96,128]{2,1,0:T(8,128)(2,1)S(1)} %get-tuple-element.21), channel_id=1, replica_groups=mesh['y'=4,'zh'=2,'za'=2,'zb'=4,'xc'=8] {'zb','xc'}, dimensions={0} | all-to-all | bytes 1572864 | tf_op jit(solution)/shard_map/all_to_all | solution.py:332
  82.8 2.3 %middle.1 = (bf16[16,4096]{1,0:T(8,128)(2,1)}, bf16[32,104,128]{2,1,0:T(8,128)(2,1)S(1)}) custom-call(s32[1,192]{1,0:T(1,128)S(1)} %copy-done.9, bf16[32,96,128]{2,1,0:T(8,128)(2,1)S(1)} %all_to_all.20.got_ref, bf16[16,4096]{1,0:T(8,128)(2,1)S(1)} %copy-done.1, bf16[16,4096]{1,0:T(8,128)(2,1)S(1)} %copy-done.2, f32[1,2,4096]{2,1,0:T(2,128)S(1)} %copy-done.7), custom_call_target="tpu_custom_call" | custom-call | tf_op jit(solution)/shard_map/middle/pallas_call | solution.py:308
  85.0 27.3 %all_to_all.21.got_ref = bf16[32,104,128]{2,1,0:T(8,128)(2,1)S(1)} all-to-all(bf16[32,104,128]{2,1,0:T(8,128)(2,1)S(1)} %get-tuple-element.23), channel_id=1, replica_groups=mesh['y'=4,'zh'=2,'za'=2,'zb'=4,'xc'=8] {'zb','xc'}, dimensions={0} | all-to-all | bytes 1703936 | tf_op jit(solution)/shard_map/all_to_all | solution.py:332
  112.3 3.1 %backward.1 = (bf16[32,104,128]{2,1,0:T(8,128)(2,1)}, f32[3,3,128,128]{3,2,1,0:T(8,128)S(1)}, bf16[3,3,128,128]{3,2,1,0:T(8,128)(2,1)S(1)}) custom-call(s32[1,192]{1,0:T(1,128)S(1)} %copy-done.9, bf16[32,104,128]{2,1,0:T(8,128)(2,1)S(1)} %all_to_all.21.got_ref, bf16[32,96,128]{2,1,0:T(8,128)(2,1)S(1)} %all-to-all-done.got_ref.picked_ref, ...), custom_call_target="tpu_custom_call" | custom-call | tf_op jit(solution)/shard_map/backward/pallas_call | solution.py:308
  115.4 5.3 %all-to-all-start.3 = ((bf16[32,104,128]{2,1,0:T(8,128)(2,1)}), bf16[32,104,128]{2,1,0:T(8,128)(2,1)S(1)}, u32[]{:S(2)}, u32[]{:S(2)}) async-start(bf16[32,104,128]{2,1,0:T(8,128)(2,1)} %get-tuple-element.27), calls=%async_computation.3 | async-start | bytes 1703936 | tf_op jit(solution)/shard_map/all_to_all | solution.py:332
  120.7 4.7 %collective-permute-start.4 = (bf16[3,3,128,128]{3,2,1,0:T(8,128)(2,1)S(1)}, bf16[3,3,128,128]{3,2,1,0:T(8,128)(2,1)S(1)}, u32[]{:S(2)}, u32[]{:S(2)}) collective-permute-start(bf16[3,3,128,128]{3,2,1,0:T(8,128)(2,1)S(1)} %get-tuple-element.30), channel_id=1, source_target_pairs={{0,32},{32,0},{1,33},{33,1},{2,34},{34,2},{3,35},{35,3},{4,36},{36... | collective-permute-start | bytes 884744 | tf_op jit(solution)/shard_map/ppermute | solution.py:329
  125.4 29.4 %all-to-all-done.3.got_ref = bf16[32,104,128]{2,1,0:T(8,128)(2,1)S(1)} async-done(((bf16[32,104,128]{2,1,0:T(8,128)(2,1)}), bf16[32,104,128]{2,1,0:T(8,128)(2,1)S(1)}, u32[]{:S(2)}, u32[]{:S(2)}) %all-to-all-start.3) | async-done | bytes 852000 | tf_op jit(solution)/shard_map/all_to_all | solution.py:332
  154.8 1.5 last.1
  156.3 7.8 %collective-permute-start.3 = (bf16[16,4096]{1,0:T(8,128)(2,1)S(1)}, bf16[16,4096]{1,0:T(8,128)(2,1)S(1)}, u32[]{:S(2)}, u32[]{:S(2)}) collective-permute-start(bf16[16,4096]{1,0:T(8,128)(2,1)S(1)} %get-tuple-element.28), channel_id=1, source_target_pairs={{64,0},{128,64},{192,128},{256,192},{320,256},{384,320},{448,384},... | collective-permute-start | bytes 393224 | tf_op jit(solution)/shard_map/ppermute | solution.py:382
  164.1 1.9 %collective-permute-start.5 = (f32[2,4096]{1,0:T(2,128)S(1)}, f32[2,4096]{1,0:T(2,128)S(1)}, u32[]{:S(2)}, u32[]{:S(2)}) collective-permute-start(f32[2,4096]{1,0:T(2,128)S(1)} %get-tuple-element.31.gain_ref), channel_id=1, source_target_pairs={{0,32},{32,0},{1,33},{33,1},{2,34},{34,2},{3,35},{35,3},{4,36},{36... | collective-permute-start | bytes 98312 | tf_op jit(solution)/shard_map/ppermute | solution.py:329
  166.0 0.0 collective-permute-done.4.other_ref
  166.0 14.6 %collective-permute-done.5.gain_other_ref = f32[2,4096]{1,0:T(2,128)S(1)} collective-permute-done((f32[2,4096]{1,0:T(2,128)S(1)}, f32[2,4096]{1,0:T(2,128)S(1)}, u32[]{:S(2)}, u32[]{:S(2)}) %collective-permute-start.5) | collective-permute-done | bytes 32800 | tf_op jit(solution)/shard_map/ppermute | solution.py:329
  180.6 0.8 finish.1
  181.4 0.0 collective-permute-done.3
  181.4 0.7 copy.14
  (13 shorter events, 0.0 us)
Async XLA Ops:
  0.6 0.9 copy-start
  1.5 0.8 copy-start.6
  2.3 0.7 copy-start.8
  4.9 9.5 %copy-start.3 = (bf16[1,3,128,128]{3,2,1,0:T(8,128)(2,1)S(1)}, bf16[1,3,128,128]{3,2,1,0:T(8,128)(2,1)}, u32[]{:S(2)}) copy-start(bf16[1,3,128,128]{3,2,1,0:T(8,128)(2,1)} %gate0.3) | copy-start | bytes 294916
  4.9 18.4 %copy-start.4 = (bf16[1,3,128,128]{3,2,1,0:T(8,128)(2,1)S(1)}, bf16[1,3,128,128]{3,2,1,0:T(8,128)(2,1)}, u32[]{:S(2)}) copy-start(bf16[1,3,128,128]{3,2,1,0:T(8,128)(2,1)} %up0.3) | copy-start | bytes 294916
  4.9 20.3 %copy-start.5 = (bf16[1,3,128,128]{3,2,1,0:T(8,128)(2,1)S(1)}, bf16[1,3,128,128]{3,2,1,0:T(8,128)(2,1)}, u32[]{:S(2)}) copy-start(bf16[1,3,128,128]{3,2,1,0:T(8,128)(2,1)} %down0.3) | copy-start | bytes 294916
  4.9 40.5 %copy-start.9 = (s32[1,192]{1,0:T(1,128)S(1)}, s32[1,192]{1,0:T(1,128)}, u32[]{:S(2)}) copy-start(s32[1,192]{1,0:T(1,128)} %place_ref.9) | copy-start | bytes 2308
  4.9 40.5 %all-to-all-start = ((bf16[32,96,128]{2,1,0:T(8,128)(2,1)}), bf16[32,96,128]{2,1,0:T(8,128)(2,1)S(1)}, u32[]{:S(2)}, u32[]{:S(2)}) async-start(bf16[32,96,128]{2,1,0:T(8,128)(2,1)} %send_normed.1), calls=%async_computation | async-start | bytes 1572864 | tf_op jit(solution)/shard_map/all_to_all | solution.py:332
  14.4 18.1 %collective-permute-start = (bf16[1,3,128,128]{3,2,1,0:T(8,128)(2,1)S(1)}, bf16[1,3,128,128]{3,2,1,0:T(8,128)(2,1)S(1)}, u32[]{:S(2)}, u32[]{:S(2)}) collective-permute-start(bf16[1,3,128,128]{3,2,1,0:T(8,128)(2,1)S(1)} %copy-done.3), channel_id=1, source_target_pairs={{0,32},{32,0},{1,33},{33,1},{2,34},{34,2},{3,35},{35,3},{4,36},{36... | collective-permute-start | bytes 294920 | tf_op jit(solution)/shard_map/ppermute | solution.py:329
  23.2 11.1 %collective-permute-start.1 = (bf16[1,3,128,128]{3,2,1,0:T(8,128)(2,1)S(1)}, bf16[1,3,128,128]{3,2,1,0:T(8,128)(2,1)S(1)}, u32[]{:S(2)}, u32[]{:S(2)}) collective-permute-start(bf16[1,3,128,128]{3,2,1,0:T(8,128)(2,1)S(1)} %copy-done.4), channel_id=1, source_target_pairs={{0,32},{32,0},{1,33},{33,1},{2,34},{34,2},{3,35},{35,3},{4,36},{36... | collective-permute-start | bytes 294920 | tf_op jit(solution)/shard_map/ppermute | solution.py:329
  25.2 20.2 %collective-permute-start.2 = (bf16[1,3,128,128]{3,2,1,0:T(8,128)(2,1)S(1)}, bf16[1,3,128,128]{3,2,1,0:T(8,128)(2,1)S(1)}, u32[]{:S(2)}, u32[]{:S(2)}) collective-permute-start(bf16[1,3,128,128]{3,2,1,0:T(8,128)(2,1)S(1)} %copy-done.5), channel_id=1, source_target_pairs={{0,32},{32,0},{1,33},{33,1},{2,34},{34,2},{3,35},{35,3},{4,36},{36... | collective-permute-start | bytes 294920 | tf_op jit(solution)/shard_map/ppermute | solution.py:329
  47.1 35.6 %copy-start.1 = (bf16[16,4096]{1,0:T(8,128)(2,1)S(1)}, bf16[16,4096]{1,0:T(8,128)(2,1)}, u32[]{:S(2)}) copy-start(bf16[16,4096]{1,0:T(8,128)(2,1)} %acts_ref.5) | copy-start | bytes 393220
  47.1 35.6 %copy-start.2 = (bf16[16,4096]{1,0:T(8,128)(2,1)S(1)}, bf16[16,4096]{1,0:T(8,128)(2,1)}, u32[]{:S(2)}) copy-start(bf16[16,4096]{1,0:T(8,128)(2,1)} %cot_ref.3) | copy-start | bytes 393220
  47.2 35.6 %copy-start.7 = (f32[1,2,4096]{2,1,0:T(2,128)S(1)}, f32[1,2,4096]{2,1,0:T(2,128)}, u32[]{:S(2)}) copy-start(f32[1,2,4096]{2,1,0:T(2,128)} %gains_ref.5) | copy-start | bytes 98308
  115.4 39.4 %all-to-all-start.3 = ((bf16[32,104,128]{2,1,0:T(8,128)(2,1)}), bf16[32,104,128]{2,1,0:T(8,128)(2,1)S(1)}, u32[]{:S(2)}, u32[]{:S(2)}) async-start(bf16[32,104,128]{2,1,0:T(8,128)(2,1)} %get-tuple-element.27), calls=%async_computation.3 | async-start | bytes 1703936 | tf_op jit(solution)/shard_map/all_to_all | solution.py:332
  120.7 45.3 %collective-permute-start.4 = (bf16[3,3,128,128]{3,2,1,0:T(8,128)(2,1)S(1)}, bf16[3,3,128,128]{3,2,1,0:T(8,128)(2,1)S(1)}, u32[]{:S(2)}, u32[]{:S(2)}) collective-permute-start(bf16[3,3,128,128]{3,2,1,0:T(8,128)(2,1)S(1)} %get-tuple-element.30), channel_id=1, source_target_pairs={{0,32},{32,0},{1,33},{33,1},{2,34},{34,2},{3,35},{35,3},{4,36},{36... | collective-permute-start | bytes 884744 | tf_op jit(solution)/shard_map/ppermute | solution.py:329
  156.3 25.1 %collective-permute-start.3 = (bf16[16,4096]{1,0:T(8,128)(2,1)S(1)}, bf16[16,4096]{1,0:T(8,128)(2,1)S(1)}, u32[]{:S(2)}, u32[]{:S(2)}) collective-permute-start(bf16[16,4096]{1,0:T(8,128)(2,1)S(1)} %get-tuple-element.28), channel_id=1, source_target_pairs={{64,0},{128,64},{192,128},{256,192},{320,256},{384,320},{448,384},... | collective-permute-start | bytes 393224 | tf_op jit(solution)/shard_map/ppermute | solution.py:382
  164.1 16.5 %collective-permute-start.5 = (f32[2,4096]{1,0:T(2,128)S(1)}, f32[2,4096]{1,0:T(2,128)S(1)}, u32[]{:S(2)}, u32[]{:S(2)}) collective-permute-start(f32[2,4096]{1,0:T(2,128)S(1)} %get-tuple-element.31.gain_ref), channel_id=1, source_target_pairs={{0,32},{32,0},{1,33},{33,1},{2,34},{34,2},{3,35},{35,3},{4,36},{36... | collective-permute-start | bytes 98312 | tf_op jit(solution)/shard_map/ppermute | solution.py:329

commit v4 on v3

--- a/solution.py
+++ b/solution.py
@@ -55,7 +55,7 @@
 
 
 def scaled_block(block, factor):
-    return (block.astype(f32) * factor).astype(bf16)
+    return block * jnp.full(block.shape, factor, f32).astype(bf16)
 
 
 def pick_blocks(place_ref, blocks_ref, out_ref, half, peers, slots):
@@ -106,50 +106,55 @@
     return lax.axis_index("zb") * lax.axis_size("xc") + lax.axis_index("xc")
 
 
-def masked_weights(place_ref, half, peer, group, peers, weights):
-    gate_ref, up_ref, down_ref = weights[3 * group : 3 * group + 3]
-    slots = gate_ref.shape[1]
-    ins, downs = [], []
-    for slot in range(slots):
-        place = slot_place(place_ref, half, peer, group, slot, peers, slots)
-        first, second = column_masks(place)
-        gate, up, down = gate_ref[0, slot], up_ref[0, slot], down_ref[0, slot]
-        ins.append(
-            jnp.concatenate(
-                [
-                    scaled_block(gate, first),
-                    scaled_block(gate, second),
-                    scaled_block(up, first),
-                    scaled_block(up, second),
-                ],
-                axis=1,
-            )
-        )
-        downs.append(jnp.concatenate([scaled_block(down, first), scaled_block(down, second)], axis=0))
-    return jnp.concatenate(ins, axis=0), jnp.concatenate(downs, axis=1)
-
-
-def forward(
-    place_ref, got_ref, gate0, up0, down0, gate1, up1, down1, terms_ref, hidden_ref, dgate_ref, dup_ref
-):
+def slot_masks(place_ref, half, peer, group, peers, slots):
+    return [
+        column_masks(slot_place(place_ref, half, peer, group, slot, peers, slots)) for slot in range(slots)
+    ]
+
+
+def masked_in(masks, gate_ref, up_ref):
+    lines = []
+    for slot, (first, second) in enumerate(masks):
+        gate, up = gate_ref[0, slot], up_ref[0, slot]
+        parts = [scaled_block(block, mask) for block in (gate, up) for mask in (first, second)]
+        lines.append(jnp.concatenate(parts, axis=1))
+    return jnp.concatenate(lines, axis=0)
+
+
+def masked_down(masks, down_ref):
+    parts = []
+    for slot, (first, second) in enumerate(masks):
+        down = down_ref[0, slot]
+        parts.append(jnp.concatenate([scaled_block(down, first), scaled_block(down, second)], axis=0))
+    return jnp.concatenate(parts, axis=1)
+
+
+def gates(place_ref, got_ref, gate0, up0, gate1, up1, hidden_ref, dgate_ref, dup_ref):
     peers = got_ref.shape[0]
-    weights = (gate0, up0, down0, gate1, up1, down1)
     slots = gate0.shape[1]
-    rows = terms_ref.shape[1] // (2 * slots)
+    rows = got_ref.shape[1] // (2 * slots)
     half, peer = lax.axis_index("za"), own_peer()
-    for group in range(2):
-        w_in, w_down = masked_weights(place_ref, half, peer, group, peers, weights)
+    for group, (gate, up) in enumerate(((gate0, up0), (gate1, up1))):
+        masks = slot_masks(place_ref, half, peer, group, peers, slots)
         picked = slots_side_by_side(got_ref, group, slots, rows)
-        sums = dot(picked, w_in, (1, 0))
+        sums = dot(picked, masked_in(masks, gate, up), (1, 0))
         gate_sum, up_sum = sums[:, : 2 * B], sums[:, 2 * B :]
         sigmoid = jax.nn.sigmoid(gate_sum)
         silu = gate_sum * sigmoid
-        hidden = (silu * up_sum).astype(bf16)
-        terms = dot(hidden, w_down, (1, 0)).astype(bf16)
-        store_slots(terms_ref, terms, group, slots, rows)
-        hidden_ref[group] = hidden
+        hidden_ref[group] = (silu * up_sum).astype(bf16)
         dgate_ref[group] = up_sum * sigmoid * (1.0 + gate_sum * (1.0 - sigmoid))
         dup_ref[group] = silu
+
+
+def down_terms(place_ref, hidden_ref, down0, down1, terms_ref):
+    peers = terms_ref.shape[0]
+    slots = down0.shape[1]
+    rows = terms_ref.shape[1] // (2 * slots)
+    half, peer = lax.axis_index("za"), own_peer()
+    for group, down in enumerate((down0, down1)):
+        masks = slot_masks(place_ref, half, peer, group, peers, slots)
+        terms = dot(hidden_ref[group], masked_down(masks, down), (1, 0)).astype(bf16)
+        store_slots(terms_ref, terms, group, slots, rows)
 
 
 def middle(
@@ -210,13 +215,13 @@
     other_grad_ref,
 ):
     peers = got_ref.shape[0]
-    weights = (gate0, up0, down0, gate1, up1, down1)
     slots = gate0.shape[1]
     rows = picked_ref.shape[1] // (2 * slots)
     half, peer = lax.axis_index("za"), own_peer()
     parts = []
-    for group in range(2):
-        w_in, w_down = masked_weights(place_ref, half, peer, group, peers, weights)
+    for group, (gate, up, down_w) in enumerate(((gate0, up0, down0), (gate1, up1, down1))):
+        masks = slot_masks(place_ref, half, peer, group, peers, slots)
+        w_in, w_down = masked_in(masks, gate, up), masked_down(masks, down_w)
         grad = slots_side_by_side(got_ref, group, slots, rows)
         grad_hidden = dot(grad, w_down, (1, 1))
         both = jnp.concatenate([grad_hidden * dgate_ref[group], grad_hidden * dup_ref[group]], axis=1).astype(bf16)
@@ -227,8 +232,7 @@
         down = dot(hidden_ref[group], grad, (0, 0))
         target = (own_grad_ref, other_grad_ref)[group]
         for slot in range(slots):
-            place = slot_place(place_ref, half, peer, group, slot, peers, slots)
-            first, second = column_masks(place)
+            first, second = masks[slot]
             line = ins[block_cols(slot)]
             lane = down[:, block_cols(slot)]
             target[0, slot] = (line[:, block_cols(0)] * first + line[:, block_cols(1)] * second).astype(target.dtype)
@@ -344,16 +348,17 @@
         [feature_blocks],
     )
     picked = exchange(sent)
-    terms, hidden, dgate, dup = call(
-        forward,
-        "forward",
-        [
-            ((peers, sent_rows, B), bf16),
-            ((2, tokens, 2 * B), bf16),
-            ((2, tokens, 2 * B), f32),
-            ((2, tokens, 2 * B), f32),
-        ],
-        (block_place, picked, *both),
+    hidden, dgate, dup = call(
+        gates,
+        "gates",
+        [((2, tokens, 2 * B), bf16), ((2, tokens, 2 * B), f32), ((2, tokens, 2 * B), f32)],
+        (block_place, picked, both[0], both[1], both[3], both[4]),
+    )
+    (terms,) = call(
+        down_terms,
+        "down_terms",
+        [((peers, sent_rows, B), bf16)],
+        (block_place, hidden, both[2], both[5]),
     )
     layer_out, grad_sent = call(
         functools.partial(middle, slots),

time: 183 us -> 182 us (level)
  the two profiles are of different devices: /device:TPU:19 before, /device:TPU:27 now
where the time goes in v4:
time: 182 us; the launch traced here: 181 us
  blocking collectives  62.1 us (34%)
  waiting for transfers between devices  56 us (31%)
  starting transfers between devices  47.6 us (26%)
  Pallas kernels  11.8 us (6%)
  local copies, waits for them, and re-layouts  3.02 us (2%)
    all_to_all x2, blocking collectives, exchange(): lax.all_to_all(value, peer_axes, split_axis=0, concat_axis=0, tiled=True)  62.1 us
    all_to_all x2, waiting for transfers between devices, exchange(): lax.all_to_all(value, peer_axes, split_axis=0, concat_axis=0, tiled=True)  39.8 us
    ppermute x5, starting transfers between devices, to_other(): return lax.ppermute(value, 'za', [(0, 1), (1, 0)])  24.6 us
    ppermute x5, waiting for transfers between devices, to_other(): return lax.ppermute(value, 'za', [(0, 1), (1, 0)])  16.2 us
    all_to_all x2, starting transfers between devices, exchange(): lax.all_to_all(value, peer_axes, split_axis=0, concat_axis=0, tiled=True)  14.8 us
    pallas_call x7, Pallas kernels, call(): pl.pallas_call(kernel, name=name, out_shape=[jax.ShapeDtypeStruct(shape,...  11.8 us
    ppermute x1, starting transfers between devices, body(): lax.ppermute(input_grad, section, [(source, source - 1) for source in ran...  8.14 us
  transfers between devices with their start and end apart: 8, of which 4 were waited for; matrix products, arithmetic and copies ran while one was open for 0% of the time, Pallas kernels for 2%

profile of v4, /device:TPU:27, one launch (start us, length us, event | category | flops | bytes accessed | tf_op | source)
XLA Modules:
  0.0 181.3 jit_solution(4089517828965988957)
XLA Ops:
  0.6 0.0 copy-start
  0.6 0.9 copy-done
  1.5 0.8 copy-done.6
  2.3 0.7 copy-done.8
  3.0 1.9 %send_normed.1 = bf16[32,96,128]{2,1,0:T(8,128)(2,1)} custom-call(s32[1,192]{1,0:T(1,128)S(1)} %copy-done.8, bf16[16,4096]{1,0:T(8,128)(2,1)S(1)} %copy-done, f32[1,2,4096]{2,1,0:T(2,128)S(1)} %copy-done.6), custom_call_target="tpu_custom_call" | custom-call | tf_op jit(solution)/shard_map/send_normed/pallas_call | solution.py:312
  4.9 9.5 %all-to-all-start = ((bf16[32,96,128]{2,1,0:T(8,128)(2,1)}), bf16[32,96,128]{2,1,0:T(8,128)(2,1)S(1)}, u32[]{:S(2)}, u32[]{:S(2)}) async-start(bf16[32,96,128]{2,1,0:T(8,128)(2,1)} %send_normed.1), calls=%async_computation | async-start | bytes 1572864 | tf_op jit(solution)/shard_map/all_to_all | solution.py:336
  14.4 8.8 %collective-permute-start = (bf16[1,3,128,128]{3,2,1,0:T(8,128)(2,1)S(1)}, bf16[1,3,128,128]{3,2,1,0:T(8,128)(2,1)S(1)}, u32[]{:S(2)}, u32[]{:S(2)}) collective-permute-start(bf16[1,3,128,128]{3,2,1,0:T(8,128)(2,1)S(1)} %copy-done.4), channel_id=1, source_target_pairs={{0,32},{32,0},{1,33},{33,1},{2,34},{34,2},{3,35},{35,3},{4,36},{36... | collective-permute-start | bytes 294920 | tf_op jit(solution)/shard_map/ppermute | solution.py:333
  23.2 1.9 %collective-permute-start.1 = (bf16[1,3,128,128]{3,2,1,0:T(8,128)(2,1)S(1)}, bf16[1,3,128,128]{3,2,1,0:T(8,128)(2,1)S(1)}, u32[]{:S(2)}, u32[]{:S(2)}) collective-permute-start(bf16[1,3,128,128]{3,2,1,0:T(8,128)(2,1)S(1)} %copy-done.5), channel_id=1, source_target_pairs={{0,32},{32,0},{1,33},{33,1},{2,34},{34,2},{3,35},{35,3},{4,36},{36... | collective-permute-start | bytes 294920 | tf_op jit(solution)/shard_map/ppermute | solution.py:333
  25.2 7.3 %collective-permute-start.2 = (bf16[1,3,128,128]{3,2,1,0:T(8,128)(2,1)S(1)}, bf16[1,3,128,128]{3,2,1,0:T(8,128)(2,1)S(1)}, u32[]{:S(2)}, u32[]{:S(2)}) collective-permute-start(bf16[1,3,128,128]{3,2,1,0:T(8,128)(2,1)S(1)} %copy-done.3), channel_id=1, source_target_pairs={{0,32},{32,0},{1,33},{33,1},{2,34},{34,2},{3,35},{35,3},{4,36},{36... | collective-permute-start | bytes 294920 | tf_op jit(solution)/shard_map/ppermute | solution.py:333
  32.5 0.0 collective-permute-done.gate1
  32.5 1.9 %collective-permute-done.1.up1 = bf16[1,3,128,128]{3,2,1,0:T(8,128)(2,1)S(1)} collective-permute-done((bf16[1,3,128,128]{3,2,1,0:T(8,128)(2,1)S(1)}, bf16[1,3,128,128]{3,2,1,0:T(8,128)(2,1)S(1)}, u32[]{:S(2)}, u32[]{:S(2)}) %collective-permute-start.1) | collective-permute-done | bytes 98336 | tf_op jit(solution)/shard_map/ppermute | solution.py:333
  34.4 10.4 %all-to-all-done.got_ref.picked_ref = bf16[32,96,128]{2,1,0:T(8,128)(2,1)S(1)} async-done(((bf16[32,96,128]{2,1,0:T(8,128)(2,1)}), bf16[32,96,128]{2,1,0:T(8,128)(2,1)S(1)}, u32[]{:S(2)}, u32[]{:S(2)}) %all-to-all-start) | async-done | bytes 786464 | tf_op jit(solution)/shard_map/all_to_all | solution.py:336
  44.8 1.3 gates.1
  46.2 0.0 collective-permute-done.2.down1
  46.2 1.0 down_terms.1
  47.2 0.0 copy-start.1
  47.2 0.0 copy-start.2
  47.2 0.0 copy-start.7
  47.2 34.8 %all_to_all.20.got_ref = bf16[32,96,128]{2,1,0:T(8,128)(2,1)S(1)} all-to-all(bf16[32,96,128]{2,1,0:T(8,128)(2,1)S(1)} %down_terms.1), channel_id=1, replica_groups=mesh['y'=4,'zh'=2,'za'=2,'zb'=4,'xc'=8] {'zb','xc'}, dimensions={0} | all-to-all | bytes 1572864 | tf_op jit(solution)/shard_map/all_to_all | solution.py:336
  82.1 2.3 %middle.1 = (bf16[16,4096]{1,0:T(8,128)(2,1)}, bf16[32,104,128]{2,1,0:T(8,128)(2,1)S(1)}) custom-call(s32[1,192]{1,0:T(1,128)S(1)} %copy-done.9, bf16[32,96,128]{2,1,0:T(8,128)(2,1)S(1)} %all_to_all.20.got_ref, bf16[16,4096]{1,0:T(8,128)(2,1)S(1)} %copy-done.1, bf16[16,4096]{1,0:T(8,128)(2,1)S(1)} %copy-done.2, f32[1,2,4096]{2,1,0:T(2,128)S(1)} %copy-done.7), custom_call_target="tpu_custom_call" | custom-call | tf_op jit(solution)/shard_map/middle/pallas_call | solution.py:312
  84.4 27.3 %all_to_all.21.got_ref = bf16[32,104,128]{2,1,0:T(8,128)(2,1)S(1)} all-to-all(bf16[32,104,128]{2,1,0:T(8,128)(2,1)S(1)} %get-tuple-element.22), channel_id=1, replica_groups=mesh['y'=4,'zh'=2,'za'=2,'zb'=4,'xc'=8] {'zb','xc'}, dimensions={0} | all-to-all | bytes 1703936 | tf_op jit(solution)/shard_map/all_to_all | solution.py:336
  111.6 3.0 %backward.1 = (bf16[32,104,128]{2,1,0:T(8,128)(2,1)}, f32[3,3,128,128]{3,2,1,0:T(8,128)S(1)}, bf16[3,3,128,128]{3,2,1,0:T(8,128)(2,1)S(1)}) custom-call(s32[1,192]{1,0:T(1,128)S(1)} %copy-done.9, bf16[32,104,128]{2,1,0:T(8,128)(2,1)S(1)} %all_to_all.21.got_ref, bf16[32,96,128]{2,1,0:T(8,128)(2,1)S(1)} %all-to-all-done.got_ref.picked_ref, ...), custom_call_target="tpu_custom_call" | custom-call | tf_op jit(solution)/shard_map/backward/pallas_call | solution.py:312
  114.6 5.3 %all-to-all-start.3 = ((bf16[32,104,128]{2,1,0:T(8,128)(2,1)}), bf16[32,104,128]{2,1,0:T(8,128)(2,1)S(1)}, u32[]{:S(2)}, u32[]{:S(2)}) async-start(bf16[32,104,128]{2,1,0:T(8,128)(2,1)} %get-tuple-element.25), calls=%async_computation.3 | async-start | bytes 1703936 | tf_op jit(solution)/shard_map/all_to_all | solution.py:336
  120.0 4.7 %collective-permute-start.4 = (bf16[3,3,128,128]{3,2,1,0:T(8,128)(2,1)S(1)}, bf16[3,3,128,128]{3,2,1,0:T(8,128)(2,1)S(1)}, u32[]{:S(2)}, u32[]{:S(2)}) collective-permute-start(bf16[3,3,128,128]{3,2,1,0:T(8,128)(2,1)S(1)} %get-tuple-element.28), channel_id=1, source_target_pairs={{0,32},{32,0},{1,33},{33,1},{2,34},{34,2},{3,35},{35,3},{4,36},{36... | collective-permute-start | bytes 884744 | tf_op jit(solution)/shard_map/ppermute | solution.py:333
  124.6 29.4 %all-to-all-done.3.got_ref = bf16[32,104,128]{2,1,0:T(8,128)(2,1)S(1)} async-done(((bf16[32,104,128]{2,1,0:T(8,128)(2,1)}), bf16[32,104,128]{2,1,0:T(8,128)(2,1)S(1)}, u32[]{:S(2)}, u32[]{:S(2)}) %all-to-all-start.3) | async-done | bytes 852000 | tf_op jit(solution)/shard_map/all_to_all | solution.py:336
  154.0 1.5 last.1
  155.5 8.1 %collective-permute-start.3 = (bf16[16,4096]{1,0:T(8,128)(2,1)S(1)}, bf16[16,4096]{1,0:T(8,128)(2,1)S(1)}, u32[]{:S(2)}, u32[]{:S(2)}) collective-permute-start(bf16[16,4096]{1,0:T(8,128)(2,1)S(1)} %get-tuple-element.26), channel_id=1, source_target_pairs={{64,0},{128,64},{192,128},{256,192},{320,256},{384,320},{448,384},... | collective-permute-start | bytes 393224 | tf_op jit(solution)/shard_map/ppermute | solution.py:387
  163.7 1.9 %collective-permute-start.5 = (f32[2,4096]{1,0:T(2,128)S(1)}, f32[2,4096]{1,0:T(2,128)S(1)}, u32[]{:S(2)}, u32[]{:S(2)}) collective-permute-start(f32[2,4096]{1,0:T(2,128)S(1)} %get-tuple-element.29.gain_ref), channel_id=1, source_target_pairs={{0,32},{32,0},{1,33},{33,1},{2,34},{34,2},{3,35},{35,3},{4,36},{36... | collective-permute-start | bytes 98312 | tf_op jit(solution)/shard_map/ppermute | solution.py:333
  165.6 0.0 collective-permute-done.4.other_ref
  165.6 14.3 %collective-permute-done.5.gain_other_ref = f32[2,4096]{1,0:T(2,128)S(1)} collective-permute-done((f32[2,4096]{1,0:T(2,128)S(1)}, f32[2,4096]{1,0:T(2,128)S(1)}, u32[]{:S(2)}, u32[]{:S(2)}) %collective-permute-start.5) | collective-permute-done | bytes 32800 | tf_op jit(solution)/shard_map/ppermute | solution.py:333
  179.9 0.8 finish.1
  180.6 0.7 copy.14
  (14 shorter events, 0.0 us)
Async XLA Ops:
  0.6 0.9 copy-start
  1.5 0.8 copy-start.6
  2.3 0.7 copy-start.8
  4.9 9.5 %copy-start.4 = (bf16[1,3,128,128]{3,2,1,0:T(8,128)(2,1)S(1)}, bf16[1,3,128,128]{3,2,1,0:T(8,128)(2,1)}, u32[]{:S(2)}) copy-start(bf16[1,3,128,128]{3,2,1,0:T(8,128)(2,1)} %gate0.3) | copy-start | bytes 294916
  4.9 18.4 %copy-start.5 = (bf16[1,3,128,128]{3,2,1,0:T(8,128)(2,1)S(1)}, bf16[1,3,128,128]{3,2,1,0:T(8,128)(2,1)}, u32[]{:S(2)}) copy-start(bf16[1,3,128,128]{3,2,1,0:T(8,128)(2,1)} %up0.3) | copy-start | bytes 294916
  4.9 20.3 %copy-start.3 = (bf16[1,3,128,128]{3,2,1,0:T(8,128)(2,1)S(1)}, bf16[1,3,128,128]{3,2,1,0:T(8,128)(2,1)}, u32[]{:S(2)}) copy-start(bf16[1,3,128,128]{3,2,1,0:T(8,128)(2,1)} %down0.3) | copy-start | bytes 294916
  4.9 39.9 %copy-start.9 = (s32[1,192]{1,0:T(1,128)S(1)}, s32[1,192]{1,0:T(1,128)}, u32[]{:S(2)}) copy-start(s32[1,192]{1,0:T(1,128)} %place_ref.11) | copy-start | bytes 2308
  4.9 39.9 %all-to-all-start = ((bf16[32,96,128]{2,1,0:T(8,128)(2,1)}), bf16[32,96,128]{2,1,0:T(8,128)(2,1)S(1)}, u32[]{:S(2)}, u32[]{:S(2)}) async-start(bf16[32,96,128]{2,1,0:T(8,128)(2,1)} %send_normed.1), calls=%async_computation | async-start | bytes 1572864 | tf_op jit(solution)/shard_map/all_to_all | solution.py:336
  14.4 18.1 %collective-permute-start = (bf16[1,3,128,128]{3,2,1,0:T(8,128)(2,1)S(1)}, bf16[1,3,128,128]{3,2,1,0:T(8,128)(2,1)S(1)}, u32[]{:S(2)}, u32[]{:S(2)}) collective-permute-start(bf16[1,3,128,128]{3,2,1,0:T(8,128)(2,1)S(1)} %copy-done.4), channel_id=1, source_target_pairs={{0,32},{32,0},{1,33},{33,1},{2,34},{34,2},{3,35},{35,3},{4,36},{36... | collective-permute-start | bytes 294920 | tf_op jit(solution)/shard_map/ppermute | solution.py:333
  23.2 11.1 %collective-permute-start.1 = (bf16[1,3,128,128]{3,2,1,0:T(8,128)(2,1)S(1)}, bf16[1,3,128,128]{3,2,1,0:T(8,128)(2,1)S(1)}, u32[]{:S(2)}, u32[]{:S(2)}) collective-permute-start(bf16[1,3,128,128]{3,2,1,0:T(8,128)(2,1)S(1)} %copy-done.5), channel_id=1, source_target_pairs={{0,32},{32,0},{1,33},{33,1},{2,34},{34,2},{3,35},{35,3},{4,36},{36... | collective-permute-start | bytes 294920 | tf_op jit(solution)/shard_map/ppermute | solution.py:333
  25.2 21.0 %collective-permute-start.2 = (bf16[1,3,128,128]{3,2,1,0:T(8,128)(2,1)S(1)}, bf16[1,3,128,128]{3,2,1,0:T(8,128)(2,1)S(1)}, u32[]{:S(2)}, u32[]{:S(2)}) collective-permute-start(bf16[1,3,128,128]{3,2,1,0:T(8,128)(2,1)S(1)} %copy-done.3), channel_id=1, source_target_pairs={{0,32},{32,0},{1,33},{33,1},{2,34},{34,2},{3,35},{35,3},{4,36},{36... | collective-permute-start | bytes 294920 | tf_op jit(solution)/shard_map/ppermute | solution.py:333
  47.2 34.9 %copy-start.1 = (bf16[16,4096]{1,0:T(8,128)(2,1)S(1)}, bf16[16,4096]{1,0:T(8,128)(2,1)}, u32[]{:S(2)}) copy-start(bf16[16,4096]{1,0:T(8,128)(2,1)} %acts_ref.5) | copy-start | bytes 393220
  47.2 34.9 %copy-start.2 = (bf16[16,4096]{1,0:T(8,128)(2,1)S(1)}, bf16[16,4096]{1,0:T(8,128)(2,1)}, u32[]{:S(2)}) copy-start(bf16[16,4096]{1,0:T(8,128)(2,1)} %cot_ref.3) | copy-start | bytes 393220
  47.2 34.9 %copy-start.7 = (f32[1,2,4096]{2,1,0:T(2,128)S(1)}, f32[1,2,4096]{2,1,0:T(2,128)}, u32[]{:S(2)}) copy-start(f32[1,2,4096]{2,1,0:T(2,128)} %gains_ref.5) | copy-start | bytes 98308
  114.6 39.4 %all-to-all-start.3 = ((bf16[32,104,128]{2,1,0:T(8,128)(2,1)}), bf16[32,104,128]{2,1,0:T(8,128)(2,1)S(1)}, u32[]{:S(2)}, u32[]{:S(2)}) async-start(bf16[32,104,128]{2,1,0:T(8,128)(2,1)} %get-tuple-element.25), calls=%async_computation.3 | async-start | bytes 1703936 | tf_op jit(solution)/shard_map/all_to_all | solution.py:336
  120.0 45.6 %collective-permute-start.4 = (bf16[3,3,128,128]{3,2,1,0:T(8,128)(2,1)S(1)}, bf16[3,3,128,128]{3,2,1,0:T(8,128)(2,1)S(1)}, u32[]{:S(2)}, u32[]{:S(2)}) collective-permute-start(bf16[3,3,128,128]{3,2,1,0:T(8,128)(2,1)S(1)} %get-tuple-element.28), channel_id=1, source_target_pairs={{0,32},{32,0},{1,33},{33,1},{2,34},{34,2},{3,35},{35,3},{4,36},{36... | collective-permute-start | bytes 884744 | tf_op jit(solution)/shard_map/ppermute | solution.py:333
  155.5 25.1 %collective-permute-start.3 = (bf16[16,4096]{1,0:T(8,128)(2,1)S(1)}, bf16[16,4096]{1,0:T(8,128)(2,1)S(1)}, u32[]{:S(2)}, u32[]{:S(2)}) collective-permute-start(bf16[16,4096]{1,0:T(8,128)(2,1)S(1)} %get-tuple-element.26), channel_id=1, source_target_pairs={{64,0},{128,64},{192,128},{256,192},{320,256},{384,320},{448,384},... | collective-permute-start | bytes 393224 | tf_op jit(solution)/shard_map/ppermute | solution.py:387
  163.7 16.2 %collective-permute-start.5 = (f32[2,4096]{1,0:T(2,128)S(1)}, f32[2,4096]{1,0:T(2,128)S(1)}, u32[]{:S(2)}, u32[]{:S(2)}) collective-permute-start(f32[2,4096]{1,0:T(2,128)S(1)} %get-tuple-element.29.gain_ref), channel_id=1, source_target_pairs={{0,32},{32,0},{1,33},{33,1},{2,34},{34,2},{3,35},{35,3},{4,36},{36... | collective-permute-start | bytes 98312 | tf_op jit(solution)/shard_map/ppermute | solution.py:333

commit v5 on v4

--- a/solution.py
+++ b/solution.py
@@ -39,7 +39,9 @@
 
 
 def slot_place(place_ref, half, peer, group, slot, peers, slots):
-    return place_ref[0, ((half ^ group) * peers + peer) * slots + slot]
+    zs = lax.axis_size("zb")
+    device = peer % zs * (peers // zs) + peer // zs
+    return place_ref[0, ((half ^ group) * peers + device) * slots + slot]
 
 
 def feature_block(place):
@@ -103,7 +105,7 @@
 
 
 def own_peer():
-    return lax.axis_index("zb") * lax.axis_size("xc") + lax.axis_index("xc")
+    return lax.axis_index("xc") * lax.axis_size("zb") + lax.axis_index("zb")
 
 
 def slot_masks(place_ref, half, peer, group, peers, slots):
@@ -257,6 +259,7 @@
     cot_ref,
     gains_ref,
     grad_ref,
+    gain_out,
     gain_ref,
     total_ref,
     *more_refs,
@@ -287,6 +290,7 @@
         gain = gains_ref[0, 0:1, cols]
         mixed = mixed + total_ref[block] * gain * normed_in
         gain_ref[0:1, cols] = sum(ref[block] for ref in gain_refs) / gain
+    gain_out[...] = gain_ref[...].astype(bf16)
     mean = jnp.sum(mixed, axis=1, keepdims=True) / width
     for block in range(width // B):
         cols = block_cols(block)
@@ -296,10 +300,11 @@
         grad_ref[:, cols] = (grad + scale_in * (scaled_in - normed_in * mean)).astype(bf16)
 
 
-def finish(own_ref, other_ref, gain_ref, gain_other_ref, gate_ref, up_ref, down_ref, gain_out):
+def finish(own_ref, other_ref, gain_ref, gain_other_ref, input_ref, gate_ref, up_ref, down_ref, gain_out, back_ref):
     for kind, target in enumerate((gate_ref, up_ref, down_ref)):
         target[0] = (own_ref[kind] + other_ref[kind].astype(f32)).astype(bf16)
-    gain_out[0] = gain_ref[...] + gain_other_ref[...]
+    gain_out[0] = gain_ref[...].astype(f32) + gain_other_ref[...].astype(f32)
+    back_ref[...] = input_ref[...]
 
 
 def call(kernel, name, outs, operands, scratch=(), far_in=(), far_out=()):
@@ -323,7 +328,7 @@
 def body(acts, cotangent, gains, gate_blocks, up_blocks, down_blocks, block_place):
     rows, width = acts.shape
     slots = gate_blocks.shape[1]
-    peer_axes = ("zb", "xc")
+    peer_axes = ("xc", "zb")
     peers = lax.axis_size(peer_axes)
     features = width // B
     sent_rows = 2 * slots * rows
@@ -378,19 +383,19 @@
     input_grad, gain_half = call(
         functools.partial(last, slots),
         "last",
-        [((rows, width), bf16), ((2, width), f32)],
+        [((rows, width), bf16), ((2, width), bf16)],
         (block_place, exchange(back_sent), acts, cotangent, gains),
-        [feature_sums] * SUMS + [pltpu.VMEM((features, 1, B), f32)] * SUMS,
+        [pltpu.VMEM((2, width), f32)] + [feature_sums] * SUMS + [pltpu.VMEM((features, 1, B), f32)] * SUMS,
     )
     section = ("y", "zh")
     count = lax.axis_size(section)
     grad_back = lax.ppermute(input_grad, section, [(source, source - 1) for source in range(1, count)])
     gain_other = to_other(gain_half)
-    gate_grad, up_grad, down_grad, gain_grad = call(
+    gate_grad, up_grad, down_grad, gain_grad, grad_back = call(
         finish,
         "finish",
-        [((1, slots, B, B), bf16)] * 3 + [((1, 2, width), f32)],
-        (own_grads, grads_got, gain_half, gain_other),
+        [((1, slots, B, B), bf16)] * 3 + [((1, 2, width), f32), ((rows, width), bf16)],
+        (own_grads, grads_got, gain_half, gain_other, grad_back),
     )
     return (layer_out, grad_back, gate_grad, up_grad, down_grad, gain_grad)
 

time: 182 us -> 182 us (level)
  the two profiles are of different devices: /device:TPU:27 before, /device:TPU:29 now
where the time goes in v5:
time: 182 us; the launch traced here: 181 us
  blocking collectives  63.1 us (35%)
  waiting for transfers between devices  54.5 us (30%)
  starting transfers between devices  48.3 us (27%)
  Pallas kernels  11.9 us (7%)
  local copies, waits for them, and re-layouts  2.37 us (1%)
    all_to_all x2, blocking collectives, exchange(): lax.all_to_all(value, peer_axes, split_axis=0, concat_axis=0, tiled=True)  63.1 us
    all_to_all x2, waiting for transfers between devices, exchange(): lax.all_to_all(value, peer_axes, split_axis=0, concat_axis=0, tiled=True)  37.8 us
    ppermute x5, starting transfers between devices, to_other(): return lax.ppermute(value, 'za', [(0, 1), (1, 0)])  24.7 us
    ppermute x5, waiting for transfers between devices, to_other(): return lax.ppermute(value, 'za', [(0, 1), (1, 0)])  15.8 us
    all_to_all x2, starting transfers between devices, exchange(): lax.all_to_all(value, peer_axes, split_axis=0, concat_axis=0, tiled=True)  15.7 us
    pallas_call x7, Pallas kernels, call(): pl.pallas_call(kernel, name=name, out_shape=[jax.ShapeDtypeStruct(shape,...  11.9 us
    ppermute x1, starting transfers between devices, body(): lax.ppermute(input_grad, section, [(source, source - 1) for source in ran...  7.87 us
  transfers between devices with their start and end apart: 8, of which 5 were waited for; matrix products, arithmetic and copies ran while one was open for 0% of the time, Pallas kernels for 2%

profile of v5, /device:TPU:29, one launch (start us, length us, event | category | flops | bytes accessed | tf_op | source)
XLA Modules:
  0.0 180.9 jit_solution(4086564513871880509)
XLA Ops:
  0.6 0.0 copy-start
  0.6 0.9 copy-done
  1.5 0.8 copy-done.6
  2.3 0.7 copy-done.8
  3.0 1.9 %send_normed.1 = bf16[32,96,128]{2,1,0:T(8,128)(2,1)} custom-call(s32[1,192]{1,0:T(1,128)S(1)} %copy-done.8, bf16[16,4096]{1,0:T(8,128)(2,1)S(1)} %copy-done, f32[1,2,4096]{2,1,0:T(2,128)S(1)} %copy-done.6), custom_call_target="tpu_custom_call" | custom-call | tf_op jit(solution)/shard_map/send_normed/pallas_call | solution.py:317
  4.9 9.5 %all-to-all-start = ((bf16[32,96,128]{2,1,0:T(8,128)(2,1)}), bf16[32,96,128]{2,1,0:T(8,128)(2,1)S(1)}, u32[]{:S(2)}, u32[]{:S(2)}) async-start(bf16[32,96,128]{2,1,0:T(8,128)(2,1)} %send_normed.1), calls=%async_computation | async-start | bytes 1572864 | tf_op jit(solution)/shard_map/all_to_all | solution.py:341
  14.4 8.8 %collective-permute-start = (bf16[1,3,128,128]{3,2,1,0:T(8,128)(2,1)S(1)}, bf16[1,3,128,128]{3,2,1,0:T(8,128)(2,1)S(1)}, u32[]{:S(2)}, u32[]{:S(2)}) collective-permute-start(bf16[1,3,128,128]{3,2,1,0:T(8,128)(2,1)S(1)} %copy-done.4), channel_id=1, source_target_pairs={{0,32},{32,0},{1,33},{33,1},{2,34},{34,2},{3,35},{35,3},{4,36},{36... | collective-permute-start | bytes 294920 | tf_op jit(solution)/shard_map/ppermute | solution.py:338
  23.2 1.9 %collective-permute-start.1 = (bf16[1,3,128,128]{3,2,1,0:T(8,128)(2,1)S(1)}, bf16[1,3,128,128]{3,2,1,0:T(8,128)(2,1)S(1)}, u32[]{:S(2)}, u32[]{:S(2)}) collective-permute-start(bf16[1,3,128,128]{3,2,1,0:T(8,128)(2,1)S(1)} %copy-done.5), channel_id=1, source_target_pairs={{0,32},{32,0},{1,33},{33,1},{2,34},{34,2},{3,35},{35,3},{4,36},{36... | collective-permute-start | bytes 294920 | tf_op jit(solution)/shard_map/ppermute | solution.py:338
  25.2 7.3 %collective-permute-start.2 = (bf16[1,3,128,128]{3,2,1,0:T(8,128)(2,1)S(1)}, bf16[1,3,128,128]{3,2,1,0:T(8,128)(2,1)S(1)}, u32[]{:S(2)}, u32[]{:S(2)}) collective-permute-start(bf16[1,3,128,128]{3,2,1,0:T(8,128)(2,1)S(1)} %copy-done.3), channel_id=1, source_target_pairs={{0,32},{32,0},{1,33},{33,1},{2,34},{34,2},{3,35},{35,3},{4,36},{36... | collective-permute-start | bytes 294920 | tf_op jit(solution)/shard_map/ppermute | solution.py:338
  32.4 0.0 collective-permute-done.gate1
  32.4 2.4 %collective-permute-done.1.up1 = bf16[1,3,128,128]{3,2,1,0:T(8,128)(2,1)S(1)} collective-permute-done((bf16[1,3,128,128]{3,2,1,0:T(8,128)(2,1)S(1)}, bf16[1,3,128,128]{3,2,1,0:T(8,128)(2,1)S(1)}, u32[]{:S(2)}, u32[]{:S(2)}) %collective-permute-start.1) | collective-permute-done | bytes 98336 | tf_op jit(solution)/shard_map/ppermute | solution.py:338
  34.8 8.9 %all-to-all-done.got_ref.picked_ref = bf16[32,96,128]{2,1,0:T(8,128)(2,1)S(1)} async-done(((bf16[32,96,128]{2,1,0:T(8,128)(2,1)}), bf16[32,96,128]{2,1,0:T(8,128)(2,1)S(1)}, u32[]{:S(2)}, u32[]{:S(2)}) %all-to-all-start) | async-done | bytes 786464 | tf_op jit(solution)/shard_map/all_to_all | solution.py:341
  43.7 1.3 gates.1
  45.1 0.0 collective-permute-done.2.down1
  45.1 1.0 down_terms.1
  46.1 0.0 copy-start.1
  46.1 0.0 copy-start.2
  46.2 0.0 copy-start.7
  46.2 35.3 %all_to_all.20.got_ref = bf16[32,96,128]{2,1,0:T(8,128)(2,1)S(1)} all-to-all(bf16[32,96,128]{2,1,0:T(8,128)(2,1)S(1)} %down_terms.1), channel_id=1, replica_groups=mesh['y'=4,'zh'=2,'za'=2,'zb'=4,'xc'=8] {'xc','zb'}, dimensions={0} | all-to-all | bytes 1572864 | tf_op jit(solution)/shard_map/all_to_all | solution.py:341
  81.5 2.3 %middle.1 = (bf16[16,4096]{1,0:T(8,128)(2,1)}, bf16[32,104,128]{2,1,0:T(8,128)(2,1)S(1)}) custom-call(s32[1,192]{1,0:T(1,128)S(1)} %copy-done.9, bf16[32,96,128]{2,1,0:T(8,128)(2,1)S(1)} %all_to_all.20.got_ref, bf16[16,4096]{1,0:T(8,128)(2,1)S(1)} %copy-done.1, bf16[16,4096]{1,0:T(8,128)(2,1)S(1)} %copy-done.2, f32[1,2,4096]{2,1,0:T(2,128)S(1)} %copy-done.7), custom_call_target="tpu_custom_call" | custom-call | tf_op jit(solution)/shard_map/middle/pallas_call | solution.py:317
  83.8 27.7 %all_to_all.21.got_ref = bf16[32,104,128]{2,1,0:T(8,128)(2,1)S(1)} all-to-all(bf16[32,104,128]{2,1,0:T(8,128)(2,1)S(1)} %get-tuple-element.23), channel_id=1, replica_groups=mesh['y'=4,'zh'=2,'za'=2,'zb'=4,'xc'=8] {'xc','zb'}, dimensions={0} | all-to-all | bytes 1703936 | tf_op jit(solution)/shard_map/all_to_all | solution.py:341
  111.5 3.0 %backward.1 = (bf16[32,104,128]{2,1,0:T(8,128)(2,1)}, f32[3,3,128,128]{3,2,1,0:T(8,128)S(1)}, bf16[3,3,128,128]{3,2,1,0:T(8,128)(2,1)S(1)}) custom-call(s32[1,192]{1,0:T(1,128)S(1)} %copy-done.9, bf16[32,104,128]{2,1,0:T(8,128)(2,1)S(1)} %all_to_all.21.got_ref, bf16[32,96,128]{2,1,0:T(8,128)(2,1)S(1)} %all-to-all-done.got_ref.picked_ref, ...), custom_call_target="tpu_custom_call" | custom-call | tf_op jit(solution)/shard_map/backward/pallas_call | solution.py:317
  114.6 6.2 %all-to-all-start.3 = ((bf16[32,104,128]{2,1,0:T(8,128)(2,1)}), bf16[32,104,128]{2,1,0:T(8,128)(2,1)S(1)}, u32[]{:S(2)}, u32[]{:S(2)}) async-start(bf16[32,104,128]{2,1,0:T(8,128)(2,1)} %get-tuple-element.28), calls=%async_computation.3 | async-start | bytes 1703936 | tf_op jit(solution)/shard_map/all_to_all | solution.py:341
  120.8 4.7 %collective-permute-start.3 = (bf16[3,3,128,128]{3,2,1,0:T(8,128)(2,1)S(1)}, bf16[3,3,128,128]{3,2,1,0:T(8,128)(2,1)S(1)}, u32[]{:S(2)}, u32[]{:S(2)}) collective-permute-start(bf16[3,3,128,128]{3,2,1,0:T(8,128)(2,1)S(1)} %get-tuple-element.27), channel_id=1, source_target_pairs={{0,32},{32,0},{1,33},{33,1},{2,34},{34,2},{3,35},{35,3},{4,36},{36... | collective-permute-start | bytes 884744 | tf_op jit(solution)/shard_map/ppermute | solution.py:338
  125.4 28.9 %all-to-all-done.3.got_ref = bf16[32,104,128]{2,1,0:T(8,128)(2,1)S(1)} async-done(((bf16[32,104,128]{2,1,0:T(8,128)(2,1)}), bf16[32,104,128]{2,1,0:T(8,128)(2,1)S(1)}, u32[]{:S(2)}, u32[]{:S(2)}) %all-to-all-start.3) | async-done | bytes 852000 | tf_op jit(solution)/shard_map/all_to_all | solution.py:341
  154.3 1.5 last.1
  155.9 7.9 %collective-permute-start.5 = (bf16[16,4096]{1,0:T(8,128)(2,1)S(1)}, bf16[16,4096]{1,0:T(8,128)(2,1)S(1)}, u32[]{:S(2)}, u32[]{:S(2)}) collective-permute-start(bf16[16,4096]{1,0:T(8,128)(2,1)S(1)} %get-tuple-element.30), channel_id=1, source_target_pairs={{64,0},{128,64},{192,128},{256,192},{320,256},{384,320},{448,384},... | collective-permute-start | bytes 393224 | tf_op jit(solution)/shard_map/ppermute | solution.py:392
  163.7 2.1 %collective-permute-start.4 = (bf16[2,4096]{1,0:T(2,128)(2,1)S(1)}, bf16[2,4096]{1,0:T(2,128)(2,1)S(1)}, u32[]{:S(2)}, u32[]{:S(2)}) collective-permute-start(bf16[2,4096]{1,0:T(2,128)(2,1)S(1)} %get-tuple-element.29.gain_ref), channel_id=1, source_target_pairs={{0,32},{32,0},{1,33},{33,1},{2,34},{34,2},{3,35},{35,3},{4,36},{36... | collective-permute-start | bytes 49160 | tf_op jit(solution)/shard_map/ppermute | solution.py:338
  165.8 0.0 collective-permute-done.3.other_ref
  165.8 13.4 %collective-permute-done.4.gain_other_ref = bf16[2,4096]{1,0:T(2,128)(2,1)S(1)} collective-permute-done((bf16[2,4096]{1,0:T(2,128)(2,1)S(1)}, bf16[2,4096]{1,0:T(2,128)(2,1)S(1)}, u32[]{:S(2)}, u32[]{:S(2)}) %collective-permute-start.4) | collective-permute-done | bytes 16416 | tf_op jit(solution)/shard_map/ppermute | solution.py:338
  179.3 0.9 collective-permute-done.5.input_ref
  180.1 0.8 finish.1
  (13 shorter events, 0.0 us)
Async XLA Ops:
  0.6 0.9 copy-start
  1.5 0.8 copy-start.6
  2.3 0.7 copy-start.8
  4.9 9.5 %copy-start.4 = (bf16[1,3,128,128]{3,2,1,0:T(8,128)(2,1)S(1)}, bf16[1,3,128,128]{3,2,1,0:T(8,128)(2,1)}, u32[]{:S(2)}) copy-start(bf16[1,3,128,128]{3,2,1,0:T(8,128)(2,1)} %gate0.3) | copy-start | bytes 294916
  4.9 18.3 %copy-start.5 = (bf16[1,3,128,128]{3,2,1,0:T(8,128)(2,1)S(1)}, bf16[1,3,128,128]{3,2,1,0:T(8,128)(2,1)}, u32[]{:S(2)}) copy-start(bf16[1,3,128,128]{3,2,1,0:T(8,128)(2,1)} %up0.3) | copy-start | bytes 294916
  4.9 20.3 %copy-start.3 = (bf16[1,3,128,128]{3,2,1,0:T(8,128)(2,1)S(1)}, bf16[1,3,128,128]{3,2,1,0:T(8,128)(2,1)}, u32[]{:S(2)}) copy-start(bf16[1,3,128,128]{3,2,1,0:T(8,128)(2,1)} %down0.3) | copy-start | bytes 294916
  4.9 38.8 %copy-start.9 = (s32[1,192]{1,0:T(1,128)S(1)}, s32[1,192]{1,0:T(1,128)}, u32[]{:S(2)}) copy-start(s32[1,192]{1,0:T(1,128)} %place_ref.11) | copy-start | bytes 2308
  4.9 38.8 %all-to-all-start = ((bf16[32,96,128]{2,1,0:T(8,128)(2,1)}), bf16[32,96,128]{2,1,0:T(8,128)(2,1)S(1)}, u32[]{:S(2)}, u32[]{:S(2)}) async-start(bf16[32,96,128]{2,1,0:T(8,128)(2,1)} %send_normed.1), calls=%async_computation | async-start | bytes 1572864 | tf_op jit(solution)/shard_map/all_to_all | solution.py:341
  14.4 18.1 %collective-permute-start = (bf16[1,3,128,128]{3,2,1,0:T(8,128)(2,1)S(1)}, bf16[1,3,128,128]{3,2,1,0:T(8,128)(2,1)S(1)}, u32[]{:S(2)}, u32[]{:S(2)}) collective-permute-start(bf16[1,3,128,128]{3,2,1,0:T(8,128)(2,1)S(1)} %copy-done.4), channel_id=1, source_target_pairs={{0,32},{32,0},{1,33},{33,1},{2,34},{34,2},{3,35},{35,3},{4,36},{36... | collective-permute-start | bytes 294920 | tf_op jit(solution)/shard_map/ppermute | solution.py:338
  23.2 11.6 %collective-permute-start.1 = (bf16[1,3,128,128]{3,2,1,0:T(8,128)(2,1)S(1)}, bf16[1,3,128,128]{3,2,1,0:T(8,128)(2,1)S(1)}, u32[]{:S(2)}, u32[]{:S(2)}) collective-permute-start(bf16[1,3,128,128]{3,2,1,0:T(8,128)(2,1)S(1)} %copy-done.5), channel_id=1, source_target_pairs={{0,32},{32,0},{1,33},{33,1},{2,34},{34,2},{3,35},{35,3},{4,36},{36... | collective-permute-start | bytes 294920 | tf_op jit(solution)/shard_map/ppermute | solution.py:338
  25.2 20.0 %collective-permute-start.2 = (bf16[1,3,128,128]{3,2,1,0:T(8,128)(2,1)S(1)}, bf16[1,3,128,128]{3,2,1,0:T(8,128)(2,1)S(1)}, u32[]{:S(2)}, u32[]{:S(2)}) collective-permute-start(bf16[1,3,128,128]{3,2,1,0:T(8,128)(2,1)S(1)} %copy-done.3), channel_id=1, source_target_pairs={{0,32},{32,0},{1,33},{33,1},{2,34},{34,2},{3,35},{35,3},{4,36},{36... | collective-permute-start | bytes 294920 | tf_op jit(solution)/shard_map/ppermute | solution.py:338
  46.1 35.4 %copy-start.1 = (bf16[16,4096]{1,0:T(8,128)(2,1)S(1)}, bf16[16,4096]{1,0:T(8,128)(2,1)}, u32[]{:S(2)}) copy-start(bf16[16,4096]{1,0:T(8,128)(2,1)} %acts_ref.5) | copy-start | bytes 393220
  46.1 35.4 %copy-start.2 = (bf16[16,4096]{1,0:T(8,128)(2,1)S(1)}, bf16[16,4096]{1,0:T(8,128)(2,1)}, u32[]{:S(2)}) copy-start(bf16[16,4096]{1,0:T(8,128)(2,1)} %cot_ref.3) | copy-start | bytes 393220
  46.2 35.3 %copy-start.7 = (f32[1,2,4096]{2,1,0:T(2,128)S(1)}, f32[1,2,4096]{2,1,0:T(2,128)}, u32[]{:S(2)}) copy-start(f32[1,2,4096]{2,1,0:T(2,128)} %gains_ref.5) | copy-start | bytes 98308
  114.6 39.8 %all-to-all-start.3 = ((bf16[32,104,128]{2,1,0:T(8,128)(2,1)}), bf16[32,104,128]{2,1,0:T(8,128)(2,1)S(1)}, u32[]{:S(2)}, u32[]{:S(2)}) async-start(bf16[32,104,128]{2,1,0:T(8,128)(2,1)} %get-tuple-element.28), calls=%async_computation.3 | async-start | bytes 1703936 | tf_op jit(solution)/shard_map/all_to_all | solution.py:341
  120.8 45.1 %collective-permute-start.3 = (bf16[3,3,128,128]{3,2,1,0:T(8,128)(2,1)S(1)}, bf16[3,3,128,128]{3,2,1,0:T(8,128)(2,1)S(1)}, u32[]{:S(2)}, u32[]{:S(2)}) collective-permute-start(bf16[3,3,128,128]{3,2,1,0:T(8,128)(2,1)S(1)} %get-tuple-element.27), channel_id=1, source_target_pairs={{0,32},{32,0},{1,33},{33,1},{2,34},{34,2},{3,35},{35,3},{4,36},{36... | collective-permute-start | bytes 884744 | tf_op jit(solution)/shard_map/ppermute | solution.py:338
  155.9 24.3 %collective-permute-start.5 = (bf16[16,4096]{1,0:T(8,128)(2,1)S(1)}, bf16[16,4096]{1,0:T(8,128)(2,1)S(1)}, u32[]{:S(2)}, u32[]{:S(2)}) collective-permute-start(bf16[16,4096]{1,0:T(8,128)(2,1)S(1)} %get-tuple-element.30), channel_id=1, source_target_pairs={{64,0},{128,64},{192,128},{256,192},{320,256},{384,320},{448,384},... | collective-permute-start | bytes 393224 | tf_op jit(solution)/shard_map/ppermute | solution.py:392
  163.7 15.5 %collective-permute-start.4 = (bf16[2,4096]{1,0:T(2,128)(2,1)S(1)}, bf16[2,4096]{1,0:T(2,128)(2,1)S(1)}, u32[]{:S(2)}, u32[]{:S(2)}) collective-permute-start(bf16[2,4096]{1,0:T(2,128)(2,1)S(1)} %get-tuple-element.29.gain_ref), channel_id=1, source_target_pairs={{0,32},{32,0},{1,33},{33,1},{2,34},{34,2},{3,35},{35,3},{4,36},{36... | collective-permute-start | bytes 49160 | tf_op jit(solution)/shard_map/ppermute | solution.py:338

commit v6 on v5

--- a/solution.py
+++ b/solution.py
@@ -39,8 +39,7 @@
 
 
 def slot_place(place_ref, half, peer, group, slot, peers, slots):
-    zs = lax.axis_size("zb")
-    device = peer % zs * (peers // zs) + peer // zs
+    device = peer % 4 * 8 + peer // 4 % 4 * 2 + peer // 16
     return place_ref[0, ((half ^ group) * peers + device) * slots + slot]
 
 
@@ -105,7 +104,7 @@
 
 
 def own_peer():
-    return lax.axis_index("xc") * lax.axis_size("zb") + lax.axis_index("zb")
+    return (lax.axis_index("c") * 4 + lax.axis_index("x")) * 4 + lax.axis_index("zb")
 
 
 def slot_masks(place_ref, half, peer, group, peers, slots):
@@ -328,7 +327,7 @@
 def body(acts, cotangent, gains, gate_blocks, up_blocks, down_blocks, block_place):
     rows, width = acts.shape
     slots = gate_blocks.shape[1]
-    peer_axes = ("xc", "zb")
+    peer_axes = ("c", "x", "zb")
     peers = lax.axis_size(peer_axes)
     features = width // B
     sent_rows = 2 * slots * rows
@@ -401,8 +400,8 @@
 
 
 def solution(mesh):
-    names = ("y", "zh", "za", "zb", "xc")
-    split = Mesh(mesh.devices.reshape(4, 2, 2, 4, 8), names)
+    names = ("y", "zh", "za", "zb", "x", "c")
+    split = Mesh(mesh.devices.reshape(4, 2, 2, 4, 4, 2), names)
     section, tp = names[:2], names[2:]
     tokens = P(names, None)
     blocks = P(section, tp, None, None)

time: 182 us -> 180 us (0.989)
  the two profiles are of different devices: /device:TPU:29 before, /device:TPU:26 now
where the time goes in v6:
time: 180 us
  blocking collectives  61.8 us (34%)
  waiting for transfers between devices  54.2 us (30%)
  starting transfers between devices  48.4 us (27%)
  Pallas kernels  12 us (7%)
  local copies, waits for them, and re-layouts  2.37 us (1%)
    all_to_all x2, blocking collectives, exchange(): lax.all_to_all(value, peer_axes, split_axis=0, concat_axis=0, tiled=True)  61.8 us
    all_to_all x2, waiting for transfers between devices, exchange(): lax.all_to_all(value, peer_axes, split_axis=0, concat_axis=0, tiled=True)  35.6 us
    ppermute x5, starting transfers between devices, to_other(): return lax.ppermute(value, 'za', [(0, 1), (1, 0)])  26.1 us
    ppermute x5, waiting for transfers between devices, to_other(): return lax.ppermute(value, 'za', [(0, 1), (1, 0)])  17.6 us
    all_to_all x2, starting transfers between devices, exchange(): lax.all_to_all(value, peer_axes, split_axis=0, concat_axis=0, tiled=True)  14.2 us
    pallas_call x7, Pallas kernels, call(): pl.pallas_call(kernel, name=name, out_shape=[jax.ShapeDtypeStruct(shape,...  12 us
    ppermute x1, starting transfers between devices, body(): lax.ppermute(input_grad, section, [(source, source - 1) for source in ran...  8.15 us
  transfers between devices with their start and end apart: 8, of which 6 were waited for; matrix products, arithmetic and copies ran while one was open for 0% of the time, Pallas kernels for 2%

profile of v6, /device:TPU:26, one launch (start us, length us, event | category | flops | bytes accessed | tf_op | source)
XLA Modules:
  0.0 179.6 jit_solution(4141293610798077232)
XLA Ops:
  0.6 0.0 copy-start
  0.6 0.9 copy-done
  1.5 0.8 copy-done.6
  2.3 0.7 copy-done.8
  3.0 1.9 %send_normed.1 = bf16[32,96,128]{2,1,0:T(8,128)(2,1)} custom-call(s32[1,192]{1,0:T(1,128)S(1)} %copy-done.8, bf16[16,4096]{1,0:T(8,128)(2,1)S(1)} %copy-done, f32[1,2,4096]{2,1,0:T(2,128)S(1)} %copy-done.6), custom_call_target="tpu_custom_call" | custom-call | tf_op jit(solution)/shard_map/send_normed/pallas_call | solution.py:316
  4.9 9.2 %all-to-all-start = ((bf16[32,96,128]{2,1,0:T(8,128)(2,1)}), bf16[32,96,128]{2,1,0:T(8,128)(2,1)S(1)}, u32[]{:S(2)}, u32[]{:S(2)}) async-start(bf16[32,96,128]{2,1,0:T(8,128)(2,1)} %send_normed.1), calls=%async_computation | async-start | bytes 1572864 | tf_op jit(solution)/shard_map/all_to_all | solution.py:340
  14.1 9.1 %collective-permute-start = (bf16[1,3,128,128]{3,2,1,0:T(8,128)(2,1)S(1)}, bf16[1,3,128,128]{3,2,1,0:T(8,128)(2,1)S(1)}, u32[]{:S(2)}, u32[]{:S(2)}) collective-permute-start(bf16[1,3,128,128]{3,2,1,0:T(8,128)(2,1)S(1)} %copy-done.4), channel_id=1, source_target_pairs={{0,32},{32,0},{1,33},{33,1},{2,34},{34,2},{3,35},{35,3},{4,36},{36... | collective-permute-start | bytes 294920 | tf_op jit(solution)/shard_map/ppermute | solution.py:337
  23.2 1.9 %collective-permute-start.1 = (bf16[1,3,128,128]{3,2,1,0:T(8,128)(2,1)S(1)}, bf16[1,3,128,128]{3,2,1,0:T(8,128)(2,1)S(1)}, u32[]{:S(2)}, u32[]{:S(2)}) collective-permute-start(bf16[1,3,128,128]{3,2,1,0:T(8,128)(2,1)S(1)} %copy-done.5), channel_id=1, source_target_pairs={{0,32},{32,0},{1,33},{33,1},{2,34},{34,2},{3,35},{35,3},{4,36},{36... | collective-permute-start | bytes 294920 | tf_op jit(solution)/shard_map/ppermute | solution.py:337
  25.1 7.8 %collective-permute-start.2 = (bf16[1,3,128,128]{3,2,1,0:T(8,128)(2,1)S(1)}, bf16[1,3,128,128]{3,2,1,0:T(8,128)(2,1)S(1)}, u32[]{:S(2)}, u32[]{:S(2)}) collective-permute-start(bf16[1,3,128,128]{3,2,1,0:T(8,128)(2,1)S(1)} %copy-done.3), channel_id=1, source_target_pairs={{0,32},{32,0},{1,33},{33,1},{2,34},{34,2},{3,35},{35,3},{4,36},{36... | collective-permute-start | bytes 294920 | tf_op jit(solution)/shard_map/ppermute | solution.py:337
  33.0 0.0 collective-permute-done.gate1
  33.0 4.3 %collective-permute-done.1.up1 = bf16[1,3,128,128]{3,2,1,0:T(8,128)(2,1)S(1)} collective-permute-done((bf16[1,3,128,128]{3,2,1,0:T(8,128)(2,1)S(1)}, bf16[1,3,128,128]{3,2,1,0:T(8,128)(2,1)S(1)}, u32[]{:S(2)}, u32[]{:S(2)}) %collective-permute-start.1) | collective-permute-done | bytes 98336 | tf_op jit(solution)/shard_map/ppermute | solution.py:337
  37.3 6.4 %all-to-all-done.got_ref.picked_ref = bf16[32,96,128]{2,1,0:T(8,128)(2,1)S(1)} async-done(((bf16[32,96,128]{2,1,0:T(8,128)(2,1)}), bf16[32,96,128]{2,1,0:T(8,128)(2,1)S(1)}, u32[]{:S(2)}, u32[]{:S(2)}) %all-to-all-start) | async-done | bytes 786464 | tf_op jit(solution)/shard_map/all_to_all | solution.py:340
  43.7 1.4 gates.1
  45.1 1.0 collective-permute-done.2.down1
  46.0 1.0 down_terms.1
  47.1 0.0 copy-start.1
  47.1 0.0 copy-start.2
  47.1 0.0 copy-start.7
  47.1 34.7 %all_to_all.20.got_ref = bf16[32,96,128]{2,1,0:T(8,128)(2,1)S(1)} all-to-all(bf16[32,96,128]{2,1,0:T(8,128)(2,1)S(1)} %down_terms.1), channel_id=1, replica_groups=mesh['y'=4,'zh'=2,'za'=2,'zb'=4,'x'=4,'c'=2] {'c','x','zb'}, dimensions={0} | all-to-all | bytes 1572864 | tf_op jit(solution)/shard_map/all_to_all | solution.py:340
  81.8 2.3 %middle.1 = (bf16[16,4096]{1,0:T(8,128)(2,1)}, bf16[32,104,128]{2,1,0:T(8,128)(2,1)S(1)}) custom-call(s32[1,192]{1,0:T(1,128)S(1)} %copy-done.9, bf16[32,96,128]{2,1,0:T(8,128)(2,1)S(1)} %all_to_all.20.got_ref, bf16[16,4096]{1,0:T(8,128)(2,1)S(1)} %copy-done.1, bf16[16,4096]{1,0:T(8,128)(2,1)S(1)} %copy-done.2, f32[1,2,4096]{2,1,0:T(2,128)S(1)} %copy-done.7), custom_call_target="tpu_custom_call" | custom-call | tf_op jit(solution)/shard_map/middle/pallas_call | solution.py:316
  84.1 27.1 %all_to_all.21.got_ref = bf16[32,104,128]{2,1,0:T(8,128)(2,1)S(1)} all-to-all(bf16[32,104,128]{2,1,0:T(8,128)(2,1)S(1)} %get-tuple-element.23), channel_id=1, replica_groups=mesh['y'=4,'zh'=2,'za'=2,'zb'=4,'x'=4,'c'=2] {'c','x','zb'}, dimensions={0} | all-to-all | bytes 1703936 | tf_op jit(solution)/shard_map/all_to_all | solution.py:340
  111.3 3.0 %backward.1 = (bf16[32,104,128]{2,1,0:T(8,128)(2,1)}, f32[3,3,128,128]{3,2,1,0:T(8,128)S(1)}, bf16[3,3,128,128]{3,2,1,0:T(8,128)(2,1)S(1)}) custom-call(s32[1,192]{1,0:T(1,128)S(1)} %copy-done.9, bf16[32,104,128]{2,1,0:T(8,128)(2,1)S(1)} %all_to_all.21.got_ref, bf16[32,96,128]{2,1,0:T(8,128)(2,1)S(1)} %all-to-all-done.got_ref.picked_ref, ...), custom_call_target="tpu_custom_call" | custom-call | tf_op jit(solution)/shard_map/backward/pallas_call | solution.py:316
  114.3 5.0 %all-to-all-start.3 = ((bf16[32,104,128]{2,1,0:T(8,128)(2,1)}), bf16[32,104,128]{2,1,0:T(8,128)(2,1)S(1)}, u32[]{:S(2)}, u32[]{:S(2)}) async-start(bf16[32,104,128]{2,1,0:T(8,128)(2,1)} %get-tuple-element.28), calls=%async_computation.3 | async-start | bytes 1703936 | tf_op jit(solution)/shard_map/all_to_all | solution.py:340
  119.3 4.9 %collective-permute-start.3 = (bf16[3,3,128,128]{3,2,1,0:T(8,128)(2,1)S(1)}, bf16[3,3,128,128]{3,2,1,0:T(8,128)(2,1)S(1)}, u32[]{:S(2)}, u32[]{:S(2)}) collective-permute-start(bf16[3,3,128,128]{3,2,1,0:T(8,128)(2,1)S(1)} %get-tuple-element.27), channel_id=1, source_target_pairs={{0,32},{32,0},{1,33},{33,1},{2,34},{34,2},{3,35},{35,3},{4,36},{36... | collective-permute-start | bytes 884744 | tf_op jit(solution)/shard_map/ppermute | solution.py:337
  124.2 29.2 %all-to-all-done.3.got_ref = bf16[32,104,128]{2,1,0:T(8,128)(2,1)S(1)} async-done(((bf16[32,104,128]{2,1,0:T(8,128)(2,1)}), bf16[32,104,128]{2,1,0:T(8,128)(2,1)S(1)}, u32[]{:S(2)}, u32[]{:S(2)}) %all-to-all-start.3) | async-done | bytes 852000 | tf_op jit(solution)/shard_map/all_to_all | solution.py:340
  153.4 1.6 last.1
  155.0 8.2 %collective-permute-start.5 = (bf16[16,4096]{1,0:T(8,128)(2,1)S(1)}, bf16[16,4096]{1,0:T(8,128)(2,1)S(1)}, u32[]{:S(2)}, u32[]{:S(2)}) collective-permute-start(bf16[16,4096]{1,0:T(8,128)(2,1)S(1)} %get-tuple-element.30), channel_id=1, source_target_pairs={{64,0},{128,64},{192,128},{256,192},{320,256},{384,320},{448,384},... | collective-permute-start | bytes 393224 | tf_op jit(solution)/shard_map/ppermute | solution.py:391
  163.2 2.3 %collective-permute-start.4 = (bf16[2,4096]{1,0:T(2,128)(2,1)S(1)}, bf16[2,4096]{1,0:T(2,128)(2,1)S(1)}, u32[]{:S(2)}, u32[]{:S(2)}) collective-permute-start(bf16[2,4096]{1,0:T(2,128)(2,1)S(1)} %get-tuple-element.29.gain_ref), channel_id=1, source_target_pairs={{0,32},{32,0},{1,33},{33,1},{2,34},{34,2},{3,35},{35,3},{4,36},{36... | collective-permute-start | bytes 49160 | tf_op jit(solution)/shard_map/ppermute | solution.py:337
  165.5 0.0 collective-permute-done.3.other_ref
  165.5 12.3 %collective-permute-done.4.gain_other_ref = bf16[2,4096]{1,0:T(2,128)(2,1)S(1)} collective-permute-done((bf16[2,4096]{1,0:T(2,128)(2,1)S(1)}, bf16[2,4096]{1,0:T(2,128)(2,1)S(1)}, u32[]{:S(2)}, u32[]{:S(2)}) %collective-permute-start.4) | collective-permute-done | bytes 16416 | tf_op jit(solution)/shard_map/ppermute | solution.py:337
  177.8 1.0 collective-permute-done.5.input_ref
  178.8 0.8 finish.1
  (13 shorter events, 0.0 us)
Async XLA Ops:
  0.6 0.9 copy-start
  1.5 0.8 copy-start.6
  2.3 0.7 copy-start.8
  4.9 9.2 %copy-start.4 = (bf16[1,3,128,128]{3,2,1,0:T(8,128)(2,1)S(1)}, bf16[1,3,128,128]{3,2,1,0:T(8,128)(2,1)}, u32[]{:S(2)}) copy-start(bf16[1,3,128,128]{3,2,1,0:T(8,128)(2,1)} %gate0.3) | copy-start | bytes 294916
  4.9 18.3 %copy-start.5 = (bf16[1,3,128,128]{3,2,1,0:T(8,128)(2,1)S(1)}, bf16[1,3,128,128]{3,2,1,0:T(8,128)(2,1)}, u32[]{:S(2)}) copy-start(bf16[1,3,128,128]{3,2,1,0:T(8,128)(2,1)} %up0.3) | copy-start | bytes 294916
  4.9 20.3 %copy-start.3 = (bf16[1,3,128,128]{3,2,1,0:T(8,128)(2,1)S(1)}, bf16[1,3,128,128]{3,2,1,0:T(8,128)(2,1)}, u32[]{:S(2)}) copy-start(bf16[1,3,128,128]{3,2,1,0:T(8,128)(2,1)} %down0.3) | copy-start | bytes 294916
  4.9 38.8 %copy-start.9 = (s32[1,192]{1,0:T(1,128)S(1)}, s32[1,192]{1,0:T(1,128)}, u32[]{:S(2)}) copy-start(s32[1,192]{1,0:T(1,128)} %place_ref.11) | copy-start | bytes 2308
  4.9 38.8 %all-to-all-start = ((bf16[32,96,128]{2,1,0:T(8,128)(2,1)}), bf16[32,96,128]{2,1,0:T(8,128)(2,1)S(1)}, u32[]{:S(2)}, u32[]{:S(2)}) async-start(bf16[32,96,128]{2,1,0:T(8,128)(2,1)} %send_normed.1), calls=%async_computation | async-start | bytes 1572864 | tf_op jit(solution)/shard_map/all_to_all | solution.py:340
  14.1 18.9 %collective-permute-start = (bf16[1,3,128,128]{3,2,1,0:T(8,128)(2,1)S(1)}, bf16[1,3,128,128]{3,2,1,0:T(8,128)(2,1)S(1)}, u32[]{:S(2)}, u32[]{:S(2)}) collective-permute-start(bf16[1,3,128,128]{3,2,1,0:T(8,128)(2,1)S(1)} %copy-done.4), channel_id=1, source_target_pairs={{0,32},{32,0},{1,33},{33,1},{2,34},{34,2},{3,35},{35,3},{4,36},{36... | collective-permute-start | bytes 294920 | tf_op jit(solution)/shard_map/ppermute | solution.py:337
  23.2 14.1 %collective-permute-start.1 = (bf16[1,3,128,128]{3,2,1,0:T(8,128)(2,1)S(1)}, bf16[1,3,128,128]{3,2,1,0:T(8,128)(2,1)S(1)}, u32[]{:S(2)}, u32[]{:S(2)}) collective-permute-start(bf16[1,3,128,128]{3,2,1,0:T(8,128)(2,1)S(1)} %copy-done.5), channel_id=1, source_target_pairs={{0,32},{32,0},{1,33},{33,1},{2,34},{34,2},{3,35},{35,3},{4,36},{36... | collective-permute-start | bytes 294920 | tf_op jit(solution)/shard_map/ppermute | solution.py:337
  25.1 20.9 %collective-permute-start.2 = (bf16[1,3,128,128]{3,2,1,0:T(8,128)(2,1)S(1)}, bf16[1,3,128,128]{3,2,1,0:T(8,128)(2,1)S(1)}, u32[]{:S(2)}, u32[]{:S(2)}) collective-permute-start(bf16[1,3,128,128]{3,2,1,0:T(8,128)(2,1)S(1)} %copy-done.3), channel_id=1, source_target_pairs={{0,32},{32,0},{1,33},{33,1},{2,34},{34,2},{3,35},{35,3},{4,36},{36... | collective-permute-start | bytes 294920 | tf_op jit(solution)/shard_map/ppermute | solution.py:337
  47.1 34.7 %copy-start.1 = (bf16[16,4096]{1,0:T(8,128)(2,1)S(1)}, bf16[16,4096]{1,0:T(8,128)(2,1)}, u32[]{:S(2)}) copy-start(bf16[16,4096]{1,0:T(8,128)(2,1)} %acts_ref.5) | copy-start | bytes 393220
  47.1 34.7 %copy-start.2 = (bf16[16,4096]{1,0:T(8,128)(2,1)S(1)}, bf16[16,4096]{1,0:T(8,128)(2,1)}, u32[]{:S(2)}) copy-start(bf16[16,4096]{1,0:T(8,128)(2,1)} %cot_ref.3) | copy-start | bytes 393220
  47.1 34.7 %copy-start.7 = (f32[1,2,4096]{2,1,0:T(2,128)S(1)}, f32[1,2,4096]{2,1,0:T(2,128)}, u32[]{:S(2)}) copy-start(f32[1,2,4096]{2,1,0:T(2,128)} %gains_ref.5) | copy-start | bytes 98308
  114.3 39.1 %all-to-all-start.3 = ((bf16[32,104,128]{2,1,0:T(8,128)(2,1)}), bf16[32,104,128]{2,1,0:T(8,128)(2,1)S(1)}, u32[]{:S(2)}, u32[]{:S(2)}) async-start(bf16[32,104,128]{2,1,0:T(8,128)(2,1)} %get-tuple-element.28), calls=%async_computation.3 | async-start | bytes 1703936 | tf_op jit(solution)/shard_map/all_to_all | solution.py:340
  119.3 46.2 %collective-permute-start.3 = (bf16[3,3,128,128]{3,2,1,0:T(8,128)(2,1)S(1)}, bf16[3,3,128,128]{3,2,1,0:T(8,128)(2,1)S(1)}, u32[]{:S(2)}, u32[]{:S(2)}) collective-permute-start(bf16[3,3,128,128]{3,2,1,0:T(8,128)(2,1)S(1)} %get-tuple-element.27), channel_id=1, source_target_pairs={{0,32},{32,0},{1,33},{33,1},{2,34},{34,2},{3,35},{35,3},{4,36},{36... | collective-permute-start | bytes 884744 | tf_op jit(solution)/shard_map/ppermute | solution.py:337
  155.0 23.8 %collective-permute-start.5 = (bf16[16,4096]{1,0:T(8,128)(2,1)S(1)}, bf16[16,4096]{1,0:T(8,128)(2,1)S(1)}, u32[]{:S(2)}, u32[]{:S(2)}) collective-permute-start(bf16[16,4096]{1,0:T(8,128)(2,1)S(1)} %get-tuple-element.30), channel_id=1, source_target_pairs={{64,0},{128,64},{192,128},{256,192},{320,256},{384,320},{448,384},... | collective-permute-start | bytes 393224 | tf_op jit(solution)/shard_map/ppermute | solution.py:391
  163.2 14.7 %collective-permute-start.4 = (bf16[2,4096]{1,0:T(2,128)(2,1)S(1)}, bf16[2,4096]{1,0:T(2,128)(2,1)S(1)}, u32[]{:S(2)}, u32[]{:S(2)}) collective-permute-start(bf16[2,4096]{1,0:T(2,128)(2,1)S(1)} %get-tuple-element.29.gain_ref), channel_id=1, source_target_pairs={{0,32},{32,0},{1,33},{33,1},{2,34},{34,2},{3,35},{35,3},{4,36},{36... | collective-permute-start | bytes 49160 | tf_op jit(solution)/shard_map/ppermute | solution.py:337
